TPU v7x, 256 devices: a whole 4x4x8 slice. The times are simulated.
256 devices in a mesh: dom: 32 (over z, x), band: 8 (over y, core).
Axes of the slice: x: 4, y: 4, z: 8, core: 2. Of those that a mesh axis runs over, the one named last changes fastest.
Arguments:
- orbitals: float32 [8, 384, 16, 128], P('band', 'dom'), may hold values from -6 to 6
- potential: float32 [384, 16, 128], P('dom'), may hold values from -1.5 to 0.5
- atom_pos: int32 [1024, 3], P('dom'), may hold values from 0 to 127, as said below
- atom_count: int32 [32], P('dom'), may hold values from 8 to 32, as said below
- projectors: float32 [1024, 8, 384], P('dom'), may hold values from -0.4375 to 0.4375
- gammas: float32 [1024, 8], P('dom'), may hold values from 0.3 to 2
- ritz: float32 [8, 8], replicated, may hold values from -2 to 2
Outputs:
- filtered: float32 [8, 384, 16, 128], P('band', 'dom')
- rotated: float32 [8, 384, 16, 128], P('band', 'dom')
Inputs may be any that keep to these rules, and one draw needn't show every extreme that they name: `atom_pos`: row a is the corner of slot a's support box: a plane within the 12 planes of slab a // 32, then a second grid index below 16 and a third below 128. Slab d's first atom_count[d] slots are live; some slab has all 32 live and some has 8.
All inputs are finite; a program needn't handle non-finite values.
Results may differ from a plain program's by a relative error of at most 0.00016.
Values sent between devices are 32-bit elements; how exact they have to be, the bound alone decides.
No kernel may reach another device: no remote copies, remote signals or barrier semaphores. Data moves between devices by JAX's collectives and lax.ppermute only.
A program may use at most 64 MiB of HBM per device.

v0:
```python
import jax
import jax.numpy as jnp
from jax import lax
from jax.sharding import PartitionSpec as P

DEGREE = 4
BX = 6
BY = 8
BZ = 8


STENCIL = (
    -5369.0 / 1800.0,
    12.0 / 7.0,
    -15.0 / 56.0,
    10.0 / 189.0,
    -1.0 / 112.0,
    2.0 / 1925.0,
    -1.0 / 16632.0,
)
LOWER = -1.6
UPPER = 24.0


def with_halo(block, sides, width):
    for axis, dim in sides:
        count = lax.axis_size(axis)
        forward = [(i, i + 1) for i in range(count - 1)]
        forward.append((count - 1, 0))
        backward = [(target, source) for source, target in forward]
        low = lax.ppermute(
            lax.slice_in_dim(block, block.shape[dim] - width, None, axis=dim), axis, forward
        )
        high = lax.ppermute(lax.slice_in_dim(block, 0, width, axis=dim), axis, backward)
        block = jnp.concatenate([low, block, high], axis=dim)
    return block


def shifted(value, axis, steps):
    count = lax.axis_size(axis)
    pairs = [(source, (source + steps) % count) for source in range(count)]
    return lax.ppermute(value, axis, pairs)


def laplace_slab(padded):
    planes_out = padded.shape[1] - 12
    middle = padded[:, 6 : 6 + planes_out]
    summed = 3.0 * STENCIL[0] * middle
    for reach in range(1, 7):
        along_x = (
            padded[:, 6 + reach : 6 + reach + planes_out]
            + padded[:, 6 - reach : 6 - reach + planes_out]
        )
        along_y = jnp.roll(middle, reach, 2) + jnp.roll(middle, -reach, 2)
        along_z = jnp.roll(middle, reach, 3) + jnp.roll(middle, -reach, 3)
        summed = (
            summed + STENCIL[reach] * along_x + STENCIL[reach] * along_y + STENCIL[reach] * along_z
        )
    return (summed, middle)


def nonlocal_term(
    field_in, in_low, atom_x, atom_y, atom_z, projectors, weighted, out_low, out_planes
):
    orbits, planes_in, rows, columns = field_in.shape
    cells = jnp.arange(BX * BY * BZ, dtype=jnp.int32)
    box_x = cells // (BY * BZ)
    box_y = cells // BZ % BY
    box_z = cells % BZ
    plane_idx = atom_x[:, None] + box_x[None]
    needed = ((atom_x + BX - 1 >= out_low) & (atom_x < out_low + out_planes)).astype(jnp.float32)
    plane_in = jnp.clip(plane_idx - in_low, 0, planes_in - 1)
    row_idx = (atom_y[:, None] + box_y[None]) % rows
    col_idx = (atom_z[:, None] + box_z[None]) % columns
    flat_in = (plane_in * rows + row_idx) * columns + col_idx
    values = field_in.reshape(orbits, -1)[:, flat_in]
    coeffs = jnp.einsum("nas,als->nal", values, projectors, precision=lax.Precision.HIGHEST)
    coeffs = coeffs * (weighted * needed[:, None])[None]
    contrib = jnp.einsum("nal,als->nas", coeffs, projectors, precision=lax.Precision.HIGHEST)
    plane_out = plane_idx - out_low
    inside = ((plane_out >= 0) & (plane_out < out_planes)).astype(jnp.float32)
    contrib = contrib * inside[None]
    flat_out = (jnp.clip(plane_out, 0, out_planes - 1) * rows + row_idx) * columns + col_idx
    summed = (
        jnp.zeros((orbits, out_planes * rows * columns), jnp.float32).at[:, flat_out].add(contrib)
    )
    return summed.reshape(orbits, out_planes, rows, columns)


def recurrence(iteration, applied, middle, previous, center, half):
    if iteration == 0:
        return (applied - center * middle) / half
    return 2.0 / half * (applied - center * middle) - previous


def shards(orbitals, potential, atom_pos, atom_count, projectors, gammas, ritz):
    orbits, planes, rows, columns = orbitals.shape
    center = 0.5 * (UPPER + LOWER)
    half = 0.5 * (UPPER - LOWER)
    slot_idx = jnp.arange(atom_pos.shape[0], dtype=jnp.int32)
    active = (slot_idx < atom_count[0]).astype(jnp.float32)
    weighted = gammas * active[:, None]
    current = orbitals
    previous = orbitals
    for iteration in range(DEGREE):
        padded = with_halo(current, (("dom", 1),), 6)
        laplace, middle = laplace_slab(padded)
        nearby = nonlocal_term(
            padded,
            -6,
            atom_pos[:, 0],
            atom_pos[:, 1],
            atom_pos[:, 2],
            projectors,
            weighted,
            0,
            planes + 6,
        )
        received = shifted(nearby[:, planes:], "dom", 1)
        nearby = nearby[:, :planes] + jnp.pad(received, ((0, 0), (0, planes - 6), (0, 0), (0, 0)))
        applied = -0.5 * laplace + potential[None] * middle + nearby
        updated = recurrence(iteration, applied, middle, previous, center, half)
        previous = current
        current = updated
    column_start = lax.axis_index("band") * orbits
    own_columns = lax.dynamic_slice_in_dim(ritz, column_start, orbits, 1)
    rotated = jnp.einsum(
        "ij,ixyz->jxyz",
        own_columns,
        lax.all_gather(current, "band", axis=0, tiled=True),
        precision=lax.Precision.HIGHEST,
    )
    return (current, rotated)


def solution(mesh):
    in_specs = (
        P("band", "dom", None, None),
        P("dom", None, None),
        P("dom", None),
        P("dom"),
        P("dom", None, None),
        P("dom", None),
        P(),
    )
    out_specs = (P("band", "dom", None, None), P("band", "dom", None, None))
    return jax.shard_map(shards, mesh=mesh, in_specs=in_specs, out_specs=out_specs, check_vma=False)
```

profile of v0, /device:TPU:1, one launch (start us, length us, event | category | flops | bytes accessed | tf_op | source)
XLA Modules:
  0.0 746.2 jit_solution(3351286483457182586)
XLA Ops:
  1.6 8.7 %collective-permute-start = (f32[1,6,16,128]{3,2,1,0:T(8,128)S(1)}, f32[1,6,16,128]{3,2,1,0:T(8,128)S(1)}, u32[]{:S(2)}, u32[]{:S(2)}) collective-permute-start(f32[1,6,16,128]{3,2,1,0:T(8,128)S(1)} %get-tuple-element.205), channel_id=1, source_target_pairs={{8,0},{16,8},{24,16},{32,24},{40,32},{48,40},{56,48},{64,56},{72,6... | collective-permute-start | bytes 147464 | tf_op jit(solution)/shard_map/ppermute | solution.py:34
  22.1 68.0 %gather_fusion = f32[12288]{0:T(1024)S(1)} fusion(f32[49152]{0:T(1024)S(1)} %bitcast.97, s32[12288]{0:T(1024)S(1)} %broadcast_clamp_fusion), kind=kCustom, calls=%fused_computation | custom fusion | bytes 147456 | tf_op jit(solution)/shard_map/gather | solution.py:76
  92.6 84.1 %scatter_custom_fusion = f32[36864]{0:T(1024)S(1)} fusion(s32[12288]{0:T(1024)} %reshape.3255, f32[12288]{0:T(1024)S(1)} %reshape.3257, f32[]{:T(128)} %constant.158.clone.1), kind=kCustom, calls=%fused_computation.374 | custom fusion | flops 12288 | bytes 147968 | tf_op jit(solution)/shard_map/scatter-add | solution.py:85
  176.9 6.1 collective-permute-done.2
  183.1 1.9 broadcast_multiply_fusion
  192.8 1.3 collective-permute-start.3
  195.7 4.7 collective-permute-done.4
  200.4 68.0 %gather_fusion.1 = f32[12288]{0:T(1024)S(1)} fusion(f32[49152]{0:T(1024)S(1)} %bitcast.98, s32[12288]{0:T(1024)S(1)} %broadcast_clamp_fusion), kind=kCustom, calls=%fused_computation.1 | custom fusion | bytes 147456 | tf_op jit(solution)/shard_map/gather | solution.py:76
  271.0 84.3 %scatter_custom_fusion.1 = f32[36864]{0:T(1024)S(1)} fusion(s32[12288]{0:T(1024)} %reshape.3255, f32[12288]{0:T(1024)S(1)} %reshape.3267, f32[]{:T(128)} %constant.158.clone.1), kind=kCustom, calls=%fused_computation.372 | custom fusion | flops 12288 | bytes 147968 | tf_op jit(solution)/shard_map/scatter-add | solution.py:85
  355.5 6.2 collective-permute-done.5
  362.4 2.0 fusion.104
  372.0 1.5 collective-permute-start.7
  375.0 3.3 collective-permute-done.7
  378.9 68.0 %gather_fusion.2 = f32[12288]{0:T(1024)S(1)} fusion(f32[49152]{0:T(1024)S(1)} %bitcast.99, s32[12288]{0:T(1024)S(1)} %broadcast_clamp_fusion), kind=kCustom, calls=%fused_computation.2 | custom fusion | bytes 147456 | tf_op jit(solution)/shard_map/gather | solution.py:76
  449.4 84.1 %scatter_custom_fusion.2 = f32[36864]{0:T(1024)S(1)} fusion(s32[12288]{0:T(1024)} %reshape.3255, f32[12288]{0:T(1024)S(1)} %reshape.3277, f32[]{:T(128)} %constant.158.clone.1), kind=kCustom, calls=%fused_computation.370 | custom fusion | flops 12288 | bytes 147968 | tf_op jit(solution)/shard_map/scatter-add | solution.py:85
  533.7 6.2 collective-permute-done.8
  540.6 1.9 fusion.60
  550.2 4.8 collective-permute-start.9
  557.1 68.0 %gather_fusion.3 = f32[12288]{0:T(1024)S(1)} fusion(f32[49152]{0:T(1024)S(1)} %bitcast.96, s32[12288]{0:T(1024)S(1)} %broadcast_clamp_fusion), kind=kCustom, calls=%fused_computation.3 | custom fusion | bytes 147456 | tf_op jit(solution)/shard_map/gather | solution.py:76
  627.7 84.2 %scatter_custom_fusion.3 = f32[36864]{0:T(1024)S(1)} fusion(s32[12288]{0:T(1024)} %reshape.3255, f32[12288]{0:T(1024)S(1)} %reshape.3287, f32[]{:T(128)} %constant.158.clone.1), kind=kCustom, calls=%fused_computation.368 | custom fusion | flops 12288 | bytes 147968 | tf_op jit(solution)/shard_map/scatter-add | solution.py:85
  712.1 6.2 collective-permute-done.11
  719.0 2.0 fusion.16
  721.1 23.4 %all_gather.3 = f32[8,12,16,128]{3,2,1,0:T(8,128)S(1)} all-gather(f32[1,12,16,128]{3,2,1,0:T(8,128)S(1)} %fusion.16), channel_id=1, replica_groups=mesh['dom'=32,'band'=8] {'band'}, dimensions={0}, use_global_device_ids=true | all-gather | bytes 884736 | tf_op jit(solution)/shard_map/all_gather | solution.py:130
  744.5 1.8 fusion
  (239 shorter events, 53.0 us)
Async XLA Ops:
  0.6 89.5 %copy-start = (f32[32,8,384]{2,1,0:T(8,128)S(1)}, f32[32,8,384]{2,1,0:T(8,128)}, u32[]{:S(2)}) copy-start(f32[32,8,384]{2,1,0:T(8,128)} %param.11) | copy-start | bytes 1179652
  0.6 10.3 %copy-start.1 = (f32[1,12,16,128]{3,2,1,0:T(8,128)S(1)}, f32[1,12,16,128]{3,2,1,0:T(8,128)}, u32[]{:S(2)}) copy-start(f32[1,12,16,128]{3,2,1,0:T(8,128)} %param.7) | copy-start | bytes 294916
  1.6 20.5 %collective-permute-start = (f32[1,6,16,128]{3,2,1,0:T(8,128)S(1)}, f32[1,6,16,128]{3,2,1,0:T(8,128)S(1)}, u32[]{:S(2)}, u32[]{:S(2)}) collective-permute-start(f32[1,6,16,128]{3,2,1,0:T(8,128)S(1)} %get-tuple-element.205), channel_id=1, source_target_pairs={{8,0},{16,8},{24,16},{32,24},{40,32},{48,40},{56,48},{64,56},{72,6... | collective-permute-start | bytes 147464 | tf_op jit(solution)/shard_map/ppermute | solution.py:34
  10.2 11.8 %collective-permute-start.1 = (f32[1,6,16,128]{3,2,1,0:T(8,128)S(1)}, f32[1,6,16,128]{3,2,1,0:T(8,128)S(1)}, u32[]{:S(2)}, u32[]{:S(2)}) collective-permute-start(f32[1,6,16,128]{3,2,1,0:T(8,128)S(1)} %get-tuple-element.204), channel_id=1, source_target_pairs={{0,8},{8,16},{16,24},{24,32},{32,40},{40,48},{48,56},{56,64},{64,7... | collective-permute-start | bytes 147464 | tf_op jit(solution)/shard_map/ppermute | solution.py:31
  10.9 81.6 %copy-start.26 = (s32[32]{0:T(128)}, s32[32]{0:T(128)S(1)}, u32[]{:S(2)}) copy-start(s32[32]{0:T(128)S(1)} %get-tuple-element.208) | copy-start | bytes 388
  10.9 80.3 %copy-start.29 = (f32[32]{0:T(128)}, f32[32]{0:T(128)S(1)}, u32[]{:S(2)}) copy-start(f32[32]{0:T(128)S(1)} %fusion.248) | copy-start | bytes 388
  20.0 71.2 %copy-start.31 = (f32[32]{0:T(128)}, f32[32]{0:T(128)S(1)}, u32[]{:S(2)}) copy-start(f32[32]{0:T(128)S(1)} %compare_convert_fusion) | copy-start | bytes 388
  176.8 6.3 collective-permute-start.2
  192.8 2.9 collective-permute-start.3
  194.1 6.3 collective-permute-start.4
  355.4 6.3 collective-permute-start.5
  372.0 2.9 collective-permute-start.6
  372.0 6.3 collective-permute-start.7
  449.4 90.5 %copy-start.19 = (f32[1,6,16,128]{3,2,1,0:T(8,128)S(1)}, f32[1,6,16,128]{3,2,1,0:T(8,128)}, u32[]{:S(2)}) copy-start(f32[1,6,16,128]{3,2,1,0:T(8,128)} %copy-done.18) | copy-start | bytes 147460
  533.5 6.3 collective-permute-start.8
  550.2 6.3 collective-permute-start.10
  550.2 6.3 collective-permute-start.9
  626.9 91.4 %copy-start.23 = (f32[1,12,2,128]{3,2,1,0:T(2,128)S(1)}, f32[1,12,2,128]{3,2,1,0:T(2,128)}, u32[]{:S(2)}) copy-start(f32[1,12,2,128]{3,2,1,0:T(2,128)} %get-tuple-element.43) | copy-start | bytes 36868
  627.7 90.6 %copy-start.17 = (f32[1,6,16,128]{3,2,1,0:T(8,128)S(1)}, f32[1,6,16,128]{3,2,1,0:T(8,128)}, u32[]{:S(2)}) copy-start(f32[1,6,16,128]{3,2,1,0:T(8,128)} %copy-done.16) | copy-start | bytes 147460
  627.7 90.6 %copy-start.20 = (f32[1,12,6,128]{3,2,1,0:T(8,128)S(1)}, f32[1,12,6,128]{3,2,1,0:T(8,128)}, u32[]{:S(2)}) copy-start(f32[1,12,6,128]{3,2,1,0:T(8,128)} %get-tuple-element.10) | copy-start | bytes 110596
  712.0 6.4 copy-start.10
  712.0 6.3 collective-permute-start.11
  721.0 23.4 %copy-start.3 = (f32[1,12,16,128]{3,2,1,0:T(8,128)}, f32[1,12,16,128]{3,2,1,0:T(8,128)S(1)}, u32[]{:S(2)}) copy-start(f32[1,12,16,128]{3,2,1,0:T(8,128)S(1)} %fusion.16) | copy-start | bytes 294916
  721.0 23.4 %copy-start.36 = (f32[8]{0:T(128)S(1)}, f32[8]{0:T(128)}, u32[]{:S(2)}) copy-start(f32[8]{0:T(128)} %dynamic-slice_reduce_fusion) | copy-start | bytes 100
  (26 other events, 85.3 us)
where the time goes:
time: 747 us; the launch traced here: 746 us
  other arithmetic  345 us (46%)
  local copies, waits for them, and re-layouts  315 us (42%)
  waiting for transfers between devices  35.4 us (5%)
  blocking collectives  23.4 us (3%)
  starting transfers between devices  16.7 us (2%)
  matrix products  8.15 us (1%)
    scatter-add x4, other arithmetic, nonlocal_term(): jnp.zeros((orbits, out_planes * rows * columns), jnp.float32)  337 us
    gather x4, local copies, waits for them, and re-layouts, nonlocal_term(): values = field_in.reshape(orbits, -1)[:, flat_in]  272 us
    ppermute x4, waiting for transfers between devices, shifted(): return lax.ppermute(value, axis, pairs)  24.8 us
    all_gather x1, blocking collectives, shards(): lax.all_gather(current, 'band', axis=0, tiled=True)  23.4 us
    slice x48, local copies, waits for them, and re-layouts, laplace_slab(): along_y = jnp.roll(middle, reach, 2) + jnp.roll(middle, -reach, 2)  18.9 us
  transfers between devices with their start and end apart: 12, of which 9 were waited for; matrix products, arithmetic and copies ran while one was open for 2% of the time, Pallas kernels for 0%

commit v1 on v0

v1 whole, which is shorter than its diff:
```python
import jax
import jax.numpy as jnp
import numpy as np
from jax import lax
from jax.experimental import pallas as pl
from jax.experimental.pallas import tpu as pltpu
from jax.sharding import PartitionSpec as P

STENCIL = (
    -5369.0 / 1800.0,
    12.0 / 7.0,
    -15.0 / 56.0,
    10.0 / 189.0,
    -1.0 / 112.0,
    2.0 / 1925.0,
    -1.0 / 16632.0,
)
LOWER = -1.6
UPPER = 24.0
CENTER = 0.5 * (UPPER + LOWER)
HALF = 0.5 * (UPPER - LOWER)

CX, NY, NZ = 12, 16, 128
ATOMS = 32
NPROJ, BX, BY, BZ = 8, 6, 8, 8
LANES = ATOMS * BZ
SPAN = CX + BX - 1
ROW_Y, ROW_POT, ROW_P, ROW_META, ROWS = 0, 192, 288, 1056, 1088
META_Z, META_XY, META_ROWS = 8, 9, 16


def z_stencil():
    full = np.zeros((NZ, NZ), np.float32)
    cells = np.arange(NZ)
    for reach in range(1, 7):
        full[cells, (cells + reach) % NZ] += STENCIL[reach]
        full[cells, (cells - reach) % NZ] += STENCIL[reach]
    high = full.astype(jnp.bfloat16)
    low = (full - high.astype(np.float32)).astype(jnp.bfloat16)
    return np.concatenate([high, high, low], 0)


def group_sum():
    atoms = np.arange(LANES) // BZ
    return (atoms[:, None] == atoms[None]).astype(jnp.bfloat16)


def two_terms(value, axis):
    high = value.astype(jnp.bfloat16)
    low = (value - high.astype(jnp.float32)).astype(jnp.bfloat16)
    return jnp.concatenate([high, low], axis)


def dot(left, right):
    return jnp.dot(left, right, preferred_element_type=jnp.float32)


def pack_kernel(y_ref, pot_ref, proj_ref, meta_ref, up_ref, down_ref):
    for out, planes in ((up_ref, slice(6, 12)), (down_ref, slice(0, 6))):
        out[ROW_Y : ROW_Y + 192, :] = y_ref[...].reshape(192, NZ)
        out[ROW_POT : ROW_POT + 96, :] = pot_ref[planes].reshape(96, NZ)
        for part in range(3):
            first = ROW_P + 256 * part
            out[first : first + 256, :] = proj_ref[:, :, 128 * part : 128 * part + 128].reshape(256, NZ)
        for tile in range(2):
            first = ROW_META + META_ROWS * tile
            out[first : first + META_ROWS, :] = meta_ref[:, 128 * tile : 128 * tile + 128]


def spread_projectors(read, work, table, group):
    lane = lax.broadcasted_iota(jnp.int32, (8, 128), 1)
    for tile in range(2):
        cols = slice(128 * tile, 128 * tile + 128)
        for part in range(3):
            items = [read(part, 16 * tile + a) for a in range(16)]
            for bit in (1, 2, 4, 8):
                upper = (lane & (8 * bit)) != 0
                for p in range(16):
                    if p & bit:
                        continue
                    q = p | bit
                    first, second = items[p], items[q]
                    items[p] = jnp.where(upper, pltpu.roll(second, 8 * bit, 1), first)
                    items[q] = jnp.where(upper, second, pltpu.roll(first, 128 - 8 * bit, 1))
            for g in range(16):
                i, j = 2 * part + g // 8, g % 8
                work[i, 8 * j : 8 * j + 8, :] = items[g]
        for i in range(BX):
            for l in range(NPROJ):
                table[group, l * BX + i, :, cols] = work.at[i][pl.ds(l, 8, stride=8), :]


def fill(padded, plane, value):
    count = value.shape[0]
    padded[plane : plane + count, 8:24, :] = value
    padded[plane : plane + count, 0:8, :] = value[:, 8:16]
    padded[plane : plane + count, 24:32, :] = value[:, 0:8]


def nonlocal_group(group, field2, first_in, planes_in, skip, gathered, placed, table, place, weight, onehot, sums):
    rows = slice(NY * first_in, NY * (first_in + planes_in))
    columns = dot(field2[rows, :], jnp.concatenate([onehot, onehot], 0)).reshape(planes_in, NY, LANES)
    for tile in range(2):
        part = columns[:, :, 128 * tile : 128 * tile + 128]
        gathered[group, tile, skip : skip + planes_in, 0:16, :] = part
        gathered[group, tile, skip : skip + planes_in, 16:24, :] = part[:, 0:8]
    lane = lax.broadcasted_iota(jnp.int32, (8, 128), 1)
    values = [[jnp.zeros((8, 128), jnp.float32)] * 2 for _ in range(BX)]
    for a in range(16):
        mine = (lane >> 3) == a
        for tile in range(2):
            x0, y0 = place(group, 16 * tile + a)
            for i in range(BX):
                values[i][tile] = jnp.where(mine, gathered[group, tile, x0 + i, pl.ds(y0, 8), :], values[i][tile])
    values = [jnp.concatenate(v, 1) for v in values]
    coeffs = []
    for l in range(NPROJ):
        total = values[0] * table[group, l * BX]
        for i in range(1, BX):
            total = total + values[i] * table[group, l * BX + i]
        coeffs.append(jnp.sum(total, 0, keepdims=True))
    coeffs = jnp.concatenate(coeffs, 0)
    both = dot(two_terms(coeffs, 0), sums)
    coeffs = (both[:8] + both[8:]) * weight
    contrib = []
    for i in range(BX):
        total = coeffs[0:1] * table[group, i]
        for l in range(1, NPROJ):
            total = total + coeffs[l : l + 1] * table[group, l * BX + i]
        contrib.append(total)
    for a in range(16):
        mine = (lane >> 3) == a
        for tile in range(2):
            x0, y0 = place(group, 16 * tile + a)
            cols = slice(128 * tile, 128 * tile + 128)
            for i in range(BX):
                pltpu.store(placed.at[group, tile, x0 + i, pl.ds(y0, 8), :], contrib[i][:, cols], mask=mine)


def spread_group(group, first, count, placed, onehot):
    planes = slice(first, first + count)
    tiles = []
    for tile in range(2):
        folded = placed[group, tile, planes, 0:8, :] + placed[group, tile, planes, 16:24, :]
        tiles.append(jnp.concatenate([folded, placed[group, tile, planes, 8:16, :]], 1).reshape(count * NY, 128))
    value = jnp.concatenate(tiles, 1)
    twice = jnp.concatenate([onehot, onehot], 1)
    spread = lax.dot_general(
        two_terms(value, 1), twice, (((1,), (1,)), ((), ())), preferred_element_type=jnp.float32
    )
    return spread.reshape(count, NY, NZ)


def stencil_plane(padded, plane):
    total = 3.0 * STENCIL[0] * padded[plane, 8:24, :]
    for reach in range(1, 7):
        along_x = padded[plane + reach, 8:24, :] + padded[plane - reach, 8:24, :]
        along_y = padded[plane, 8 + reach : 24 + reach, :] + padded[plane, 8 - reach : 24 - reach, :]
        total = total + STENCIL[reach] * (along_x + along_y)
    return total


def pair_kernel(first_pair, *refs):
    if first_pair:
        (mid_ref, low_ref, high_ref, pot_ref, proj_ref, meta_ref, zst_ref, sums_ref,
         out_ref, kept_ref, table,
         low_xy, high_xy, own_xy, padded, padded1, field2, gathered, placed, local, nonlocal_, work, sems) = refs
    else:
        (mid_ref, lowy_ref, highy_ref, kept_ref, table, low_ref, high_ref, pot_ref, meta_ref, zst_ref, sums_ref,
         out_ref,
         low_xy, high_xy, own_xy, padded, padded1, field2, gathered, placed, local, nonlocal_, sems) = refs

    copies = []
    for n, (source, target) in enumerate(((low_ref, low_xy), (meta_ref, own_xy), (high_ref, high_xy))):
        rows = pl.ds(8, 8) if n == 1 else pl.ds(ROW_META + 8, 8)
        copies.append(pltpu.make_async_copy(source.at[rows, pl.ds(0, 128)], target, sems.at[n]))
        copies[-1].start()

    def place(group, atom):
        held = (low_xy, own_xy, high_xy)[group]
        return held[1, atom].astype(jnp.int32), held[1, 32 + atom].astype(jnp.int32)

    def meta(group, rows):
        if group == 1:
            return meta_ref[rows, :]
        source = (low_ref, None, high_ref)[group]
        return jnp.concatenate(
            [source[ROW_META + META_ROWS * t + rows.start : ROW_META + META_ROWS * t + rows.stop, :] for t in range(2)], 1
        )

    def one_hot(group):
        column = lax.broadcasted_iota(jnp.int32, (NZ, LANES), 0).astype(jnp.float32)
        return jnp.where(column == meta(group, slice(META_Z, META_Z + 1)), 1.0, 0.0).astype(jnp.bfloat16)

    if first_pair:
        low_y, high_y = low_ref[ROW_Y : ROW_Y + 192, :], high_ref[ROW_Y : ROW_Y + 192, :]
    else:
        low_y, high_y = lowy_ref[...].reshape(192, NZ), highy_ref[...].reshape(192, NZ)
    mid_y = mid_ref[...].reshape(192, NZ)
    for n, value in enumerate((low_y, mid_y, high_y)):
        fill(padded, 12 * n, value.reshape(CX, NY, NZ))
        field2[192 * n : 192 * n + 192, :] = two_terms(value, 1)
    placed[...] = jnp.zeros_like(placed)
    gathered[2, :, 12:SPAN] = jnp.zeros((2, SPAN - 12, 24, 128), jnp.float32)

    if first_pair:
        for group, source in enumerate((low_ref, None, high_ref)):
            if group == 1:
                read = lambda part, a: proj_ref[a, :, 128 * part : 128 * part + 128]
            else:
                read = lambda part, a, s=source: s[ROW_P + 256 * part + 8 * a : ROW_P + 256 * part + 8 * a + 8, :]
            spread_projectors(read, work, table, group)
    hots = [one_hot(g) for g in range(3)]
    weights = [meta(g, slice(0, 8)) for g in range(3)]
    for copy in copies:
        copy.wait()

    for group, planes in ((0, SPAN), (1, SPAN), (2, 12)):
        nonlocal_group(group, field2, 12 * group, planes, 0, gathered, placed, table, place, weights[group],
                       hots[group], sums_ref[...])
    along_z = dot(field2[96:480, :], zst_ref[0:256, :]) + dot(field2[96:480, 0:128], zst_ref[256:384, :])
    local[...] = along_z.reshape(24, NY, NZ)
    nonlocal_[0:11] = spread_group(0, 6, 11, placed, hots[0])
    nonlocal_[11:24] = jnp.zeros((13, NY, NZ), jnp.float32)
    nonlocal_[6:23] += spread_group(1, 0, 17, placed, hots[1])
    nonlocal_[18:24] += spread_group(2, 0, 6, placed, hots[2])
    scale = (1.0 if first_pair else 2.0) / HALF
    for p in range(24):
        if p < 6:
            pot = low_ref[ROW_POT + 16 * p : ROW_POT + 16 * p + 16, :]
        elif p < 18:
            pot = pot_ref[p - 6]
        else:
            pot = high_ref[ROW_POT + 16 * (p - 18) : ROW_POT + 16 * (p - 18) + 16, :]
        here = padded[p + 6, 8:24, :]
        laplace = stencil_plane(padded, p + 6) + local[p]
        applied = -0.5 * laplace + (pot - CENTER) * here + nonlocal_[p]
        updated = scale * applied
        if first_pair:
            kept_ref[p] = updated
        else:
            updated = updated - kept_ref[p]
        fill(padded1, p, updated[None])
        field2[16 * p : 16 * p + 16, :] = two_terms(updated, 1)

    nonlocal_group(0, field2, 0, 11, 6, gathered, placed, table, place, weights[0], hots[0], sums_ref[...])
    nonlocal_group(1, field2, 6, SPAN, 0, gathered, placed, table, place, weights[1], hots[1], sums_ref[...])
    along_z = dot(field2[96:288, :], zst_ref[0:256, :]) + dot(field2[96:288, 0:128], zst_ref[256:384, :])
    local[0:12] = along_z.reshape(12, NY, NZ)
    nonlocal_[0:12] = spread_group(1, 0, 12, placed, hots[1])
    nonlocal_[0:5] += spread_group(0, 12, 5, placed, hots[0])
    for p in range(12):
        here = padded1[p + 6, 8:24, :]
        laplace = stencil_plane(padded1, p + 6) + local[p]
        applied = -0.5 * laplace + (pot_ref[p] - CENTER) * here + nonlocal_[p]
        out_ref[0, p] = (2.0 / HALF) * applied - padded[p + 12, 8:24, :]


def run_pair(first_pair, args):
    shape = lambda *dims: jax.ShapeDtypeStruct(dims, jnp.float32)
    outs = [shape(1, CX, NY, NZ)]
    scratch = [pltpu.SMEM((8, 128), jnp.float32)] * 3 + [
        pltpu.VMEM((36, 32, NZ), jnp.float32),
        pltpu.VMEM((24, 32, NZ), jnp.float32),
        pltpu.VMEM((576, 2 * NZ), jnp.bfloat16),
        pltpu.VMEM((3, 2, SPAN, 24, 128), jnp.float32),
        pltpu.VMEM((3, 2, SPAN, 24, 128), jnp.float32),
        pltpu.VMEM((24, NY, NZ), jnp.float32),
        pltpu.VMEM((24, NY, NZ), jnp.float32),
    ]
    if first_pair:
        outs += [shape(24, NY, NZ), shape(3, NPROJ * BX, BY, LANES)]
        scratch += [pltpu.VMEM((BX, BY * NPROJ, 128), jnp.float32)]
    scratch += [pltpu.SemaphoreType.DMA((3,))]
    vmem = pl.BlockSpec(memory_space=pltpu.VMEM)
    return pl.pallas_call(
        lambda *refs: pair_kernel(first_pair, *refs),
        out_shape=outs,
        in_specs=[vmem] * len(args),
        out_specs=[vmem] * len(outs),
        scratch_shapes=scratch,
        compiler_params=pltpu.CompilerParams(vmem_limit_bytes=40 * 2**20),
        name="two_steps",
    )(*args)


def ring(axis, step):
    count = lax.axis_size(axis)
    return [(i, (i + step) % count) for i in range(count)]


def shards(orbitals, potential, atom_pos, atom_count, projectors, gammas, ritz):
    live = (jnp.arange(ATOMS, dtype=jnp.int32) < atom_count[0]).astype(jnp.float32)
    weight = jnp.repeat((gammas * live[:, None]).T, BZ, axis=1)
    columns = (atom_pos[:, 2:3] + jnp.arange(BZ, dtype=jnp.int32)[None]) % NZ
    corners = jnp.concatenate([atom_pos[:, 0], atom_pos[:, 1]])
    meta = jnp.concatenate(
        [
            weight,
            columns.reshape(1, LANES).astype(jnp.float32),
            jnp.pad(corners.astype(jnp.float32), (0, LANES - 2 * ATOMS))[None],
            jnp.zeros((META_ROWS - 10, LANES), jnp.float32),
        ],
        0,
    )
    vmem = pl.BlockSpec(memory_space=pltpu.VMEM)
    up, down = pl.pallas_call(
        pack_kernel,
        out_shape=[jax.ShapeDtypeStruct((ROWS, NZ), jnp.float32)] * 2,
        in_specs=[vmem] * 4,
        out_specs=[vmem] * 2,
        compiler_params=pltpu.CompilerParams(vmem_limit_bytes=16 * 2**20),
        name="pack",
    )(orbitals, potential, projectors, meta)
    low = lax.ppermute(up, "dom", ring("dom", 1))
    high = lax.ppermute(down, "dom", ring("dom", -1))
    zst, sums = jnp.asarray(z_stencil()), jnp.asarray(group_sum())
    second, first, table = run_pair(True, (orbitals, low, high, potential, projectors, meta, zst, sums))
    low_y = lax.ppermute(second, "dom", ring("dom", 1))
    high_y = lax.ppermute(second, "dom", ring("dom", -1))
    (filtered,) = run_pair(
        False, (second, low_y, high_y, first, table, low, high, potential, meta, zst, sums)
    )

    count = lax.axis_size("band")
    band = lax.axis_index("band")
    other = lax.ppermute(filtered, "band", [(i, i ^ 1) for i in range(count)])
    picked = jnp.arange(count, dtype=jnp.int32)
    own_row = jnp.sum(jnp.where((picked == band)[:, None], ritz, 0.0), 0)
    other_row = jnp.sum(jnp.where((picked == band ^ 1)[:, None], ritz, 0.0), 0)

    def part(hop):
        to = picked == band ^ (2 * hop)
        return (
            jnp.sum(jnp.where(to, own_row, 0.0)) * filtered
            + jnp.sum(jnp.where(to, other_row, 0.0)) * other
        )

    rotated = part(0)
    arrived = [lax.ppermute(part(hop), "band", [(i, i ^ (2 * hop)) for i in range(count)]) for hop in (1, 2, 3)]
    for value in arrived:
        rotated = rotated + value
    return (filtered, rotated)


def solution(mesh):
    in_specs = (
        P("band", "dom", None, None),
        P("dom", None, None),
        P("dom", None),
        P("dom"),
        P("dom", None, None),
        P("dom", None),
        P(),
    )
    out_specs = (P("band", "dom", None, None), P("band", "dom", None, None))
    return jax.shard_map(shards, mesh=mesh, in_specs=in_specs, out_specs=out_specs, check_vma=False)
```

time: 747 us -> 73.3 us (0.10)
  other arithmetic: 345 us -> 9.15 us
  local copies, waits for them, and re-layouts: 315 us -> 8.54 us
  blocking collectives: 23.4 us -> 0 us
  waiting for transfers between devices: 35.4 us -> 21.9 us
  Pallas kernels: 0 us -> 11.8 us
  matrix products: 8.15 us -> 0 us
    scatter-add x4 -> x0, other arithmetic: 337 us -> none  [nonlocal_term(): jnp.zeros((orbits, out_planes * rows * columns), jnp.float32)]
    gather x4 -> x0, local copies, waits for them, and re-layouts: 272 us -> none  [nonlocal_term(): values = field_in.reshape(orbits, -1)[:, flat_in]]
    slice x104 -> x0, local copies, waits for them, and re-layouts: 33.6 us -> none  [the longest x48 18.9 us: laplace_slab(): along_y = jnp.roll(middle, reach, 2) + jnp.roll(middle, -reach, 2)]
    all_gather x1 -> x0, blocking collectives: 23.4 us -> none  [shards(): lax.all_gather(current, 'band', axis=0, tiled=True)]
    ppermute x12 -> x8, waiting for transfers between devices: 35.4 us -> 21.9 us  [the longest x1 12.2 us: shards(): low = lax.ppermute(up, 'dom', ring('dom', 1))]
    pallas_call x0 -> x3, Pallas kernels: none -> 11.8 us  [the longest x2 11.7 us: run_pair(): pl.pallas_call(lambda *refs: pair_kernel(first_pair, *refs), out_shape=ou...]
    dot_general x9 -> x0, matrix products: 8.15 us -> none  [the longest x4 4.14 us: nonlocal_term(): jnp.einsum('nas,als->nal', values, projectors, precision=lax.Precision.HI...]
    add x0 -> x3, other arithmetic: none -> 7.51 us  [the longest x1 4.62 us: part(): jnp.sum(jnp.where(to, own_row, 0.0)) * filtered]
  transfers between devices with their start and end apart: 12 -> 8, of which waited for: 9 -> 6; matrix products, arithmetic and copies ran while one was open for 2% -> 1% of each run, Pallas kernels for 0% -> 0%
where the time goes in v1:
time: 73.3 us; the launch traced here: 72.8 us
  waiting for transfers between devices  21.9 us (30%)
  starting transfers between devices  20.1 us (27%)
  Pallas kernels  11.8 us (16%)
  other arithmetic  9.15 us (12%)
  local copies, waits for them, and re-layouts  8.54 us (12%)
  between operations  1.37 us (2%)
    ppermute x1, waiting for transfers between devices, shards(): low = lax.ppermute(up, 'dom', ring('dom', 1))  12.2 us
    pallas_call x2, Pallas kernels, run_pair(): pl.pallas_call(lambda *refs: pair_kernel(first_pair, *refs), out_shape=ou...  11.7 us
    unnamed x20, local copies, waits for them, and re-layouts  7.36 us
    ppermute x3, waiting for transfers between devices, shards(): lax.ppermute(part(hop), 'band', [(i, i ^ 2 * hop) for i in range(count)])  7.24 us
    ppermute x1, starting transfers between devices, shards(): high = lax.ppermute(down, 'dom', ring('dom', -1))  6.65 us
    ppermute x1, starting transfers between devices, shards(): high_y = lax.ppermute(second, 'dom', ring('dom', -1))  4.77 us
    add x1, other arithmetic, part(): jnp.sum(jnp.where(to, own_row, 0.0)) * filtered  4.62 us
    ppermute x3, starting transfers between devices, shards(): lax.ppermute(part(hop), 'band', [(i, i ^ 2 * hop) for i in range(count)])  4 us
  transfers between devices with their start and end apart: 8, of which 6 were waited for; matrix products, arithmetic and copies ran while one was open for 1% of the time, Pallas kernels for 0%

profile of v1, /device:TPU:1, one launch (start us, length us, event | category | flops | bytes accessed | tf_op | source)
XLA Modules:
  0.0 72.8 jit_solution(14579425251309071828)
XLA Ops:
  0.6 0.8 %slice_bitcast_fusion.2 = (s32[32]{0:T(128)S(1)}, s32[32]{0:T(128)S(1)}, s32[32]{0:T(128)S(1)}) fusion(s32[32,3]{0,1:T(4,128)} %param.11), kind=kLoop, calls=%fused_computation.34 | loop fusion | bytes 768 | tf_op jit(solution)/shard_map/add | solution.py:295
  2.3 0.7 multiply_bitcast_fusion
  3.4 1.0 %copy-done = f32[32,8,384]{2,1,0:T(8,128)S(1)} copy-done((f32[32,8,384]{2,1,0:T(8,128)S(1)}, f32[32,8,384]{2,1,0:T(8,128)}, u32[]{:S(2)}) %copy-start) | copy-done | bytes 393240
  4.4 0.9 %copy-done.2 = f32[12,16,128]{2,1,0:T(8,128)S(1)} copy-done((f32[12,16,128]{2,1,0:T(8,128)S(1)}, f32[12,16,128]{2,1,0:T(8,128)}, u32[]{:S(2)}) %copy-start.2) | copy-done | bytes 98328
  5.3 0.9 %copy-done.7 = f32[1,12,16,128]{3,2,1,0:T(8,128)S(1)} copy-done((f32[1,12,16,128]{3,2,1,0:T(8,128)S(1)}, f32[1,12,16,128]{3,2,1,0:T(8,128)}, u32[]{:S(2)}) %copy-start.7) | copy-done | bytes 98328
  6.3 2.1 %collective-permute-start = (f32[1088,128]{1,0:T(8,128)S(1)}, f32[1088,128]{1,0:T(8,128)S(1)}, u32[]{:S(2)}, u32[]{:S(2)}) collective-permute-start(f32[1088,128]{1,0:T(8,128)S(1)} %get-tuple-element.7), channel_id=1, source_target_pairs={{0,8},{8,16},{16,24},{24,32},{32,40},{40,48},{48,56},{56,64},{64,7... | collective-permute-start | bytes 1671176 | tf_op jit(solution)/shard_map/ppermute | solution.py:315
  8.4 6.6 %collective-permute-start.1 = (f32[1088,128]{1,0:T(8,128)S(1)}, f32[1088,128]{1,0:T(8,128)S(1)}, u32[]{:S(2)}, u32[]{:S(2)}) collective-permute-start(f32[1088,128]{1,0:T(8,128)S(1)} %get-tuple-element.8), channel_id=1, source_target_pairs={{0,248},{8,0},{16,8},{24,16},{32,24},{40,32},{48,40},{56,48},{64,5... | collective-permute-start | bytes 1671176 | tf_op jit(solution)/shard_map/ppermute | solution.py:316
  15.1 12.2 %collective-permute-done.refs_1_.refs_5_ = f32[1088,128]{1,0:T(8,128)S(1)} collective-permute-done((f32[1088,128]{1,0:T(8,128)S(1)}, f32[1088,128]{1,0:T(8,128)S(1)}, u32[]{:S(2)}, u32[]{:S(2)}) %collective-permute-start) | collective-permute-done | bytes 557088 | tf_op jit(solution)/shard_map/ppermute | solution.py:315
  27.3 1.0 %copy-done.1 = f32[32,8,384]{2,1,0:T(8,128)S(1)} copy-done((f32[32,8,384]{2,1,0:T(8,128)S(1)}, f32[32,8,384]{2,1,0:T(8,128)}, u32[]{:S(2)}) %copy-start.1) | copy-done | bytes 393240
  28.3 0.9 %copy-done.3 = f32[12,16,128]{2,1,0:T(8,128)S(1)} copy-done((f32[12,16,128]{2,1,0:T(8,128)S(1)}, f32[12,16,128]{2,1,0:T(8,128)}, u32[]{:S(2)}) %copy-start.3) | copy-done | bytes 98328
  29.2 0.9 %copy-done.5 = bf16[256,256]{1,0:T(8,128)(2,1)S(1)} copy-done((bf16[256,256]{1,0:T(8,128)(2,1)S(1)}, bf16[256,256]{1,0:T(8,128)(2,1)}, u32[]{:S(2)}) %copy-start.5) | copy-done | bytes 131096
  30.1 0.9 %copy-done.6 = bf16[384,128]{1,0:T(8,128)(2,1)S(1)} copy-done((bf16[384,128]{1,0:T(8,128)(2,1)S(1)}, bf16[384,128]{1,0:T(8,128)(2,1)}, u32[]{:S(2)}) %copy-start.6) | copy-done | bytes 98328
  31.0 0.9 %copy-done.8 = f32[1,12,16,128]{3,2,1,0:T(8,128)S(1)} copy-done((f32[1,12,16,128]{3,2,1,0:T(8,128)S(1)}, f32[1,12,16,128]{3,2,1,0:T(8,128)}, u32[]{:S(2)}) %copy-start.8) | copy-done | bytes 98328
  31.9 7.3 %two_steps.2 = (f32[1,12,16,128]{3,2,1,0:T(8,128)S(1)}, f32[24,16,128]{2,1,0:T(8,128)S(1)}, f32[3,48,8,256]{3,2,1,0:T(8,128)S(1)}) custom-call(f32[1,12,16,128]{3,2,1,0:T(8,128)S(1)} %copy-done.8, f32[1088,128]{1,0:T(8,128)S(1)} %collective-permute-done.refs_1_.refs_5_, f32[1088,128]{1,0:T(8,128)S(1)} %collective-permute-done.1.refs_2_.refs_6_, ...), custom_call_target="tpu_custom_call" | custom-call | tf_op jit(solution)/shard_map/two_steps/pallas_call | solution.py:276
  39.3 4.8 %collective-permute-start.3 = (f32[1,12,16,128]{3,2,1,0:T(8,128)S(1)}, f32[1,12,16,128]{3,2,1,0:T(8,128)S(1)}, u32[]{:S(2)}, u32[]{:S(2)}) collective-permute-start(f32[1,12,16,128]{3,2,1,0:T(8,128)S(1)} %get-tuple-element.9.refs_0_), channel_id=1, source_target_pairs={{0,248},{8,0},{16,8},{24,16},{32,24},{40,32},{48,40},{56,48},{64,5... | collective-permute-start | bytes 294920 | tf_op jit(solution)/shard_map/ppermute | solution.py:320
  44.2 1.9 %collective-permute-done.2.refs_1_ = f32[1,12,16,128]{3,2,1,0:T(8,128)S(1)} collective-permute-done((f32[1,12,16,128]{3,2,1,0:T(8,128)S(1)}, f32[1,12,16,128]{3,2,1,0:T(8,128)S(1)}, u32[]{:S(2)}, u32[]{:S(2)}) %collective-permute-start.2) | collective-permute-done | bytes 98336 | tf_op jit(solution)/shard_map/ppermute | solution.py:319
  46.1 4.3 %two_steps.3 = f32[1,12,16,128]{3,2,1,0:T(8,128)} custom-call(f32[1,12,16,128]{3,2,1,0:T(8,128)S(1)} %get-tuple-element.9.refs_0_, f32[1,12,16,128]{3,2,1,0:T(8,128)S(1)} %collective-permute-done.2.refs_1_, f32[1,12,16,128]{3,2,1,0:T(8,128)S(1)} %collective-permute-done.3.refs_2_, f32[24,16,128]{2,1,0:T(8,128)S(1)} %get-tuple-element.10.refs_3_, ...), custom_call_target="tpu_custom_call" | custom-call | tf_op jit(solution)/shard_map/two_steps/pallas_call | solution.py:276
  50.5 2.5 %collective-permute-start.4 = (f32[1,12,16,128]{3,2,1,0:T(8,128)}, f32[1,12,16,128]{3,2,1,0:T(8,128)S(1)}, u32[]{:S(2)}, u32[]{:S(2)}) collective-permute-start(f32[1,12,16,128]{3,2,1,0:T(8,128)} %two_steps.3), channel_id=1, source_target_pairs={{0,1},{1,0},{2,3},{3,2},{4,5},{5,4},{6,7},{7,6},{8,9},{9,8},{10,11... | collective-permute-start | bytes 294920 | tf_op jit(solution)/shard_map/ppermute | solution.py:327
  54.1 4.6 %multiply_add_fusion.2 = (f32[1,12,16,128]{3,2,1,0:T(8,128)S(1)}, f32[1,12,16,128]{3,2,1,0:T(8,128)S(1)}, f32[1,12,16,128]{3,2,1,0:T(8,128)S(1)}) fusion(f32[1,12,16,128]{3,2,1,0:T(8,128)S(1)} %collective-permute-done.4, f32[1,12,16,128]{3,2,1,0:T(8,128)} %two_steps.3, f32[]{:T(128)} %get-tuple-element.21, f32[]{:T(128)} %get-tuple-element.28, ...), kind=kLoop, calls=%fused_computation.3 | loop fusion | flops 221184 | bytes 491544 | tf_op jit(solution)/shard_map/add | solution.py:335
  58.7 1.4 %collective-permute-start.5 = (f32[1,12,16,128]{3,2,1,0:T(8,128)S(1)}, f32[1,12,16,128]{3,2,1,0:T(8,128)S(1)}, u32[]{:S(2)}, u32[]{:S(2)}) collective-permute-start(f32[1,12,16,128]{3,2,1,0:T(8,128)S(1)} %get-tuple-element.22), channel_id=1, source_target_pairs={{0,2},{1,3},{2,0},{3,1},{4,6},{5,7},{6,4},{7,5},{8,10},{9,11},{10,... | collective-permute-start | bytes 294920 | tf_op jit(solution)/shard_map/ppermute | solution.py:340
  60.1 2.6 %collective-permute-start.6 = (f32[1,12,16,128]{3,2,1,0:T(8,128)S(1)}, f32[1,12,16,128]{3,2,1,0:T(8,128)S(1)}, u32[]{:S(2)}, u32[]{:S(2)}) collective-permute-start(f32[1,12,16,128]{3,2,1,0:T(8,128)S(1)} %get-tuple-element.24), channel_id=1, source_target_pairs={{0,4},{1,5},{2,6},{3,7},{4,0},{5,1},{6,2},{7,3},{8,12},{9,13},{10,... | collective-permute-start | bytes 294920 | tf_op jit(solution)/shard_map/ppermute | solution.py:340
  62.8 4.6 %collective-permute-done.6 = f32[1,12,16,128]{3,2,1,0:T(8,128)S(1)} collective-permute-done((f32[1,12,16,128]{3,2,1,0:T(8,128)S(1)}, f32[1,12,16,128]{3,2,1,0:T(8,128)S(1)}, u32[]{:S(2)}, u32[]{:S(2)}) %collective-permute-start.6) | collective-permute-done | bytes 98336 | tf_op jit(solution)/shard_map/ppermute | solution.py:340
  67.4 2.6 %collective-permute-done.7 = f32[1,12,16,128]{3,2,1,0:T(8,128)S(1)} collective-permute-done((f32[1,12,16,128]{3,2,1,0:T(8,128)S(1)}, f32[1,12,16,128]{3,2,1,0:T(8,128)S(1)}, u32[]{:S(2)}, u32[]{:S(2)}) %collective-permute-start.7) | collective-permute-done | bytes 98336 | tf_op jit(solution)/shard_map/ppermute | solution.py:340
  70.0 2.8 %add_add_fusion = f32[1,12,16,128]{3,2,1,0:T(8,128)} fusion(f32[1,12,16,128]{3,2,1,0:T(8,128)S(1)} %collective-permute-done.7, f32[1,12,16,128]{3,2,1,0:T(8,128)S(1)} %collective-permute-done.6, f32[1,12,16,128]{3,2,1,0:T(8,128)S(1)} %collective-permute-done.5, f32[1,12,16,128]{3,2,1,0:T(8,128)S(1)} %collective-permute-done.4, ...), kind=kLoop, calls=%fused_computation.1 | loop fusion | flops 147456 | bytes 589832 | tf_op jit(solution)/shard_map/add | solution.py:342
  (34 shorter events, 2.2 us)
Async XLA Ops:
  3.4 1.0 %copy-start = (f32[32,8,384]{2,1,0:T(8,128)S(1)}, f32[32,8,384]{2,1,0:T(8,128)}, u32[]{:S(2)}) copy-start(f32[32,8,384]{2,1,0:T(8,128)} %refs_4_.1) | copy-start | bytes 1179652
  4.4 0.9 %copy-start.2 = (f32[12,16,128]{2,1,0:T(8,128)S(1)}, f32[12,16,128]{2,1,0:T(8,128)}, u32[]{:S(2)}) copy-start(f32[12,16,128]{2,1,0:T(8,128)} %refs_7_.2) | copy-start | bytes 294916
  5.3 0.9 %copy-start.7 = (f32[1,12,16,128]{3,2,1,0:T(8,128)S(1)}, f32[1,12,16,128]{3,2,1,0:T(8,128)}, u32[]{:S(2)}) copy-start(f32[1,12,16,128]{3,2,1,0:T(8,128)} %refs_0_.1) | copy-start | bytes 294916
  6.2 37.9 %copy-start.9 = (f32[8,8]{1,0:T(8,128)S(1)}, f32[8,8]{1,0:T(8,128)}, u32[]{:S(2)}) copy-start(f32[8,8]{1,0:T(8,128)} %param.15) | copy-start | bytes 772
  6.2 39.9 %copy-start.4 = (f32[12,16,128]{2,1,0:T(8,128)S(1)}, f32[12,16,128]{2,1,0:T(8,128)}, u32[]{:S(2)}) copy-start(f32[12,16,128]{2,1,0:T(8,128)} %refs_7_.2) | copy-start | bytes 294916
  6.3 21.0 %collective-permute-start = (f32[1088,128]{1,0:T(8,128)S(1)}, f32[1088,128]{1,0:T(8,128)S(1)}, u32[]{:S(2)}, u32[]{:S(2)}) collective-permute-start(f32[1088,128]{1,0:T(8,128)S(1)} %get-tuple-element.7), channel_id=1, source_target_pairs={{0,8},{8,16},{16,24},{24,32},{32,40},{40,48},{48,56},{56,64},{64,7... | collective-permute-start | bytes 1671176 | tf_op jit(solution)/shard_map/ppermute | solution.py:315
  8.4 18.9 %collective-permute-start.1 = (f32[1088,128]{1,0:T(8,128)S(1)}, f32[1088,128]{1,0:T(8,128)S(1)}, u32[]{:S(2)}, u32[]{:S(2)}) collective-permute-start(f32[1088,128]{1,0:T(8,128)S(1)} %get-tuple-element.8), channel_id=1, source_target_pairs={{0,248},{8,0},{16,8},{24,16},{32,24},{40,32},{48,40},{56,48},{64,5... | collective-permute-start | bytes 1671176 | tf_op jit(solution)/shard_map/ppermute | solution.py:316
  27.3 1.0 %copy-start.1 = (f32[32,8,384]{2,1,0:T(8,128)S(1)}, f32[32,8,384]{2,1,0:T(8,128)}, u32[]{:S(2)}) copy-start(f32[32,8,384]{2,1,0:T(8,128)} %refs_4_.1) | copy-start | bytes 1179652
  28.3 0.9 %copy-start.3 = (f32[12,16,128]{2,1,0:T(8,128)S(1)}, f32[12,16,128]{2,1,0:T(8,128)}, u32[]{:S(2)}) copy-start(f32[12,16,128]{2,1,0:T(8,128)} %refs_7_.2) | copy-start | bytes 294916
  29.2 0.9 %copy-start.5 = (bf16[256,256]{1,0:T(8,128)(2,1)S(1)}, bf16[256,256]{1,0:T(8,128)(2,1)}, u32[]{:S(2)}) copy-start(bf16[256,256]{1,0:T(8,128)(2,1)} %constant.37.clone.refs_7_.refs_10_) | copy-start | bytes 393220
  30.1 0.9 %copy-start.6 = (bf16[384,128]{1,0:T(8,128)(2,1)S(1)}, bf16[384,128]{1,0:T(8,128)(2,1)}, u32[]{:S(2)}) copy-start(bf16[384,128]{1,0:T(8,128)(2,1)} %constant.36.clone.refs_6_.refs_9_) | copy-start | bytes 294916
  31.0 0.9 %copy-start.8 = (f32[1,12,16,128]{3,2,1,0:T(8,128)S(1)}, f32[1,12,16,128]{3,2,1,0:T(8,128)}, u32[]{:S(2)}) copy-start(f32[1,12,16,128]{3,2,1,0:T(8,128)} %refs_0_.1) | copy-start | bytes 294916
  39.3 6.9 %collective-permute-start.2 = (f32[1,12,16,128]{3,2,1,0:T(8,128)S(1)}, f32[1,12,16,128]{3,2,1,0:T(8,128)S(1)}, u32[]{:S(2)}, u32[]{:S(2)}) collective-permute-start(f32[1,12,16,128]{3,2,1,0:T(8,128)S(1)} %get-tuple-element.9.refs_0_), channel_id=1, source_target_pairs={{0,8},{8,16},{16,24},{24,32},{32,40},{40,48},{48,56},{56,64},{64,7... | collective-permute-start | bytes 294920 | tf_op jit(solution)/shard_map/ppermute | solution.py:319
  39.3 6.8 %collective-permute-start.3 = (f32[1,12,16,128]{3,2,1,0:T(8,128)S(1)}, f32[1,12,16,128]{3,2,1,0:T(8,128)S(1)}, u32[]{:S(2)}, u32[]{:S(2)}) collective-permute-start(f32[1,12,16,128]{3,2,1,0:T(8,128)S(1)} %get-tuple-element.9.refs_0_), channel_id=1, source_target_pairs={{0,248},{8,0},{16,8},{24,16},{32,24},{40,32},{48,40},{56,48},{64,5... | collective-permute-start | bytes 294920 | tf_op jit(solution)/shard_map/ppermute | solution.py:320
  50.5 3.6 %collective-permute-start.4 = (f32[1,12,16,128]{3,2,1,0:T(8,128)}, f32[1,12,16,128]{3,2,1,0:T(8,128)S(1)}, u32[]{:S(2)}, u32[]{:S(2)}) collective-permute-start(f32[1,12,16,128]{3,2,1,0:T(8,128)} %two_steps.3), channel_id=1, source_target_pairs={{0,1},{1,0},{2,3},{3,2},{4,5},{5,4},{6,7},{7,6},{8,9},{9,8},{10,11... | collective-permute-start | bytes 294920 | tf_op jit(solution)/shard_map/ppermute | solution.py:327
  58.7 4.1 %collective-permute-start.5 = (f32[1,12,16,128]{3,2,1,0:T(8,128)S(1)}, f32[1,12,16,128]{3,2,1,0:T(8,128)S(1)}, u32[]{:S(2)}, u32[]{:S(2)}) collective-permute-start(f32[1,12,16,128]{3,2,1,0:T(8,128)S(1)} %get-tuple-element.22), channel_id=1, source_target_pairs={{0,2},{1,3},{2,0},{3,1},{4,6},{5,7},{6,4},{7,5},{8,10},{9,11},{10,... | collective-permute-start | bytes 294920 | tf_op jit(solution)/shard_map/ppermute | solution.py:340
  60.1 7.3 %collective-permute-start.6 = (f32[1,12,16,128]{3,2,1,0:T(8,128)S(1)}, f32[1,12,16,128]{3,2,1,0:T(8,128)S(1)}, u32[]{:S(2)}, u32[]{:S(2)}) collective-permute-start(f32[1,12,16,128]{3,2,1,0:T(8,128)S(1)} %get-tuple-element.24), channel_id=1, source_target_pairs={{0,4},{1,5},{2,6},{3,7},{4,0},{5,1},{6,2},{7,3},{8,12},{9,13},{10,... | collective-permute-start | bytes 294920 | tf_op jit(solution)/shard_map/ppermute | solution.py:340
  62.7 7.2 %collective-permute-start.7 = (f32[1,12,16,128]{3,2,1,0:T(8,128)S(1)}, f32[1,12,16,128]{3,2,1,0:T(8,128)S(1)}, u32[]{:S(2)}, u32[]{:S(2)}) collective-permute-start(f32[1,12,16,128]{3,2,1,0:T(8,128)S(1)} %get-tuple-element.23), channel_id=1, source_target_pairs={{0,6},{1,7},{2,4},{3,5},{4,2},{5,3},{6,0},{7,1},{8,14},{9,15},{10,... | collective-permute-start | bytes 294920 | tf_op jit(solution)/shard_map/ppermute | solution.py:340

commit v2 on v0

v2 whole, which is shorter than its diff:
```python
import jax
import jax.numpy as jnp
from jax import lax
from jax.experimental import pallas as pl
from jax.experimental.pallas import tpu as pltpu
from jax.sharding import PartitionSpec as P

STENCIL = (
    -5369.0 / 1800.0,
    12.0 / 7.0,
    -15.0 / 56.0,
    10.0 / 189.0,
    -1.0 / 112.0,
    2.0 / 1925.0,
    -1.0 / 16632.0,
)
LOWER = -1.6
UPPER = 24.0
CENTER = 0.5 * (UPPER + LOWER)
HALF = 0.5 * (UPPER - LOWER)

CX, NY, NZ = 12, 16, 128
ATOMS = 32
NPROJ, BX, BY, BZ = 8, 6, 8, 8
LANES = ATOMS * BZ
SPAN = CX + BX - 1
PAIRS = NPROJ * BX
TILE_Y, TILE_POT, TILE_P, TILE_META, TILES = 0, 24, 36, 84, 88
ROW_Z, ROW_X0, ROW_Y0 = 0, 1, 2

VMEM = pl.BlockSpec(memory_space=pltpu.VMEM)
HBM = pl.BlockSpec(memory_space=pltpu.HBM)
SMEM = pl.BlockSpec(memory_space=pltpu.SMEM)


def shape(*dims, dtype=jnp.float32):
    return jax.ShapeDtypeStruct(dims, dtype)


def call(kernel, outs, ins, args, name, scratch=(), out_specs=None, flops=1_000_000):
    return pl.pallas_call(
        kernel,
        out_shape=outs,
        in_specs=ins,
        out_specs=out_specs or [VMEM] * len(outs),
        scratch_shapes=list(scratch),
        compiler_params=pltpu.CompilerParams(vmem_limit_bytes=32 * 2**20),
        cost_estimate=pl.CostEstimate(flops=flops, bytes_accessed=2_000_000, transcendentals=0),
        name=name,
    )(*args)


def two_terms(value, axis):
    high = value.astype(jnp.bfloat16)
    low = (value - high.astype(jnp.float32)).astype(jnp.bfloat16)
    return jnp.concatenate([high, low], axis)


def dot(left, right):
    return jnp.dot(left, right, preferred_element_type=jnp.float32)


def half(tile):
    return slice(128 * tile, 128 * tile + 128)


def pack_kernel(y_hbm, pot_hbm, proj_hbm, gamma_hbm, pos_hbm, count_ref,
                up_ref, down_ref, pot_ref, proj_ref, gamma_ref, pos_ref, sems):
    core = lax.axis_index("band") % 2
    first = 16 * core
    copies = [
        pltpu.make_async_copy(gamma_hbm, gamma_ref, sems.at[0]),
        pltpu.make_async_copy(pos_hbm, pos_ref, sems.at[1]),
    ]
    moves = [
        (pot_hbm, pot_ref),
        (pot_hbm.at[pl.ds(12, 12)], up_ref.at[pl.ds(TILE_POT, 12)]),
        (pot_hbm.at[pl.ds(0, 12)], down_ref.at[pl.ds(TILE_POT, 12)]),
    ]
    for out in (up_ref, down_ref):
        moves.append((y_hbm, out.at[pl.ds(TILE_Y, 24)]))
        for part in range(3):
            source = proj_hbm.at[pl.ds(first, 16), pl.ds(0, 8), pl.ds(128 * part, 128)]
            moves.append((source, out.at[pl.ds(TILE_P + 16 * part, 16)]))
    for part in range(3):
        source = proj_hbm.at[pl.ds(0, ATOMS), pl.ds(0, 8), pl.ds(128 * part, 128)]
        moves.append((source, proj_ref.at[pl.ds(ATOMS * part, ATOMS)]))
    for n, (source, target) in enumerate(moves):
        copies.append(pltpu.make_async_copy(source, target, sems.at[2 + n]))
    for copy in copies:
        copy.start()
    copies[0].wait()
    copies[1].wait()
    live = lax.broadcasted_iota(jnp.int32, (1, ATOMS), 1) < count_ref[0]
    weight = jnp.where(live, gamma_ref[...], 0.0)
    repeat = lax.broadcasted_iota(jnp.int32, (ATOMS, LANES), 1) >> 3
    repeat = jnp.where(repeat == lax.broadcasted_iota(jnp.int32, (ATOMS, LANES), 0), 1.0, 0.0)
    corner = pos_ref[...].astype(jnp.float32)
    spread = lambda v: jnp.dot(v, repeat, preferred_element_type=jnp.float32, precision=lax.Precision.HIGHEST)
    weight = spread(weight)
    column = spread(corner)[2:3] + (lax.broadcasted_iota(jnp.int32, (1, LANES), 1) & 7).astype(jnp.float32)
    column = jnp.where(column >= NZ, column - NZ, column)
    for out in (up_ref, down_ref):
        for tile in range(2):
            out[TILE_META + 2 * tile] = weight[:, half(tile)]
            out[TILE_META + 2 * tile + 1] = jnp.broadcast_to(column[:, half(tile)], (8, 128))
        out[TILE_META + 1, ROW_X0 : ROW_X0 + 1, 0:ATOMS] = corner[0:1]
        out[TILE_META + 1, ROW_Y0 : ROW_Y0 + 1, 0:ATOMS] = corner[1:2]
    for copy in copies[2:]:
        copy.wait()


def spread_projectors(read, work, table):
    lane = lax.broadcasted_iota(jnp.int32, (8, 128), 1)
    for part in range(3):
        items = [read(part, a) for a in range(16)]
        for bit in (1, 2, 4, 8):
            upper = (lane & (8 * bit)) != 0
            for p in range(16):
                if p & bit:
                    continue
                q = p | bit
                first, second = items[p], items[q]
                items[p] = jnp.where(upper, pltpu.roll(second, 8 * bit, 1), first)
                items[q] = jnp.where(upper, second, pltpu.roll(first, 128 - 8 * bit, 1))
        for g in range(16):
            i, j = 2 * part + g // 8, g % 8
            work[i, 8 * j : 8 * j + 8, :] = items[g]
    for i in range(BX):
        for l in range(NPROJ):
            table[l * BX + i] = work.at[i][pl.ds(l, 8, stride=8), :]


def prepare_kernel(proj_ref, table_ref, zst_ref, sums_ref, work):
    for tile in range(2):
        read = lambda part, a: proj_ref[ATOMS * part + 16 * tile + a]
        spread_projectors(read, work, table_ref.at[tile])
    apart = lax.broadcasted_iota(jnp.int32, (NZ, NZ), 0) - lax.broadcasted_iota(jnp.int32, (NZ, NZ), 1)
    full = jnp.zeros((NZ, NZ), jnp.float32)
    for reach in range(1, 7):
        near = ((apart & (NZ - 1)) == reach) | ((apart & (NZ - 1)) == NZ - reach)
        full = jnp.where(near, STENCIL[reach], full)
    high = full.astype(jnp.bfloat16)
    zst_ref[0:128, :] = high
    zst_ref[128:256, :] = high
    zst_ref[256:384, :] = (full - high.astype(jnp.float32)).astype(jnp.bfloat16)
    atom = lambda axis: lax.broadcasted_iota(jnp.int32, (LANES, LANES), axis) >> 3
    sums_ref[...] = jnp.where(atom(0) == atom(1), 1.0, 0.0).astype(jnp.bfloat16)


def fill(padded, plane, value):
    count = value.shape[0]
    padded[plane : plane + count, 8:24, :] = value
    padded[plane : plane + count, 0:8, :] = value[:, 8:16]
    padded[plane : plane + count, 24:32, :] = value[:, 0:8]


class Boxes:
    def __init__(self, sources, held, sems):
        self.sources, self.held = sources, held
        self.copies = [
            pltpu.make_async_copy(s.at[TILE_META + 1], h, sems.at[n]) for n, (s, h) in enumerate(zip(sources, held))
        ]
        for copy in self.copies:
            copy.start()

    def wait(self):
        for copy in self.copies:
            copy.wait()

    def place(self, group, atom):
        held = self.held[group]
        return held[ROW_X0, atom].astype(jnp.int32), held[ROW_Y0, atom].astype(jnp.int32)

    def weight(self, group):
        source = self.sources[group]
        return jnp.concatenate([source[TILE_META], source[TILE_META + 2]], 1)

    def one_hot(self, group):
        source = self.sources[group]
        column = jnp.concatenate(
            [source[TILE_META + 1 + 2 * t, ROW_Z : ROW_Z + 1, :] for t in range(2)], 1
        )
        cells = lax.broadcasted_iota(jnp.int32, (NZ, LANES), 0).astype(jnp.float32)
        return jnp.where(cells == column, 1.0, 0.0).astype(jnp.bfloat16)


def gather_columns(group, field2, first_in, planes_in, skip, gathered, onehot):
    rows = slice(NY * first_in, NY * (first_in + planes_in))
    columns = dot(field2[rows, :], jnp.concatenate([onehot, onehot], 0)).reshape(planes_in, NY, LANES)
    for tile in range(2):
        part = columns[:, :, half(tile)]
        gathered[group, tile, skip : skip + planes_in, 0:16, :] = part
        gathered[group, tile, skip : skip + planes_in, 16:24, :] = part[:, 0:8]


def read_windows(group, gathered, boxes):
    lane = lax.broadcasted_iota(jnp.int32, (8, 128), 1)
    values = [[jnp.zeros((8, 128), jnp.float32)] * 2 for _ in range(BX)]
    for a in range(16):
        mine = (lane >> 3) == a
        for tile in range(2):
            x0, y0 = boxes.place(group, 16 * tile + a)
            for i in range(BX):
                values[i][tile] = jnp.where(mine, gathered[group, tile, x0 + i, pl.ds(y0, 8), :], values[i][tile])
    return values


def contributions(group, values, table, placed, boxes, sums):
    coeffs = []
    for tile in range(2):
        rows = []
        for l in range(NPROJ):
            total = values[0][tile] * table[tile, l * BX]
            for i in range(1, BX):
                total = total + values[i][tile] * table[tile, l * BX + i]
            rows.append(jnp.sum(total, 0, keepdims=True))
        coeffs.append(jnp.concatenate(rows, 0))
    both = dot(two_terms(jnp.concatenate(coeffs, 1), 0), sums)
    coeffs = (both[:8] + both[8:]) * boxes.weight(group)
    lane = lax.broadcasted_iota(jnp.int32, (8, 128), 1)
    contrib = [[None] * 2 for _ in range(BX)]
    for tile in range(2):
        rows = [jnp.broadcast_to(coeffs[l : l + 1, half(tile)], (8, 128)) for l in range(NPROJ)]
        for i in range(BX):
            total = rows[0] * table[tile, i]
            for l in range(1, NPROJ):
                total = total + rows[l] * table[tile, l * BX + i]
            contrib[i][tile] = total
    for a in range(16):
        mine = (lane >> 3) == a
        for tile in range(2):
            x0, y0 = boxes.place(group, 16 * tile + a)
            for i in range(BX):
                pltpu.store(placed.at[group, tile, x0 + i, pl.ds(y0, 8), :], contrib[i][tile], mask=mine)


def spread_group(group, first, count, placed, onehot):
    planes = slice(first, first + count)
    tiles = []
    for tile in range(2):
        folded = placed[group, tile, planes, 0:8, :] + placed[group, tile, planes, 16:24, :]
        tiles.append(jnp.concatenate([folded, placed[group, tile, planes, 8:16, :]], 1).reshape(count * NY, 128))
    twice = jnp.concatenate([onehot, onehot], 1)
    spread = lax.dot_general(
        two_terms(jnp.concatenate(tiles, 1), 1), twice, (((1,), (1,)), ((), ())),
        preferred_element_type=jnp.float32,
    )
    return spread.reshape(count, NY, NZ)


def along_z(field2, rows, zst_ref):
    return dot(field2[rows, :], zst_ref[0:256, :]) + dot(field2[rows, 0:128], zst_ref[256:384, :])


def stencil_plane(padded, plane):
    total = 3.0 * STENCIL[0] * padded[plane, 8:24, :]
    for reach in range(1, 7):
        along_x = padded[plane + reach, 8:24, :] + padded[plane - reach, 8:24, :]
        along_y = padded[plane, 8 + reach : 24 + reach, :] + padded[plane, 8 - reach : 24 - reach, :]
        total = total + STENCIL[reach] * (along_x + along_y)
    return total


def potential_plane(p, low_ref, pot_ref, high_ref):
    source, tile = (
        (low_ref, TILE_POT + 2 * p) if p < 6 else (pot_ref, 2 * (p - 6)) if p < 18 else (high_ref, TILE_POT + 2 * (p - 18))
    )
    return source[tile : tile + 2].reshape(NY, NZ)


def load_fields(fields, padded, field2):
    for n, value in enumerate(fields):
        fill(padded, 12 * n, value.reshape(CX, NY, NZ))
        field2[192 * n : 192 * n + 192, :] = two_terms(value.reshape(192, NZ), 1)


def head_kernel(up_ref, low_ref, high_ref, pot_ref, table_ref, zst_ref, sums_ref,
                half_ref, values_ref, partial_ref,
                low_xy, own_xy, high_xy, padded, field2, gathered, placed, local, nonlocal_, work, sems):
    boxes = Boxes((low_ref, up_ref, high_ref), (low_xy, own_xy, high_xy), sems)
    load_fields([r[TILE_Y : TILE_Y + 24] for r in (low_ref, up_ref, high_ref)], padded, field2)
    placed[...] = jnp.zeros_like(placed)
    gathered[2, :, 12:SPAN] = jnp.zeros((2, SPAN - 12, 24, 128), jnp.float32)
    own_hot = boxes.one_hot(1)
    gather_columns(1, field2, 12, SPAN, 0, gathered, own_hot)
    gather_columns(0, field2, 0, SPAN, 0, gathered, boxes.one_hot(0))
    gather_columns(2, field2, 24, 12, 0, gathered, boxes.one_hot(2))
    boxes.wait()
    contributions(1, read_windows(1, gathered, boxes), table_ref, placed, boxes, sums_ref[...])
    for n, group in enumerate((0, 2)):
        values = read_windows(group, gathered, boxes)
        for i in range(BX):
            for tile in range(2):
                values_ref[n, i, tile] = values[i][tile]
    local[...] = along_z(field2, slice(96, 480), zst_ref).reshape(24, NY, NZ)
    nonlocal_[0:6] = jnp.zeros((6, NY, NZ), jnp.float32)
    nonlocal_[6:23] = spread_group(1, 0, 17, placed, own_hot)
    nonlocal_[23] = jnp.zeros((NY, NZ), jnp.float32)
    for n, source in enumerate((low_ref, high_ref)):
        spread_projectors(lambda part, a: source[TILE_P + 16 * part + a], work, half_ref.at[n])
    for p in range(24):
        laplace = stencil_plane(padded, p + 6) + local[p]
        pot = potential_plane(p, low_ref, pot_ref, high_ref)
        partial_ref[p] = (-0.5 * laplace + (pot - CENTER) * padded[p + 6, 8:24, :] + nonlocal_[p]) * (1.0 / HALF)


def second_step(boxes, hots, padded1, field2, gathered, placed, local, nonlocal_, pot_ref, tables, zst_ref, sums):
    for group, first, planes, skip in ((0, 0, 11, 6), (1, 6, SPAN, 0)):
        gather_columns(group, field2, first, planes, skip, gathered, hots[group])
    for group in range(2):
        contributions(group, read_windows(group, gathered, boxes), tables[group], placed, boxes, sums)
    local[0:12] = along_z(field2, slice(96, 288), zst_ref).reshape(12, NY, NZ)
    nonlocal_[0:12] = spread_group(1, 0, 12, placed, hots[1])
    nonlocal_[0:5] += spread_group(0, 12, 5, placed, hots[0])
    for p in range(12):
        here = padded1[p + 6, 8:24, :]
        laplace = stencil_plane(padded1, p + 6) + local[p]
        pot = potential_plane(p + 6, None, pot_ref, None)
        yield p, (-0.5 * laplace + (pot - CENTER) * here + nonlocal_[p]) * (2.0 / HALF)


def tail_kernel(up_ref, low_ref, high_ref, pot_ref, table_ref, zst_ref, sums_ref,
                half_ref, values_ref, partial_ref, lowsib_ref, highsib_ref,
                out_ref, kept_ref, tables_ref,
                low_xy, own_xy, high_xy, padded1, field2, gathered, placed, local, nonlocal_, work, sems):
    core = lax.axis_index("band") % 2
    boxes = Boxes((low_ref, up_ref, high_ref), (low_xy, own_xy, high_xy), sems)
    placed[...] = jnp.zeros_like(placed)
    gathered[0, :, 0:6] = jnp.zeros((2, 6, 24, 128), jnp.float32)
    for n, source in enumerate((lowsib_ref, highsib_ref)):
        spread_projectors(lambda part, a: source[TILE_P + 16 * part + a], work, tables_ref.at[n, 1 - core])
        tables_ref[n, core] = half_ref[n]
    hots = [boxes.one_hot(g) for g in range(3)]
    boxes.wait()
    sums = sums_ref[...]
    for n, group in enumerate((0, 2)):
        values = [[values_ref[n, i, tile] for tile in range(2)] for i in range(BX)]
        contributions(group, values, tables_ref.at[n], placed, boxes, sums)
    nonlocal_[0:11] = spread_group(0, 6, 11, placed, hots[0])
    nonlocal_[11:18] = jnp.zeros((7, NY, NZ), jnp.float32)
    nonlocal_[18:24] = spread_group(2, 0, 6, placed, hots[2])
    for p in range(24):
        updated = partial_ref[p] + nonlocal_[p] * (1.0 / HALF)
        kept_ref[p] = updated
        fill(padded1, p, updated[None])
        field2[16 * p : 16 * p + 16, :] = two_terms(updated, 1)
    tables = (tables_ref.at[0], table_ref)
    for p, value in second_step(boxes, hots, padded1, field2, gathered, placed, local, nonlocal_, pot_ref, tables,
                                zst_ref, sums):
        out_ref[2 * p : 2 * p + 2] = (value - up_ref[TILE_Y + 2 * p : TILE_Y + 2 * p + 2].reshape(NY, NZ)).reshape(2, 8, 128)


def last_kernel(up_ref, low_ref, high_ref, pot_ref, table_ref, zst_ref, sums_ref, kept_ref, tables_ref,
                mid_ref, lowy_ref, highy_ref,
                out_ref,
                low_xy, own_xy, high_xy, padded, padded1, field2, gathered, placed, local, nonlocal_, sems):
    boxes = Boxes((low_ref, up_ref, high_ref), (low_xy, own_xy, high_xy), sems)
    load_fields([r[...] for r in (lowy_ref, mid_ref, highy_ref)], padded, field2)
    placed[...] = jnp.zeros_like(placed)
    gathered[2, :, 12:SPAN] = jnp.zeros((2, SPAN - 12, 24, 128), jnp.float32)
    hots = [boxes.one_hot(g) for g in range(3)]
    boxes.wait()
    sums = sums_ref[...]
    tables = (tables_ref.at[0], table_ref, tables_ref.at[1])
    for group, planes in ((0, SPAN), (1, SPAN), (2, 12)):
        gather_columns(group, field2, 12 * group, planes, 0, gathered, hots[group])
    for group in range(3):
        contributions(group, read_windows(group, gathered, boxes), tables[group], placed, boxes, sums)
    local[...] = along_z(field2, slice(96, 480), zst_ref).reshape(24, NY, NZ)
    nonlocal_[0:11] = spread_group(0, 6, 11, placed, hots[0])
    nonlocal_[11:24] = jnp.zeros((13, NY, NZ), jnp.float32)
    nonlocal_[6:23] += spread_group(1, 0, 17, placed, hots[1])
    nonlocal_[18:24] += spread_group(2, 0, 6, placed, hots[2])
    for p in range(24):
        laplace = stencil_plane(padded, p + 6) + local[p]
        pot = potential_plane(p, low_ref, pot_ref, high_ref)
        applied = -0.5 * laplace + (pot - CENTER) * padded[p + 6, 8:24, :] + nonlocal_[p]
        updated = applied * (2.0 / HALF) - kept_ref[p]
        fill(padded1, p, updated[None])
        field2[16 * p : 16 * p + 16, :] = two_terms(updated, 1)
    for p, value in second_step(boxes, hots, padded1, field2, gathered, placed, local, nonlocal_, pot_ref, tables,
                                zst_ref, sums):
        out_ref[2 * p : 2 * p + 2] = (value - padded[p + 12, 8:24, :]).reshape(2, 8, 128)


XY = [pltpu.SMEM((8, 128), jnp.float32)] * 3
PADDED = pltpu.VMEM((36, 32, NZ), jnp.float32)
PADDED1 = pltpu.VMEM((24, 32, NZ), jnp.float32)
FIELD2 = pltpu.VMEM((576, 2 * NZ), jnp.bfloat16)
BOXED = pltpu.VMEM((3, 2, SPAN, 24, 128), jnp.float32)
PLANES = pltpu.VMEM((24, NY, NZ), jnp.float32)
WORK = pltpu.VMEM((BX, BY * NPROJ, 128), jnp.float32)
COPIES = pltpu.SemaphoreType.DMA((3,))


def parts_kernel(ritz_ref, own_ref, other_ref, base_ref, one_ref, two_ref, three_ref, out_hbm, sem):
    copy = pltpu.make_async_copy(own_ref, out_hbm, sem.at[0])
    copy.start()
    band = lax.axis_index("band")
    for hop, target in enumerate((base_ref, one_ref, two_ref, three_ref)):
        to = band ^ (2 * hop)
        target[...] = ritz_ref[band, to] * own_ref[...] + ritz_ref[band ^ 1, to] * other_ref[...]
    copy.wait()


def total_kernel(base_ref, one_ref, two_ref, three_ref, out_ref):
    out_ref[...] = (base_ref[...] + one_ref[...]) + (two_ref[...] + three_ref[...])


def ring(axis, step):
    count = lax.axis_size(axis)
    return [(i, (i + step) % count) for i in range(count)]


def meet(axis, bits):
    return [(i, i ^ bits) for i in range(lax.axis_size(axis))]


def shards(orbitals, potential, atom_pos, atom_count, projectors, gammas, ritz):
    up, down, pot, proj = call(
        pack_kernel,
        [shape(TILES, 8, 128), shape(TILES, 8, 128), shape(24, 8, 128), shape(3 * ATOMS, 8, 128)],
        [HBM] * 5 + [SMEM],
        (orbitals.reshape(24, 8, 128), potential.reshape(24, 8, 128), projectors, gammas.T, atom_pos.T, atom_count),
        "pack",
        [pltpu.VMEM((NPROJ, ATOMS), jnp.float32), pltpu.VMEM((3, ATOMS), jnp.int32), pltpu.SemaphoreType.DMA((16,))],
    )
    low = lax.ppermute(up, "dom", ring("dom", 1))
    high = lax.ppermute(down, "dom", ring("dom", -1))
    table, zst, sums = call(
        prepare_kernel,
        [shape(2, PAIRS, 8, 128), shape(384, NZ, dtype=jnp.bfloat16), shape(LANES, LANES, dtype=jnp.bfloat16)],
        [VMEM],
        (proj,),
        "prepare",
        [WORK],
    )
    lowsib = lax.ppermute(low, "band", meet("band", 1))
    highsib = lax.ppermute(high, "band", meet("band", 1))
    common = (up, low, high, pot, table, zst, sums)
    halves, values, partial = call(
        head_kernel,
        [shape(2, PAIRS, 8, 128), shape(2, BX, 2, 8, 128), shape(24, NY, NZ)],
        [VMEM] * 7,
        common,
        "head",
        XY + [PADDED, FIELD2, BOXED, BOXED, PLANES, PLANES, WORK, COPIES],
    )
    second, first, tables = call(
        tail_kernel,
        [shape(24, 8, 128), shape(24, NY, NZ), shape(2, 2, PAIRS, 8, 128)],
        [VMEM] * 12,
        common + (halves, values, partial, lowsib, highsib),
        "tail",
        XY + [PADDED1, FIELD2, BOXED, BOXED, PLANES, PLANES, WORK, COPIES],
    )
    low_y = lax.ppermute(second, "dom", ring("dom", 1))
    high_y = lax.ppermute(second, "dom", ring("dom", -1))
    (fourth,) = call(
        last_kernel,
        [shape(24, 8, 128)],
        [VMEM] * 12,
        common + (first, tables, second, low_y, high_y),
        "last",
        XY + [PADDED, PADDED1, FIELD2, BOXED, BOXED, PLANES, PLANES, COPIES],
    )
    other = lax.ppermute(fourth, "band", meet("band", 1))
    field = shape(24, 8, 128)
    base, one, two, three, filtered = call(
        parts_kernel,
        [field] * 5,
        [SMEM, VMEM, VMEM],
        (ritz, fourth, other),
        "parts",
        [pltpu.SemaphoreType.DMA((1,))],
        [VMEM] * 4 + [HBM],
    )
    arrived = [lax.ppermute(v, "band", meet("band", 2 * hop)) for hop, v in ((1, one), (2, two), (3, three))]
    (rotated,) = call(total_kernel, [field], [VMEM] * 4, (base, *arrived), "total")
    return (filtered.reshape(orbitals.shape), rotated.reshape(orbitals.shape))


def solution(mesh):
    in_specs = (
        P("band", "dom", None, None),
        P("dom", None, None),
        P("dom", None),
        P("dom"),
        P("dom", None, None),
        P("dom", None),
        P(),
    )
    out_specs = (P("band", "dom", None, None), P("band", "dom", None, None))
    return jax.shard_map(shards, mesh=mesh, in_specs=in_specs, out_specs=out_specs, check_vma=False)
```

time: 747 us -> 61.6 us (0.08)
  other arithmetic: 345 us -> 0 us
  local copies, waits for them, and re-layouts: 315 us -> 3.47 us
  blocking collectives: 23.4 us -> 0 us
  Pallas kernels: 0 us -> 12.6 us
  waiting for transfers between devices: 35.4 us -> 24.3 us
  matrix products: 8.15 us -> 0 us
    scatter-add x4 -> x0, other arithmetic: 337 us -> none  [nonlocal_term(): jnp.zeros((orbits, out_planes * rows * columns), jnp.float32)]
    gather x4 -> x0, local copies, waits for them, and re-layouts: 272 us -> none  [nonlocal_term(): values = field_in.reshape(orbits, -1)[:, flat_in]]
    slice x104 -> x0, local copies, waits for them, and re-layouts: 33.6 us -> none  [the longest x48 18.9 us: laplace_slab(): along_y = jnp.roll(middle, reach, 2) + jnp.roll(middle, -reach, 2)]
    all_gather x1 -> x0, blocking collectives: 23.4 us -> none  [shards(): lax.all_gather(current, 'band', axis=0, tiled=True)]
    pallas_call x0 -> x7, Pallas kernels: none -> 12.6 us  [call(): pl.pallas_call(kernel, out_shape=outs, in_specs=ins, out_specs=out_specs...]
    ppermute x12 -> x10, waiting for transfers between devices: 35.4 us -> 24.3 us  [the longest x3 7.24 us: shards(): lax.ppermute(v, 'band', meet('band', 2 * hop))]
    dot_general x9 -> x0, matrix products: 8.15 us -> none  [the longest x4 4.14 us: nonlocal_term(): jnp.einsum('nas,als->nal', values, projectors, precision=lax.Precision.HI...]
    ppermute x12 -> x10, starting transfers between devices: 16.7 us -> 19.6 us  [the longest x1 8.68 us: shards(): high = lax.ppermute(down, 'dom', ring('dom', -1))]
  transfers between devices with their start and end apart: 12 -> 10, of which waited for: 9 -> 8; matrix products, arithmetic and copies ran while one was open for 2% -> 0% of each run, Pallas kernels for 0% -> 5%
where the time goes in v2:
time: 61.6 us; the launch traced here: 61.4 us
  waiting for transfers between devices  24.3 us (39%)
  starting transfers between devices  19.6 us (32%)
  Pallas kernels  12.6 us (20%)
  local copies, waits for them, and re-layouts  3.47 us (6%)
  between operations  1.37 us (2%)
    pallas_call x7, Pallas kernels, call(): pl.pallas_call(kernel, out_shape=outs, in_specs=ins, out_specs=out_specs...  12.6 us
    ppermute x1, starting transfers between devices, shards(): high = lax.ppermute(down, 'dom', ring('dom', -1))  8.68 us
    ppermute x3, waiting for transfers between devices, shards(): lax.ppermute(v, 'band', meet('band', 2 * hop))  7.24 us
    ppermute x1, waiting for transfers between devices, shards(): high = lax.ppermute(down, 'dom', ring('dom', -1))  7.08 us
    ppermute x3, starting transfers between devices, shards(): lax.ppermute(v, 'band', meet('band', 2 * hop))  4.01 us
    ppermute x1, waiting for transfers between devices, shards(): low = lax.ppermute(up, 'dom', ring('dom', 1))  3.66 us
    unnamed x12, local copies, waits for them, and re-layouts  3.47 us
    ppermute x1, waiting for transfers between devices, shards(): high_y = lax.ppermute(second, 'dom', ring('dom', -1))  2.96 us
  transfers between devices with their start and end apart: 10, of which 8 were waited for; matrix products, arithmetic and copies ran while one was open for 0% of the time, Pallas kernels for 5%

profile of v2, /device:TPU:1, one launch (start us, length us, event | category | flops | bytes accessed | tf_op | source)
XLA Modules:
  0.0 61.4 jit_solution(6049911769841343275)
XLA Ops:
  1.3 0.7 %copy-done.3 = f32[32,8]{0,1:T(8,128)S(1)} copy-done((f32[32,8]{0,1:T(8,128)S(1)}, f32[32,8]{0,1:T(8,128)}, u32[]{:S(2)}) %copy-start.3) | copy-done | bytes 1048
  2.0 1.0 %copy-done = f32[32,8,384]{2,1,0:T(8,128)S(1)} copy-done((f32[32,8,384]{2,1,0:T(8,128)S(1)}, f32[32,8,384]{2,1,0:T(8,128)}, u32[]{:S(2)}) %copy-start) | copy-done | bytes 393240
  3.0 0.9 %copy-done.1 = f32[1,12,16,128]{3,2,1,0:T(8,128)S(1)} copy-done((f32[1,12,16,128]{3,2,1,0:T(8,128)S(1)}, f32[1,12,16,128]{3,2,1,0:T(8,128)}, u32[]{:S(2)}) %copy-start.1) | copy-done | bytes 98328
  3.9 0.9 %copy-done.2 = f32[12,16,128]{2,1,0:T(8,128)S(1)} copy-done((f32[12,16,128]{2,1,0:T(8,128)S(1)}, f32[12,16,128]{2,1,0:T(8,128)}, u32[]{:S(2)}) %copy-start.2) | copy-done | bytes 98328
  4.8 0.9 %pack.1 = (f32[88,8,128]{2,1,0:T(8,128)S(1)}, f32[88,8,128]{2,1,0:T(8,128)S(1)}, f32[24,8,128]{2,1,0:T(8,128)S(1)}, f32[96,8,128]{2,1,0:T(8,128)S(1)}) custom-call(f32[24,8,128]{2,1,0:T(8,128)S(1)} %bitcast.6, f32[24,8,128]{2,1,0:T(8,128)S(1)} %bitcast.7, f32[32,8,384]{2,1,0:T(8,128)S(1)} %copy-done, f32[8,32]{1,0:T(8,128)S(1)} %bitcast.8, ...), custom_call_target="tpu_custom_call" | custom-call | flops 1000000 | bytes 2000000 | tf_op jit(solution)/shard_map/pack/pallas_call | solution.py:41
  5.6 8.7 %collective-permute-start.1 = (f32[88,8,128]{2,1,0:T(8,128)S(1)}, f32[88,8,128]{2,1,0:T(8,128)S(1)}, u32[]{:S(2)}, u32[]{:S(2)}) collective-permute-start(f32[88,8,128]{2,1,0:T(8,128)S(1)} %get-tuple-element.21), channel_id=1, source_target_pairs={{0,248},{8,0},{16,8},{24,16},{32,24},{40,32},{48,40},{56,48},{64,5... | collective-permute-start | bytes 1081352 | tf_op jit(solution)/shard_map/ppermute | solution.py:430
  14.3 7.1 %collective-permute-done.1.high_ref = f32[88,8,128]{2,1,0:T(8,128)S(1)} collective-permute-done((f32[88,8,128]{2,1,0:T(8,128)S(1)}, f32[88,8,128]{2,1,0:T(8,128)S(1)}, u32[]{:S(2)}, u32[]{:S(2)}) %collective-permute-start.1) | collective-permute-done | bytes 360480 | tf_op jit(solution)/shard_map/ppermute | solution.py:430
  21.4 1.5 %collective-permute-start.3 = (f32[88,8,128]{2,1,0:T(8,128)S(1)}, f32[88,8,128]{2,1,0:T(8,128)S(1)}, u32[]{:S(2)}, u32[]{:S(2)}) collective-permute-start(f32[88,8,128]{2,1,0:T(8,128)S(1)} %collective-permute-done.1.high_ref), channel_id=1, source_target_pairs={{0,1},{1,0},{2,3},{3,2},{4,5},{5,4},{6,7},{7,6},{8,9},{9,8},{10,11... | collective-permute-start | bytes 1081352 | tf_op jit(solution)/shard_map/ppermute | solution.py:440
  23.0 3.7 %collective-permute-done.low_ref = f32[88,8,128]{2,1,0:T(8,128)S(1)} collective-permute-done((f32[88,8,128]{2,1,0:T(8,128)S(1)}, f32[88,8,128]{2,1,0:T(8,128)S(1)}, u32[]{:S(2)}, u32[]{:S(2)}) %collective-permute-start) | collective-permute-done | bytes 360480 | tf_op jit(solution)/shard_map/ppermute | solution.py:429
  26.6 1.9 %collective-permute-start.2 = (f32[88,8,128]{2,1,0:T(8,128)S(1)}, f32[88,8,128]{2,1,0:T(8,128)S(1)}, u32[]{:S(2)}, u32[]{:S(2)}) collective-permute-start(f32[88,8,128]{2,1,0:T(8,128)S(1)} %collective-permute-done.low_ref), channel_id=1, source_target_pairs={{0,1},{1,0},{2,3},{3,2},{4,5},{5,4},{6,7},{7,6},{8,9},{9,8},{10,11... | collective-permute-start | bytes 1081352 | tf_op jit(solution)/shard_map/ppermute | solution.py:439
  28.5 0.9 %prepare.1 = (f32[2,48,8,128]{3,2,1,0:T(8,128)S(1)}, bf16[384,128]{1,0:T(8,128)(2,1)S(1)}, bf16[256,256]{1,0:T(8,128)(2,1)S(1)}) custom-call(f32[96,8,128]{2,1,0:T(8,128)S(1)} %get-tuple-element.23.proj_ref), custom_call_target="tpu_custom_call" | custom-call | flops 1000000 | bytes 2000000 | tf_op jit(solution)/shard_map/prepare/pallas_call | solution.py:41
  29.4 2.2 %head.1 = (f32[2,48,8,128]{3,2,1,0:T(8,128)S(1)}, f32[2,6,2,8,128]{4,3,2,1,0:T(8,128)S(1)}, f32[24,16,128]{2,1,0:T(8,128)S(1)}) custom-call(f32[88,8,128]{2,1,0:T(8,128)S(1)} %get-tuple-element.20.up_ref, f32[88,8,128]{2,1,0:T(8,128)S(1)} %collective-permute-done.low_ref, f32[88,8,128]{2,1,0:T(8,128)S(1)} %collective-permute-done.1.high_ref, ...), custom_call_target="tpu_custom_call" | custom-call | flops 1000000 | bytes 2000000 | tf_op jit(solution)/shard_map/head/pallas_call | solution.py:41
  31.7 3.2 %tail.1 = (f32[24,8,128]{2,1,0:T(8,128)S(1)}, f32[24,16,128]{2,1,0:T(8,128)S(1)}, f32[2,2,48,8,128]{4,3,2,1,0:T(8,128)S(1)}) custom-call(f32[88,8,128]{2,1,0:T(8,128)S(1)} %get-tuple-element.20.up_ref, f32[88,8,128]{2,1,0:T(8,128)S(1)} %collective-permute-done.low_ref, f32[88,8,128]{2,1,0:T(8,128)S(1)} %collective-permute-done.1.high_ref, ...), custom_call_target="tpu_custom_call" | custom-call | flops 1000000 | bytes 2000000 | tf_op jit(solution)/shard_map/tail/pallas_call | solution.py:41
  35.0 1.5 %collective-permute-start.4 = (f32[24,8,128]{2,1,0:T(8,128)S(1)}, f32[24,8,128]{2,1,0:T(8,128)S(1)}, u32[]{:S(2)}, u32[]{:S(2)}) collective-permute-start(f32[24,8,128]{2,1,0:T(8,128)S(1)} %get-tuple-element.32.mid_ref), channel_id=1, source_target_pairs={{0,8},{8,16},{16,24},{24,32},{32,40},{40,48},{48,56},{56,64},{64,7... | collective-permute-start | bytes 294920 | tf_op jit(solution)/shard_map/ppermute | solution.py:458
  36.4 3.0 %collective-permute-done.5.highy_ref = f32[24,8,128]{2,1,0:T(8,128)S(1)} collective-permute-done((f32[24,8,128]{2,1,0:T(8,128)S(1)}, f32[24,8,128]{2,1,0:T(8,128)S(1)}, u32[]{:S(2)}, u32[]{:S(2)}) %collective-permute-start.5) | collective-permute-done | bytes 98336 | tf_op jit(solution)/shard_map/ppermute | solution.py:459
  39.4 2.4 %collective-permute-done.4.lowy_ref = f32[24,8,128]{2,1,0:T(8,128)S(1)} collective-permute-done((f32[24,8,128]{2,1,0:T(8,128)S(1)}, f32[24,8,128]{2,1,0:T(8,128)S(1)}, u32[]{:S(2)}, u32[]{:S(2)}) %collective-permute-start.4) | collective-permute-done | bytes 98336 | tf_op jit(solution)/shard_map/ppermute | solution.py:458
  41.9 3.4 %last.1.own_ref = f32[24,8,128]{2,1,0:T(8,128)S(1)} custom-call(f32[88,8,128]{2,1,0:T(8,128)S(1)} %get-tuple-element.20.up_ref, f32[88,8,128]{2,1,0:T(8,128)S(1)} %collective-permute-done.low_ref, f32[88,8,128]{2,1,0:T(8,128)S(1)} %collective-permute-done.1.high_ref, f32[24,8,128]{2,1,0:T(8,128)S(1)} %get-tuple-element.22.pot_ref, ...), custom_call_target="tpu_custom_call" | custom-call | flops 1000000 | bytes 2000000 | tf_op jit(solution)/shard_map/last/pallas_call | solution.py:41
  45.3 1.9 %collective-permute-start.6 = (f32[24,8,128]{2,1,0:T(8,128)S(1)}, f32[24,8,128]{2,1,0:T(8,128)S(1)}, u32[]{:S(2)}, u32[]{:S(2)}) collective-permute-start(f32[24,8,128]{2,1,0:T(8,128)S(1)} %last.1.own_ref), channel_id=1, source_target_pairs={{0,1},{1,0},{2,3},{3,2},{4,5},{5,4},{6,7},{7,6},{8,9},{9,8},{10,11... | collective-permute-start | bytes 294920 | tf_op jit(solution)/shard_map/ppermute | solution.py:468
  47.2 0.9 %collective-permute-done.6.other_ref = f32[24,8,128]{2,1,0:T(8,128)S(1)} collective-permute-done((f32[24,8,128]{2,1,0:T(8,128)S(1)}, f32[24,8,128]{2,1,0:T(8,128)S(1)}, u32[]{:S(2)}, u32[]{:S(2)}) %collective-permute-start.6) | collective-permute-done | bytes 98336 | tf_op jit(solution)/shard_map/ppermute | solution.py:468
  48.2 1.2 %parts.1 = (f32[24,8,128]{2,1,0:T(8,128)S(1)}, f32[24,8,128]{2,1,0:T(8,128)S(1)}, f32[24,8,128]{2,1,0:T(8,128)S(1)}, f32[24,8,128]{2,1,0:T(8,128)S(1)}, f32[24,8,128]{2,1,0:T(8,128)}) custom-call(f32[8,8]{1,0:T(8,128)S(1)} %copy-done.4, f32[24,8,128]{2,1,0:T(8,128)S(1)} %last.1.own_ref, f32[24,8,128]{2,1,0:T(8,128)S(1)} %collective-permute-done.6.other_ref), custom_call_target="tpu_custom_call" | custom-call | flops 1000000 | bytes 2000000 | tf_op jit(solution)/shard_map/parts/pallas_call | solution.py:41
  49.4 1.4 %collective-permute-start.7 = (f32[24,8,128]{2,1,0:T(8,128)S(1)}, f32[24,8,128]{2,1,0:T(8,128)S(1)}, u32[]{:S(2)}, u32[]{:S(2)}) collective-permute-start(f32[24,8,128]{2,1,0:T(8,128)S(1)} %get-tuple-element.35), channel_id=1, source_target_pairs={{0,2},{1,3},{2,0},{3,1},{4,6},{5,7},{6,4},{7,5},{8,10},{9,11},{10,... | collective-permute-start | bytes 294920 | tf_op jit(solution)/shard_map/ppermute | solution.py:479
  50.8 2.6 %collective-permute-start.8 = (f32[24,8,128]{2,1,0:T(8,128)S(1)}, f32[24,8,128]{2,1,0:T(8,128)S(1)}, u32[]{:S(2)}, u32[]{:S(2)}) collective-permute-start(f32[24,8,128]{2,1,0:T(8,128)S(1)} %get-tuple-element.36), channel_id=1, source_target_pairs={{0,4},{1,5},{2,6},{3,7},{4,0},{5,1},{6,2},{7,3},{8,12},{9,13},{10,... | collective-permute-start | bytes 294920 | tf_op jit(solution)/shard_map/ppermute | solution.py:479
  53.6 4.6 %collective-permute-done.8.two_ref = f32[24,8,128]{2,1,0:T(8,128)S(1)} collective-permute-done((f32[24,8,128]{2,1,0:T(8,128)S(1)}, f32[24,8,128]{2,1,0:T(8,128)S(1)}, u32[]{:S(2)}, u32[]{:S(2)}) %collective-permute-start.8) | collective-permute-done | bytes 98336 | tf_op jit(solution)/shard_map/ppermute | solution.py:479
  58.1 2.6 %collective-permute-done.9.three_ref = f32[24,8,128]{2,1,0:T(8,128)S(1)} collective-permute-done((f32[24,8,128]{2,1,0:T(8,128)S(1)}, f32[24,8,128]{2,1,0:T(8,128)S(1)}, u32[]{:S(2)}, u32[]{:S(2)}) %collective-permute-start.9) | collective-permute-done | bytes 98336 | tf_op jit(solution)/shard_map/ppermute | solution.py:479
  (15 shorter events, 0.9 us)
Async XLA Ops:
  1.3 0.7 %copy-start.3 = (f32[32,8]{0,1:T(8,128)S(1)}, f32[32,8]{0,1:T(8,128)}, u32[]{:S(2)}) copy-start(f32[32,8]{0,1:T(8,128)} %param.12) | copy-start | bytes 3076
  1.3 0.7 %copy-start.5 = (s32[32,3]{0,1:T(4,128)S(1)}, s32[32,3]{0,1:T(4,128)}, u32[]{:S(2)}) copy-start(s32[32,3]{0,1:T(4,128)} %param.9) | copy-start | bytes 1156
  2.0 1.0 %copy-start = (f32[32,8,384]{2,1,0:T(8,128)S(1)}, f32[32,8,384]{2,1,0:T(8,128)}, u32[]{:S(2)}) copy-start(f32[32,8,384]{2,1,0:T(8,128)} %proj_hbm.1) | copy-start | bytes 1179652
  3.0 0.9 %copy-start.1 = (f32[1,12,16,128]{3,2,1,0:T(8,128)S(1)}, f32[1,12,16,128]{3,2,1,0:T(8,128)}, u32[]{:S(2)}) copy-start(f32[1,12,16,128]{3,2,1,0:T(8,128)} %param.7) | copy-start | bytes 294916
  3.9 0.9 %copy-start.2 = (f32[12,16,128]{2,1,0:T(8,128)S(1)}, f32[12,16,128]{2,1,0:T(8,128)}, u32[]{:S(2)}) copy-start(f32[12,16,128]{2,1,0:T(8,128)} %param.8) | copy-start | bytes 294916
  5.6 15.8 %collective-permute-start.1 = (f32[88,8,128]{2,1,0:T(8,128)S(1)}, f32[88,8,128]{2,1,0:T(8,128)S(1)}, u32[]{:S(2)}, u32[]{:S(2)}) collective-permute-start(f32[88,8,128]{2,1,0:T(8,128)S(1)} %get-tuple-element.21), channel_id=1, source_target_pairs={{0,248},{8,0},{16,8},{24,16},{32,24},{40,32},{48,40},{56,48},{64,5... | collective-permute-start | bytes 1081352 | tf_op jit(solution)/shard_map/ppermute | solution.py:430
  14.3 12.3 %collective-permute-start = (f32[88,8,128]{2,1,0:T(8,128)S(1)}, f32[88,8,128]{2,1,0:T(8,128)S(1)}, u32[]{:S(2)}, u32[]{:S(2)}) collective-permute-start(f32[88,8,128]{2,1,0:T(8,128)S(1)} %get-tuple-element.20.up_ref), channel_id=1, source_target_pairs={{0,8},{8,16},{16,24},{24,32},{32,40},{40,48},{48,56},{56,64},{64,7... | collective-permute-start | bytes 1081352 | tf_op jit(solution)/shard_map/ppermute | solution.py:429
  21.4 10.3 %collective-permute-start.3 = (f32[88,8,128]{2,1,0:T(8,128)S(1)}, f32[88,8,128]{2,1,0:T(8,128)S(1)}, u32[]{:S(2)}, u32[]{:S(2)}) collective-permute-start(f32[88,8,128]{2,1,0:T(8,128)S(1)} %collective-permute-done.1.high_ref), channel_id=1, source_target_pairs={{0,1},{1,0},{2,3},{3,2},{4,5},{5,4},{6,7},{7,6},{8,9},{9,8},{10,11... | collective-permute-start | bytes 1081352 | tf_op jit(solution)/shard_map/ppermute | solution.py:440
  26.6 5.1 %collective-permute-start.2 = (f32[88,8,128]{2,1,0:T(8,128)S(1)}, f32[88,8,128]{2,1,0:T(8,128)S(1)}, u32[]{:S(2)}, u32[]{:S(2)}) collective-permute-start(f32[88,8,128]{2,1,0:T(8,128)S(1)} %collective-permute-done.low_ref), channel_id=1, source_target_pairs={{0,1},{1,0},{2,3},{3,2},{4,5},{5,4},{6,7},{7,6},{8,9},{9,8},{10,11... | collective-permute-start | bytes 1081352 | tf_op jit(solution)/shard_map/ppermute | solution.py:439
  34.9 4.5 %collective-permute-start.5 = (f32[24,8,128]{2,1,0:T(8,128)S(1)}, f32[24,8,128]{2,1,0:T(8,128)S(1)}, u32[]{:S(2)}, u32[]{:S(2)}) collective-permute-start(f32[24,8,128]{2,1,0:T(8,128)S(1)} %get-tuple-element.32.mid_ref), channel_id=1, source_target_pairs={{0,248},{8,0},{16,8},{24,16},{32,24},{40,32},{48,40},{56,48},{64,5... | collective-permute-start | bytes 294920 | tf_op jit(solution)/shard_map/ppermute | solution.py:459
  35.0 6.9 %collective-permute-start.4 = (f32[24,8,128]{2,1,0:T(8,128)S(1)}, f32[24,8,128]{2,1,0:T(8,128)S(1)}, u32[]{:S(2)}, u32[]{:S(2)}) collective-permute-start(f32[24,8,128]{2,1,0:T(8,128)S(1)} %get-tuple-element.32.mid_ref), channel_id=1, source_target_pairs={{0,8},{8,16},{16,24},{24,32},{32,40},{40,48},{48,56},{56,64},{64,7... | collective-permute-start | bytes 294920 | tf_op jit(solution)/shard_map/ppermute | solution.py:458
  41.9 6.3 %copy-start.4 = (f32[8,8]{1,0:T(8,128)S(1)}, f32[8,8]{1,0:T(8,128)}, u32[]{:S(2)}) copy-start(f32[8,8]{1,0:T(8,128)} %ritz_ref.1) | copy-start | bytes 772
  45.3 2.9 %collective-permute-start.6 = (f32[24,8,128]{2,1,0:T(8,128)S(1)}, f32[24,8,128]{2,1,0:T(8,128)S(1)}, u32[]{:S(2)}, u32[]{:S(2)}) collective-permute-start(f32[24,8,128]{2,1,0:T(8,128)S(1)} %last.1.own_ref), channel_id=1, source_target_pairs={{0,1},{1,0},{2,3},{3,2},{4,5},{5,4},{6,7},{7,6},{8,9},{9,8},{10,11... | collective-permute-start | bytes 294920 | tf_op jit(solution)/shard_map/ppermute | solution.py:468
  49.4 4.1 %collective-permute-start.7 = (f32[24,8,128]{2,1,0:T(8,128)S(1)}, f32[24,8,128]{2,1,0:T(8,128)S(1)}, u32[]{:S(2)}, u32[]{:S(2)}) collective-permute-start(f32[24,8,128]{2,1,0:T(8,128)S(1)} %get-tuple-element.35), channel_id=1, source_target_pairs={{0,2},{1,3},{2,0},{3,1},{4,6},{5,7},{6,4},{7,5},{8,10},{9,11},{10,... | collective-permute-start | bytes 294920 | tf_op jit(solution)/shard_map/ppermute | solution.py:479
  50.8 7.3 %collective-permute-start.8 = (f32[24,8,128]{2,1,0:T(8,128)S(1)}, f32[24,8,128]{2,1,0:T(8,128)S(1)}, u32[]{:S(2)}, u32[]{:S(2)}) collective-permute-start(f32[24,8,128]{2,1,0:T(8,128)S(1)} %get-tuple-element.36), channel_id=1, source_target_pairs={{0,4},{1,5},{2,6},{3,7},{4,0},{5,1},{6,2},{7,3},{8,12},{9,13},{10,... | collective-permute-start | bytes 294920 | tf_op jit(solution)/shard_map/ppermute | solution.py:479
  53.4 7.2 %collective-permute-start.9 = (f32[24,8,128]{2,1,0:T(8,128)S(1)}, f32[24,8,128]{2,1,0:T(8,128)S(1)}, u32[]{:S(2)}, u32[]{:S(2)}) collective-permute-start(f32[24,8,128]{2,1,0:T(8,128)S(1)} %get-tuple-element.37), channel_id=1, source_target_pairs={{0,6},{1,7},{2,4},{3,5},{4,2},{5,3},{6,0},{7,1},{8,14},{9,15},{10,... | collective-permute-start | bytes 294920 | tf_op jit(solution)/shard_map/ppermute | solution.py:479

commit v3 on v2

--- a/solution.py
+++ b/solution.py
@@ -131,7 +131,15 @@
             table[l * BX + i] = work.at[i][pl.ds(l, 8, stride=8), :]
 
 
-def prepare_kernel(proj_ref, table_ref, zst_ref, sums_ref, work):
+def prepare_kernel(proj_ref, ritz_ref, table_ref, zst_ref, sums_ref, factors_ref, work):
+    band = lax.axis_index("band")
+    row = lax.broadcasted_iota(jnp.int32, (8, 8), 0)
+    column = lax.broadcasted_iota(jnp.int32, (8, 8), 1)
+    for hop in range(4):
+        for n, orbital in enumerate((band, band ^ 1)):
+            picked = jnp.where((row == orbital) & (column == band ^ (2 * hop)), ritz_ref[...], 0.0)
+            picked = jnp.sum(jnp.sum(picked, 1, keepdims=True), 0, keepdims=True)
+            factors_ref[2 * hop + n] = jnp.broadcast_to(picked, (8, 128))
     for tile in range(2):
         read = lambda part, a: proj_ref[ATOMS * part + 16 * tile + a]
         spread_projectors(read, work, table_ref.at[tile])
@@ -190,8 +198,8 @@
     columns = dot(field2[rows, :], jnp.concatenate([onehot, onehot], 0)).reshape(planes_in, NY, LANES)
     for tile in range(2):
         part = columns[:, :, half(tile)]
-        gathered[group, tile, skip : skip + planes_in, 0:16, :] = part
-        gathered[group, tile, skip : skip + planes_in, 16:24, :] = part[:, 0:8]
+        gathered[group][tile, skip : skip + planes_in, 0:16, :] = part
+        gathered[group][tile, skip : skip + planes_in, 16:24, :] = part[:, 0:8]
 
 
 def read_windows(group, gathered, boxes):
@@ -202,7 +210,7 @@
         for tile in range(2):
             x0, y0 = boxes.place(group, 16 * tile + a)
             for i in range(BX):
-                values[i][tile] = jnp.where(mine, gathered[group, tile, x0 + i, pl.ds(y0, 8), :], values[i][tile])
+                values[i][tile] = jnp.where(mine, gathered[group][tile, x0 + i, pl.ds(y0, 8), :], values[i][tile])
     return values
 
 
@@ -232,15 +240,15 @@
         for tile in range(2):
             x0, y0 = boxes.place(group, 16 * tile + a)
             for i in range(BX):
-                pltpu.store(placed.at[group, tile, x0 + i, pl.ds(y0, 8), :], contrib[i][tile], mask=mine)
+                pltpu.store(placed[group].at[tile, x0 + i, pl.ds(y0, 8), :], contrib[i][tile], mask=mine)
 
 
 def spread_group(group, first, count, placed, onehot):
     planes = slice(first, first + count)
     tiles = []
     for tile in range(2):
-        folded = placed[group, tile, planes, 0:8, :] + placed[group, tile, planes, 16:24, :]
-        tiles.append(jnp.concatenate([folded, placed[group, tile, planes, 8:16, :]], 1).reshape(count * NY, 128))
+        folded = placed[group][tile, planes, 0:8, :] + placed[group][tile, planes, 16:24, :]
+        tiles.append(jnp.concatenate([folded, placed[group][tile, planes, 8:16, :]], 1).reshape(count * NY, 128))
     twice = jnp.concatenate([onehot, onehot], 1)
     spread = lax.dot_general(
         two_terms(jnp.concatenate(tiles, 1), 1), twice, (((1,), (1,)), ((), ())),
@@ -269,6 +277,11 @@
     return source[tile : tile + 2].reshape(NY, NZ)
 
 
+def clear(boxed):
+    for ref in boxed:
+        ref[...] = jnp.zeros_like(ref)
+
+
 def load_fields(fields, padded, field2):
     for n, value in enumerate(fields):
         fill(padded, 12 * n, value.reshape(CX, NY, NZ))
@@ -277,15 +290,22 @@
 
 def head_kernel(up_ref, low_ref, high_ref, pot_ref, table_ref, zst_ref, sums_ref,
                 half_ref, values_ref, partial_ref,
-                low_xy, own_xy, high_xy, padded, field2, gathered, placed, local, nonlocal_, work, sems):
+                low_xy, own_xy, high_xy, padded, field2, gathered, placed, local, work, sems):
     boxes = Boxes((low_ref, up_ref, high_ref), (low_xy, own_xy, high_xy), sems)
     load_fields([r[TILE_Y : TILE_Y + 24] for r in (low_ref, up_ref, high_ref)], padded, field2)
-    placed[...] = jnp.zeros_like(placed)
-    gathered[2, :, 12:SPAN] = jnp.zeros((2, SPAN - 12, 24, 128), jnp.float32)
+    clear(placed)
+    gathered[2][:, 12:SPAN] = jnp.zeros((2, SPAN - 12, 24, 128), jnp.float32)
     own_hot = boxes.one_hot(1)
     gather_columns(1, field2, 12, SPAN, 0, gathered, own_hot)
     gather_columns(0, field2, 0, SPAN, 0, gathered, boxes.one_hot(0))
     gather_columns(2, field2, 24, 12, 0, gathered, boxes.one_hot(2))
+    local[...] = along_z(field2, slice(96, 480), zst_ref).reshape(24, NY, NZ)
+    for p in range(24):
+        laplace = stencil_plane(padded, p + 6) + local[p]
+        pot = potential_plane(p, low_ref, pot_ref, high_ref)
+        local[p] = (-0.5 * laplace + (pot - CENTER) * padded[p + 6, 8:24, :]) * (1.0 / HALF)
+    for n, source in enumerate((low_ref, high_ref)):
+        spread_projectors(lambda part, a: source[TILE_P + 16 * part + a], work, half_ref.at[n])
     boxes.wait()
     contributions(1, read_windows(1, gathered, boxes), table_ref, placed, boxes, sums_ref[...])
     for n, group in enumerate((0, 2)):
@@ -293,16 +313,9 @@
         for i in range(BX):
             for tile in range(2):
                 values_ref[n, i, tile] = values[i][tile]
-    local[...] = along_z(field2, slice(96, 480), zst_ref).reshape(24, NY, NZ)
-    nonlocal_[0:6] = jnp.zeros((6, NY, NZ), jnp.float32)
-    nonlocal_[6:23] = spread_group(1, 0, 17, placed, own_hot)
-    nonlocal_[23] = jnp.zeros((NY, NZ), jnp.float32)
-    for n, source in enumerate((low_ref, high_ref)):
-        spread_projectors(lambda part, a: source[TILE_P + 16 * part + a], work, half_ref.at[n])
-    for p in range(24):
-        laplace = stencil_plane(padded, p + 6) + local[p]
-        pot = potential_plane(p, low_ref, pot_ref, high_ref)
-        partial_ref[p] = (-0.5 * laplace + (pot - CENTER) * padded[p + 6, 8:24, :] + nonlocal_[p]) * (1.0 / HALF)
+    partial_ref[0:6] = local[0:6]
+    partial_ref[6:23] = local[6:23] + spread_group(1, 0, 17, placed, own_hot) * (1.0 / HALF)
+    partial_ref[23] = local[23]
 
 
 def second_step(boxes, hots, padded1, field2, gathered, placed, local, nonlocal_, pot_ref, tables, zst_ref, sums):
@@ -311,13 +324,15 @@
     for group in range(2):
         contributions(group, read_windows(group, gathered, boxes), tables[group], placed, boxes, sums)
     local[0:12] = along_z(field2, slice(96, 288), zst_ref).reshape(12, NY, NZ)
-    nonlocal_[0:12] = spread_group(1, 0, 12, placed, hots[1])
-    nonlocal_[0:5] += spread_group(0, 12, 5, placed, hots[0])
     for p in range(12):
         here = padded1[p + 6, 8:24, :]
         laplace = stencil_plane(padded1, p + 6) + local[p]
         pot = potential_plane(p + 6, None, pot_ref, None)
-        yield p, (-0.5 * laplace + (pot - CENTER) * here + nonlocal_[p]) * (2.0 / HALF)
+        local[p] = -0.5 * laplace + (pot - CENTER) * here
+    nonlocal_[0:12] = spread_group(1, 0, 12, placed, hots[1])
+    nonlocal_[0:5] += spread_group(0, 12, 5, placed, hots[0])
+    for p in range(12):
+        yield p, (local[p] + nonlocal_[p]) * (2.0 / HALF)
 
 
 def tail_kernel(up_ref, low_ref, high_ref, pot_ref, table_ref, zst_ref, sums_ref,
@@ -326,8 +341,8 @@
                 low_xy, own_xy, high_xy, padded1, field2, gathered, placed, local, nonlocal_, work, sems):
     core = lax.axis_index("band") % 2
     boxes = Boxes((low_ref, up_ref, high_ref), (low_xy, own_xy, high_xy), sems)
-    placed[...] = jnp.zeros_like(placed)
-    gathered[0, :, 0:6] = jnp.zeros((2, 6, 24, 128), jnp.float32)
+    clear(placed)
+    gathered[0][:, 0:6] = jnp.zeros((2, 6, 24, 128), jnp.float32)
     for n, source in enumerate((lowsib_ref, highsib_ref)):
         spread_projectors(lambda part, a: source[TILE_P + 16 * part + a], work, tables_ref.at[n, 1 - core])
         tables_ref[n, core] = half_ref[n]
@@ -357,26 +372,29 @@
                 low_xy, own_xy, high_xy, padded, padded1, field2, gathered, placed, local, nonlocal_, sems):
     boxes = Boxes((low_ref, up_ref, high_ref), (low_xy, own_xy, high_xy), sems)
     load_fields([r[...] for r in (lowy_ref, mid_ref, highy_ref)], padded, field2)
-    placed[...] = jnp.zeros_like(placed)
-    gathered[2, :, 12:SPAN] = jnp.zeros((2, SPAN - 12, 24, 128), jnp.float32)
+    clear(placed)
+    gathered[2][:, 12:SPAN] = jnp.zeros((2, SPAN - 12, 24, 128), jnp.float32)
     hots = [boxes.one_hot(g) for g in range(3)]
-    boxes.wait()
     sums = sums_ref[...]
     tables = (tables_ref.at[0], table_ref, tables_ref.at[1])
     for group, planes in ((0, SPAN), (1, SPAN), (2, 12)):
         gather_columns(group, field2, 12 * group, planes, 0, gathered, hots[group])
+    local[...] = along_z(field2, slice(96, 480), zst_ref).reshape(24, NY, NZ)
+    for p in range(24):
+        laplace = stencil_plane(padded, p + 6) + local[p]
+        pot = potential_plane(p, low_ref, pot_ref, high_ref)
+        applied = -0.5 * laplace + (pot - CENTER) * padded[p + 6, 8:24, :]
+        local[p] = applied * (2.0 / HALF) - kept_ref[p]
+    boxes.wait()
+    windows = [read_windows(group, gathered, boxes) for group in range(3)]
     for group in range(3):
-        contributions(group, read_windows(group, gathered, boxes), tables[group], placed, boxes, sums)
-    local[...] = along_z(field2, slice(96, 480), zst_ref).reshape(24, NY, NZ)
+        contributions(group, windows[group], tables[group], placed, boxes, sums)
     nonlocal_[0:11] = spread_group(0, 6, 11, placed, hots[0])
     nonlocal_[11:24] = jnp.zeros((13, NY, NZ), jnp.float32)
     nonlocal_[6:23] += spread_group(1, 0, 17, placed, hots[1])
     nonlocal_[18:24] += spread_group(2, 0, 6, placed, hots[2])
     for p in range(24):
-        laplace = stencil_plane(padded, p + 6) + local[p]
-        pot = potential_plane(p, low_ref, pot_ref, high_ref)
-        applied = -0.5 * laplace + (pot - CENTER) * padded[p + 6, 8:24, :] + nonlocal_[p]
-        updated = applied * (2.0 / HALF) - kept_ref[p]
+        updated = local[p] + nonlocal_[p] * (2.0 / HALF)
         fill(padded1, p, updated[None])
         field2[16 * p : 16 * p + 16, :] = two_terms(updated, 1)
     for p, value in second_step(boxes, hots, padded1, field2, gathered, placed, local, nonlocal_, pot_ref, tables,
@@ -388,20 +406,20 @@
 PADDED = pltpu.VMEM((36, 32, NZ), jnp.float32)
 PADDED1 = pltpu.VMEM((24, 32, NZ), jnp.float32)
 FIELD2 = pltpu.VMEM((576, 2 * NZ), jnp.bfloat16)
-BOXED = pltpu.VMEM((3, 2, SPAN, 24, 128), jnp.float32)
+BOXED = [pltpu.VMEM((2, SPAN, 24, 128), jnp.float32)] * 3
 PLANES = pltpu.VMEM((24, NY, NZ), jnp.float32)
 WORK = pltpu.VMEM((BX, BY * NPROJ, 128), jnp.float32)
 COPIES = pltpu.SemaphoreType.DMA((3,))
 
 
-def parts_kernel(ritz_ref, own_ref, other_ref, base_ref, one_ref, two_ref, three_ref, out_hbm, sem):
-    copy = pltpu.make_async_copy(own_ref, out_hbm, sem.at[0])
-    copy.start()
-    band = lax.axis_index("band")
+def parts_kernel(factors_ref, own_ref, other_ref, base_ref, one_ref, two_ref, three_ref):
+    own, other = own_ref[...], other_ref[...]
     for hop, target in enumerate((base_ref, one_ref, two_ref, three_ref)):
-        to = band ^ (2 * hop)
-        target[...] = ritz_ref[band, to] * own_ref[...] + ritz_ref[band ^ 1, to] * other_ref[...]
-    copy.wait()
+        target[...] = factors_ref[2 * hop] * own + factors_ref[2 * hop + 1] * other
+
+
+def store_kernel(own_ref, out_ref):
+    out_ref[...] = own_ref[...]
 
 
 def total_kernel(base_ref, one_ref, two_ref, three_ref, out_ref):
@@ -418,21 +436,34 @@
 
 
 def shards(orbitals, potential, atom_pos, atom_count, projectors, gammas, ritz):
+    stay = lambda v: pltpu.with_memory_space_constraint(v, pltpu.HBM)
     up, down, pot, proj = call(
         pack_kernel,
         [shape(TILES, 8, 128), shape(TILES, 8, 128), shape(24, 8, 128), shape(3 * ATOMS, 8, 128)],
         [HBM] * 5 + [SMEM],
-        (orbitals.reshape(24, 8, 128), potential.reshape(24, 8, 128), projectors, gammas.T, atom_pos.T, atom_count),
+        (
+            stay(orbitals.reshape(24, 8, 128)),
+            stay(potential.reshape(24, 8, 128)),
+            stay(projectors),
+            stay(gammas.T),
+            stay(atom_pos.T),
+            atom_count,
+        ),
         "pack",
         [pltpu.VMEM((NPROJ, ATOMS), jnp.float32), pltpu.VMEM((3, ATOMS), jnp.int32), pltpu.SemaphoreType.DMA((16,))],
     )
     low = lax.ppermute(up, "dom", ring("dom", 1))
     high = lax.ppermute(down, "dom", ring("dom", -1))
-    table, zst, sums = call(
+    table, zst, sums, factors = call(
         prepare_kernel,
-        [shape(2, PAIRS, 8, 128), shape(384, NZ, dtype=jnp.bfloat16), shape(LANES, LANES, dtype=jnp.bfloat16)],
-        [VMEM],
-        (proj,),
+        [
+            shape(2, PAIRS, 8, 128),
+            shape(384, NZ, dtype=jnp.bfloat16),
+            shape(LANES, LANES, dtype=jnp.bfloat16),
+            shape(8, 8, 128),
+        ],
+        [VMEM] * 2,
+        (proj, ritz),
         "prepare",
         [WORK],
     )
@@ -445,7 +476,8 @@
         [VMEM] * 7,
         common,
         "head",
-        XY + [PADDED, FIELD2, BOXED, BOXED, PLANES, PLANES, WORK, COPIES],
+        XY + [PADDED, FIELD2, BOXED, BOXED, PLANES, WORK, COPIES],
+        flops=10_000_000_000,
     )
     second, first, tables = call(
         tail_kernel,
@@ -467,16 +499,11 @@
     )
     other = lax.ppermute(fourth, "band", meet("band", 1))
     field = shape(24, 8, 128)
-    base, one, two, three, filtered = call(
-        parts_kernel,
-        [field] * 5,
-        [SMEM, VMEM, VMEM],
-        (ritz, fourth, other),
-        "parts",
-        [pltpu.SemaphoreType.DMA((1,))],
-        [VMEM] * 4 + [HBM],
-    )
-    arrived = [lax.ppermute(v, "band", meet("band", 2 * hop)) for hop, v in ((1, one), (2, two), (3, three))]
+    base, one, two, three = call(
+        parts_kernel, [field] * 4, [VMEM] * 3, (factors, fourth, other), "parts"
+    )
+    arrived = [lax.ppermute(v, "band", meet("band", 2 * hop)) for hop, v in ((2, two), (1, one), (3, three))]
+    (filtered,) = call(store_kernel, [field], [VMEM], (fourth,), "store")
     (rotated,) = call(total_kernel, [field], [VMEM] * 4, (base, *arrived), "total")
     return (filtered.reshape(orbitals.shape), rotated.reshape(orbitals.shape))
 

time: 61.6 us -> 52.8 us (0.86)
  waiting for transfers between devices: 24.3 us -> 19.7 us
  local copies, waits for them, and re-layouts: 3.47 us -> 0.01 us
    ppermute x3, waiting for transfers between devices: 7.24 us -> 3.65 us  [shards(): lax.ppermute(v, 'band', meet('band', 2 * hop))]
    unnamed x12 -> x2, local copies, waits for them, and re-layouts: 3.47 us -> 0.01 us
    ppermute x1, waiting for transfers between devices: 7.08 us -> 6.01 us  [shards(): high = lax.ppermute(down, 'dom', ring('dom', -1))]
    pallas_call x7 -> x8, Pallas kernels: 12.6 us -> 12.3 us  [call(): pl.pallas_call(kernel, out_shape=outs, in_specs=ins, out_specs=out_specs...]
  transfers between devices with their start and end apart: 10 -> 10, of which waited for: 8 -> 7; matrix products, arithmetic and copies ran while one was open for 0% -> 0% of each run, Pallas kernels for 5% -> 8%
where the time goes in v3:
time: 52.8 us; the launch traced here: 52.7 us
  waiting for transfers between devices  19.7 us (37%)
  starting transfers between devices  19.3 us (37%)
  Pallas kernels  12.3 us (23%)
  between operations  1.36 us (3%)
    pallas_call x8, Pallas kernels, call(): pl.pallas_call(kernel, out_shape=outs, in_specs=ins, out_specs=out_specs...  12.3 us
    ppermute x1, starting transfers between devices, shards(): high = lax.ppermute(down, 'dom', ring('dom', -1))  8.68 us
    ppermute x1, waiting for transfers between devices, shards(): high = lax.ppermute(down, 'dom', ring('dom', -1))  6.01 us
    ppermute x3, starting transfers between devices, shards(): lax.ppermute(v, 'band', meet('band', 2 * hop))  3.78 us
    ppermute x1, waiting for transfers between devices, shards(): low = lax.ppermute(up, 'dom', ring('dom', 1))  3.66 us
    ppermute x3, waiting for transfers between devices, shards(): lax.ppermute(v, 'band', meet('band', 2 * hop))  3.65 us
    ppermute x1, waiting for transfers between devices, shards(): high_y = lax.ppermute(second, 'dom', ring('dom', -1))  2.96 us
    ppermute x1, waiting for transfers between devices, shards(): low_y = lax.ppermute(second, 'dom', ring('dom', 1))  2.45 us
  transfers between devices with their start and end apart: 10, of which 7 were waited for; matrix products, arithmetic and copies ran while one was open for 0% of the time, Pallas kernels for 8%

profile of v3, /device:TPU:1, one launch (start us, length us, event | category | flops | bytes accessed | tf_op | source)
XLA Modules:
  0.0 52.7 jit_solution(9308649220508805929)
XLA Ops:
  1.3 1.5 %pack.1 = (f32[88,8,128]{2,1,0:T(8,128)S(1)}, f32[88,8,128]{2,1,0:T(8,128)S(1)}, f32[24,8,128]{2,1,0:T(8,128)S(1)}, f32[96,8,128]{2,1,0:T(8,128)S(1)}) custom-call(f32[24,8,128]{2,1,0:T(8,128)} %bitcast.7, f32[24,8,128]{2,1,0:T(8,128)} %bitcast.8, f32[32,8,384]{2,1,0:T(8,128)} %proj_hbm.1, f32[8,32]{1,0:T(8,128)} %bitcast.10, s32[3,32]{1,0:T(4,128)} %bitcast.11, ...), custom_call_target="tpu_custom_call" | custom-call | flops 1000000 | bytes 2000000 | tf_op jit(solution)/shard_map/pack/pallas_call | solution.py:41
  2.8 8.7 %collective-permute-start.1 = (f32[88,8,128]{2,1,0:T(8,128)S(1)}, f32[88,8,128]{2,1,0:T(8,128)S(1)}, u32[]{:S(2)}, u32[]{:S(2)}) collective-permute-start(f32[88,8,128]{2,1,0:T(8,128)S(1)} %get-tuple-element.21), channel_id=1, source_target_pairs={{0,248},{8,0},{16,8},{24,16},{32,24},{40,32},{48,40},{56,48},{64,5... | collective-permute-start | bytes 1081352 | tf_op jit(solution)/shard_map/ppermute | solution.py:456
  11.5 1.1 %prepare.1 = (f32[2,48,8,128]{3,2,1,0:T(8,128)S(1)}, bf16[384,128]{1,0:T(8,128)(2,1)S(1)}, bf16[256,256]{1,0:T(8,128)(2,1)S(1)}, f32[8,8,128]{2,1,0:T(8,128)S(1)}) custom-call(f32[96,8,128]{2,1,0:T(8,128)S(1)} %get-tuple-element.23.proj_ref, f32[8,8]{1,0:T(8,128)S(1)} %copy-done), custom_call_target="tpu_custom_call" | custom-call | flops 1000000 | bytes 2000000 | tf_op jit(solution)/shard_map/prepare/pallas_call | solution.py:41
  12.6 6.0 %collective-permute-done.1.high_ref = f32[88,8,128]{2,1,0:T(8,128)S(1)} collective-permute-done((f32[88,8,128]{2,1,0:T(8,128)S(1)}, f32[88,8,128]{2,1,0:T(8,128)S(1)}, u32[]{:S(2)}, u32[]{:S(2)}) %collective-permute-start.1) | collective-permute-done | bytes 360480 | tf_op jit(solution)/shard_map/ppermute | solution.py:456
  18.6 1.5 %collective-permute-start.3 = (f32[88,8,128]{2,1,0:T(8,128)S(1)}, f32[88,8,128]{2,1,0:T(8,128)S(1)}, u32[]{:S(2)}, u32[]{:S(2)}) collective-permute-start(f32[88,8,128]{2,1,0:T(8,128)S(1)} %collective-permute-done.1.high_ref), channel_id=1, source_target_pairs={{0,1},{1,0},{2,3},{3,2},{4,5},{5,4},{6,7},{7,6},{8,9},{9,8},{10,11... | collective-permute-start | bytes 1081352 | tf_op jit(solution)/shard_map/ppermute | solution.py:471
  20.1 3.7 %collective-permute-done.low_ref = f32[88,8,128]{2,1,0:T(8,128)S(1)} collective-permute-done((f32[88,8,128]{2,1,0:T(8,128)S(1)}, f32[88,8,128]{2,1,0:T(8,128)S(1)}, u32[]{:S(2)}, u32[]{:S(2)}) %collective-permute-start) | collective-permute-done | bytes 360480 | tf_op jit(solution)/shard_map/ppermute | solution.py:455
  23.8 1.9 %collective-permute-start.2 = (f32[88,8,128]{2,1,0:T(8,128)S(1)}, f32[88,8,128]{2,1,0:T(8,128)S(1)}, u32[]{:S(2)}, u32[]{:S(2)}) collective-permute-start(f32[88,8,128]{2,1,0:T(8,128)S(1)} %collective-permute-done.low_ref), channel_id=1, source_target_pairs={{0,1},{1,0},{2,3},{3,2},{4,5},{5,4},{6,7},{7,6},{8,9},{9,8},{10,11... | collective-permute-start | bytes 1081352 | tf_op jit(solution)/shard_map/ppermute | solution.py:470
  25.6 2.5 %head.1 = (f32[2,48,8,128]{3,2,1,0:T(8,128)S(1)}, f32[2,6,2,8,128]{4,3,2,1,0:T(8,128)S(1)}, f32[24,16,128]{2,1,0:T(8,128)S(1)}) custom-call(f32[88,8,128]{2,1,0:T(8,128)S(1)} %get-tuple-element.20.up_ref, f32[88,8,128]{2,1,0:T(8,128)S(1)} %collective-permute-done.low_ref, f32[88,8,128]{2,1,0:T(8,128)S(1)} %collective-permute-done.1.high_ref, ...), custom_call_target="tpu_custom_call" | custom-call | flops 10000000000 | bytes 2000000 | tf_op jit(solution)/shard_map/head/pallas_call | solution.py:41
  28.1 3.1 %tail.1 = (f32[24,8,128]{2,1,0:T(8,128)S(1)}, f32[24,16,128]{2,1,0:T(8,128)S(1)}, f32[2,2,48,8,128]{4,3,2,1,0:T(8,128)S(1)}) custom-call(f32[88,8,128]{2,1,0:T(8,128)S(1)} %get-tuple-element.20.up_ref, f32[88,8,128]{2,1,0:T(8,128)S(1)} %collective-permute-done.low_ref, f32[88,8,128]{2,1,0:T(8,128)S(1)} %collective-permute-done.1.high_ref, ...), custom_call_target="tpu_custom_call" | custom-call | flops 1000000 | bytes 2000000 | tf_op jit(solution)/shard_map/tail/pallas_call | solution.py:41
  31.3 0.1 collective-permute-start.5
  31.4 1.5 %collective-permute-start.4 = (f32[24,8,128]{2,1,0:T(8,128)S(1)}, f32[24,8,128]{2,1,0:T(8,128)S(1)}, u32[]{:S(2)}, u32[]{:S(2)}) collective-permute-start(f32[24,8,128]{2,1,0:T(8,128)S(1)} %get-tuple-element.32.mid_ref), channel_id=1, source_target_pairs={{0,8},{8,16},{16,24},{24,32},{32,40},{40,48},{48,56},{56,64},{64,7... | collective-permute-start | bytes 294920 | tf_op jit(solution)/shard_map/ppermute | solution.py:490
  32.8 3.0 %collective-permute-done.5.highy_ref = f32[24,8,128]{2,1,0:T(8,128)S(1)} collective-permute-done((f32[24,8,128]{2,1,0:T(8,128)S(1)}, f32[24,8,128]{2,1,0:T(8,128)S(1)}, u32[]{:S(2)}, u32[]{:S(2)}) %collective-permute-start.5) | collective-permute-done | bytes 98336 | tf_op jit(solution)/shard_map/ppermute | solution.py:491
  35.8 2.5 %collective-permute-done.4.lowy_ref = f32[24,8,128]{2,1,0:T(8,128)S(1)} collective-permute-done((f32[24,8,128]{2,1,0:T(8,128)S(1)}, f32[24,8,128]{2,1,0:T(8,128)S(1)}, u32[]{:S(2)}, u32[]{:S(2)}) %collective-permute-start.4) | collective-permute-done | bytes 98336 | tf_op jit(solution)/shard_map/ppermute | solution.py:490
  38.2 2.8 %last.1.own_ref = f32[24,8,128]{2,1,0:T(8,128)S(1)} custom-call(f32[88,8,128]{2,1,0:T(8,128)S(1)} %get-tuple-element.20.up_ref, f32[88,8,128]{2,1,0:T(8,128)S(1)} %collective-permute-done.low_ref, f32[88,8,128]{2,1,0:T(8,128)S(1)} %collective-permute-done.1.high_ref, f32[24,8,128]{2,1,0:T(8,128)S(1)} %get-tuple-element.22.pot_ref, ...), custom_call_target="tpu_custom_call" | custom-call | flops 1000000 | bytes 2000000 | tf_op jit(solution)/shard_map/last/pallas_call | solution.py:41
  41.0 1.9 %collective-permute-start.6 = (f32[24,8,128]{2,1,0:T(8,128)S(1)}, f32[24,8,128]{2,1,0:T(8,128)S(1)}, u32[]{:S(2)}, u32[]{:S(2)}) collective-permute-start(f32[24,8,128]{2,1,0:T(8,128)S(1)} %last.1.own_ref), channel_id=1, source_target_pairs={{0,1},{1,0},{2,3},{3,2},{4,5},{5,4},{6,7},{7,6},{8,9},{9,8},{10,11... | collective-permute-start | bytes 294920 | tf_op jit(solution)/shard_map/ppermute | solution.py:500
  43.0 0.9 %collective-permute-done.6.other_ref = f32[24,8,128]{2,1,0:T(8,128)S(1)} collective-permute-done((f32[24,8,128]{2,1,0:T(8,128)S(1)}, f32[24,8,128]{2,1,0:T(8,128)S(1)}, u32[]{:S(2)}, u32[]{:S(2)}) %collective-permute-start.6) | collective-permute-done | bytes 98336 | tf_op jit(solution)/shard_map/ppermute | solution.py:500
  44.0 3.0 %collective-permute-start.7 = (f32[24,8,128]{2,1,0:T(8,128)S(1)}, f32[24,8,128]{2,1,0:T(8,128)S(1)}, u32[]{:S(2)}, u32[]{:S(2)}) collective-permute-start(f32[24,8,128]{2,1,0:T(8,128)S(1)} %get-tuple-element.35), channel_id=1, source_target_pairs={{0,4},{1,5},{2,6},{3,7},{4,0},{5,1},{6,2},{7,3},{8,12},{9,13},{10,... | collective-permute-start | bytes 294920 | tf_op jit(solution)/shard_map/ppermute | solution.py:505
  47.0 0.4 collective-permute-start.8
  47.4 0.4 collective-permute-start.9
  47.7 0.6 %store.1 = f32[24,8,128]{2,1,0:T(8,128)} custom-call(f32[24,8,128]{2,1,0:T(8,128)S(1)} %last.1.own_ref), custom_call_target="tpu_custom_call" | custom-call | flops 1000000 | bytes 2000000 | tf_op jit(solution)/shard_map/store/pallas_call | solution.py:41
  48.4 1.2 %collective-permute-done.7.one_ref = f32[24,8,128]{2,1,0:T(8,128)S(1)} collective-permute-done((f32[24,8,128]{2,1,0:T(8,128)S(1)}, f32[24,8,128]{2,1,0:T(8,128)S(1)}, u32[]{:S(2)}, u32[]{:S(2)}) %collective-permute-start.7) | collective-permute-done | bytes 98336 | tf_op jit(solution)/shard_map/ppermute | solution.py:505
  49.6 2.5 %collective-permute-done.8.two_ref = f32[24,8,128]{2,1,0:T(8,128)S(1)} collective-permute-done((f32[24,8,128]{2,1,0:T(8,128)S(1)}, f32[24,8,128]{2,1,0:T(8,128)S(1)}, u32[]{:S(2)}, u32[]{:S(2)}) %collective-permute-start.8) | collective-permute-done | bytes 98336 | tf_op jit(solution)/shard_map/ppermute | solution.py:505
  52.0 0.0 collective-permute-done.9.three_ref
  52.0 0.7 %total.1 = f32[24,8,128]{2,1,0:T(8,128)} custom-call(f32[24,8,128]{2,1,0:T(8,128)S(1)} %get-tuple-element.34.base_ref, f32[24,8,128]{2,1,0:T(8,128)S(1)} %collective-permute-done.7.one_ref, f32[24,8,128]{2,1,0:T(8,128)S(1)} %collective-permute-done.8.two_ref, f32[24,8,128]{2,1,0:T(8,128)S(1)} %collective-permute-done.9.three_ref), custom_call_target="tpu_custom_call" | custom-call | flops 1000000 | bytes 2000000 | tf_op jit(solution)/shard_map/total/pallas_call | solution.py:41
  (6 shorter events, 0.1 us)
Async XLA Ops:
  2.8 8.7 %copy-start = (f32[8,8]{1,0:T(8,128)S(1)}, f32[8,8]{1,0:T(8,128)}, u32[]{:S(2)}) copy-start(f32[8,8]{1,0:T(8,128)} %ritz_ref.1) | copy-start | bytes 772
  2.8 15.8 %collective-permute-start.1 = (f32[88,8,128]{2,1,0:T(8,128)S(1)}, f32[88,8,128]{2,1,0:T(8,128)S(1)}, u32[]{:S(2)}, u32[]{:S(2)}) collective-permute-start(f32[88,8,128]{2,1,0:T(8,128)S(1)} %get-tuple-element.21), channel_id=1, source_target_pairs={{0,248},{8,0},{16,8},{24,16},{32,24},{40,32},{48,40},{56,48},{64,5... | collective-permute-start | bytes 1081352 | tf_op jit(solution)/shard_map/ppermute | solution.py:456
  11.5 12.3 %collective-permute-start = (f32[88,8,128]{2,1,0:T(8,128)S(1)}, f32[88,8,128]{2,1,0:T(8,128)S(1)}, u32[]{:S(2)}, u32[]{:S(2)}) collective-permute-start(f32[88,8,128]{2,1,0:T(8,128)S(1)} %get-tuple-element.20.up_ref), channel_id=1, source_target_pairs={{0,8},{8,16},{16,24},{24,32},{32,40},{40,48},{48,56},{56,64},{64,7... | collective-permute-start | bytes 1081352 | tf_op jit(solution)/shard_map/ppermute | solution.py:455
  18.6 9.5 %collective-permute-start.3 = (f32[88,8,128]{2,1,0:T(8,128)S(1)}, f32[88,8,128]{2,1,0:T(8,128)S(1)}, u32[]{:S(2)}, u32[]{:S(2)}) collective-permute-start(f32[88,8,128]{2,1,0:T(8,128)S(1)} %collective-permute-done.1.high_ref), channel_id=1, source_target_pairs={{0,1},{1,0},{2,3},{3,2},{4,5},{5,4},{6,7},{7,6},{8,9},{9,8},{10,11... | collective-permute-start | bytes 1081352 | tf_op jit(solution)/shard_map/ppermute | solution.py:471
  23.8 4.4 %collective-permute-start.2 = (f32[88,8,128]{2,1,0:T(8,128)S(1)}, f32[88,8,128]{2,1,0:T(8,128)S(1)}, u32[]{:S(2)}, u32[]{:S(2)}) collective-permute-start(f32[88,8,128]{2,1,0:T(8,128)S(1)} %collective-permute-done.low_ref), channel_id=1, source_target_pairs={{0,1},{1,0},{2,3},{3,2},{4,5},{5,4},{6,7},{7,6},{8,9},{9,8},{10,11... | collective-permute-start | bytes 1081352 | tf_op jit(solution)/shard_map/ppermute | solution.py:470
  31.3 4.5 %collective-permute-start.5 = (f32[24,8,128]{2,1,0:T(8,128)S(1)}, f32[24,8,128]{2,1,0:T(8,128)S(1)}, u32[]{:S(2)}, u32[]{:S(2)}) collective-permute-start(f32[24,8,128]{2,1,0:T(8,128)S(1)} %get-tuple-element.32.mid_ref), channel_id=1, source_target_pairs={{0,248},{8,0},{16,8},{24,16},{32,24},{40,32},{48,40},{56,48},{64,5... | collective-permute-start | bytes 294920 | tf_op jit(solution)/shard_map/ppermute | solution.py:491
  31.4 6.9 %collective-permute-start.4 = (f32[24,8,128]{2,1,0:T(8,128)S(1)}, f32[24,8,128]{2,1,0:T(8,128)S(1)}, u32[]{:S(2)}, u32[]{:S(2)}) collective-permute-start(f32[24,8,128]{2,1,0:T(8,128)S(1)} %get-tuple-element.32.mid_ref), channel_id=1, source_target_pairs={{0,8},{8,16},{16,24},{24,32},{32,40},{40,48},{48,56},{56,64},{64,7... | collective-permute-start | bytes 294920 | tf_op jit(solution)/shard_map/ppermute | solution.py:490
  41.0 2.9 %collective-permute-start.6 = (f32[24,8,128]{2,1,0:T(8,128)S(1)}, f32[24,8,128]{2,1,0:T(8,128)S(1)}, u32[]{:S(2)}, u32[]{:S(2)}) collective-permute-start(f32[24,8,128]{2,1,0:T(8,128)S(1)} %last.1.own_ref), channel_id=1, source_target_pairs={{0,1},{1,0},{2,3},{3,2},{4,5},{5,4},{6,7},{7,6},{8,9},{9,8},{10,11... | collective-permute-start | bytes 294920 | tf_op jit(solution)/shard_map/ppermute | solution.py:500
  44.0 5.6 %collective-permute-start.7 = (f32[24,8,128]{2,1,0:T(8,128)S(1)}, f32[24,8,128]{2,1,0:T(8,128)S(1)}, u32[]{:S(2)}, u32[]{:S(2)}) collective-permute-start(f32[24,8,128]{2,1,0:T(8,128)S(1)} %get-tuple-element.35), channel_id=1, source_target_pairs={{0,4},{1,5},{2,6},{3,7},{4,0},{5,1},{6,2},{7,3},{8,12},{9,13},{10,... | collective-permute-start | bytes 294920 | tf_op jit(solution)/shard_map/ppermute | solution.py:505
  47.0 5.1 %collective-permute-start.8 = (f32[24,8,128]{2,1,0:T(8,128)S(1)}, f32[24,8,128]{2,1,0:T(8,128)S(1)}, u32[]{:S(2)}, u32[]{:S(2)}) collective-permute-start(f32[24,8,128]{2,1,0:T(8,128)S(1)} %get-tuple-element.36), channel_id=1, source_target_pairs={{0,2},{1,3},{2,0},{3,1},{4,6},{5,7},{6,4},{7,5},{8,10},{9,11},{10,... | collective-permute-start | bytes 294920 | tf_op jit(solution)/shard_map/ppermute | solution.py:505
  47.4 4.7 %collective-permute-start.9 = (f32[24,8,128]{2,1,0:T(8,128)S(1)}, f32[24,8,128]{2,1,0:T(8,128)S(1)}, u32[]{:S(2)}, u32[]{:S(2)}) collective-permute-start(f32[24,8,128]{2,1,0:T(8,128)S(1)} %get-tuple-element.37), channel_id=1, source_target_pairs={{0,6},{1,7},{2,4},{3,5},{4,2},{5,3},{6,0},{7,1},{8,14},{9,15},{10,... | collective-permute-start | bytes 294920 | tf_op jit(solution)/shard_map/ppermute | solution.py:505

commit v4 on v3

--- a/solution.py
+++ b/solution.py
@@ -131,7 +131,8 @@
             table[l * BX + i] = work.at[i][pl.ds(l, 8, stride=8), :]
 
 
-def prepare_kernel(proj_ref, ritz_ref, table_ref, zst_ref, sums_ref, factors_ref, work):
+def prepare_kernel(proj_ref, up_ref, ritz_ref, table_ref, zst_ref, sums_ref, hot_ref, back_ref, factors_ref, work):
+    write_one_hot(up_ref, hot_ref, back_ref)
     band = lax.axis_index("band")
     row = lax.broadcasted_iota(jnp.int32, (8, 8), 0)
     column = lax.broadcasted_iota(jnp.int32, (8, 8), 1)
@@ -184,18 +185,21 @@
         source = self.sources[group]
         return jnp.concatenate([source[TILE_META], source[TILE_META + 2]], 1)
 
-    def one_hot(self, group):
-        source = self.sources[group]
-        column = jnp.concatenate(
-            [source[TILE_META + 1 + 2 * t, ROW_Z : ROW_Z + 1, :] for t in range(2)], 1
-        )
-        cells = lax.broadcasted_iota(jnp.int32, (NZ, LANES), 0).astype(jnp.float32)
-        return jnp.where(cells == column, 1.0, 0.0).astype(jnp.bfloat16)
+
+def write_one_hot(source, hot_ref, back_ref):
+    column = jnp.concatenate([source[TILE_META + 1 + 2 * t, ROW_Z : ROW_Z + 1, :] for t in range(2)], 1)
+    cells = lax.broadcasted_iota(jnp.int32, (NZ, LANES), 0).astype(jnp.float32)
+    hot = jnp.where(cells == column, 1.0, 0.0)
+    back = hot.T.astype(jnp.bfloat16)
+    hot = hot.astype(jnp.bfloat16)
+    for term in range(2):
+        hot_ref[NZ * term : NZ * term + NZ, :] = hot
+        back_ref[LANES * term : LANES * term + LANES, :] = back
 
 
 def gather_columns(group, field2, first_in, planes_in, skip, gathered, onehot):
     rows = slice(NY * first_in, NY * (first_in + planes_in))
-    columns = dot(field2[rows, :], jnp.concatenate([onehot, onehot], 0)).reshape(planes_in, NY, LANES)
+    columns = dot(field2[rows, :], onehot[...]).reshape(planes_in, NY, LANES)
     for tile in range(2):
         part = columns[:, :, half(tile)]
         gathered[group][tile, skip : skip + planes_in, 0:16, :] = part
@@ -243,18 +247,13 @@
                 pltpu.store(placed[group].at[tile, x0 + i, pl.ds(y0, 8), :], contrib[i][tile], mask=mine)
 
 
-def spread_group(group, first, count, placed, onehot):
+def spread_group(group, first, count, placed, back):
     planes = slice(first, first + count)
     tiles = []
     for tile in range(2):
         folded = placed[group][tile, planes, 0:8, :] + placed[group][tile, planes, 16:24, :]
         tiles.append(jnp.concatenate([folded, placed[group][tile, planes, 8:16, :]], 1).reshape(count * NY, 128))
-    twice = jnp.concatenate([onehot, onehot], 1)
-    spread = lax.dot_general(
-        two_terms(jnp.concatenate(tiles, 1), 1), twice, (((1,), (1,)), ((), ())),
-        preferred_element_type=jnp.float32,
-    )
-    return spread.reshape(count, NY, NZ)
+    return dot(two_terms(jnp.concatenate(tiles, 1), 1), back[...]).reshape(count, NY, NZ)
 
 
 def along_z(field2, rows, zst_ref):
@@ -288,17 +287,18 @@
         field2[192 * n : 192 * n + 192, :] = two_terms(value.reshape(192, NZ), 1)
 
 
-def head_kernel(up_ref, low_ref, high_ref, pot_ref, table_ref, zst_ref, sums_ref,
-                half_ref, values_ref, partial_ref,
+def head_kernel(up_ref, high_ref, low_ref, pot_ref, table_ref, zst_ref, sums_ref, hot_ref, back_ref,
+                half_ref, values_ref, partial_ref, hots_ref, backs_ref,
                 low_xy, own_xy, high_xy, padded, field2, gathered, placed, local, work, sems):
     boxes = Boxes((low_ref, up_ref, high_ref), (low_xy, own_xy, high_xy), sems)
     load_fields([r[TILE_Y : TILE_Y + 24] for r in (low_ref, up_ref, high_ref)], padded, field2)
     clear(placed)
     gathered[2][:, 12:SPAN] = jnp.zeros((2, SPAN - 12, 24, 128), jnp.float32)
-    own_hot = boxes.one_hot(1)
-    gather_columns(1, field2, 12, SPAN, 0, gathered, own_hot)
-    gather_columns(0, field2, 0, SPAN, 0, gathered, boxes.one_hot(0))
-    gather_columns(2, field2, 24, 12, 0, gathered, boxes.one_hot(2))
+    for n, source in enumerate((low_ref, high_ref)):
+        write_one_hot(source, hots_ref.at[n], backs_ref.at[n])
+    gather_columns(1, field2, 12, SPAN, 0, gathered, hot_ref)
+    gather_columns(0, field2, 0, SPAN, 0, gathered, hots_ref.at[0])
+    gather_columns(2, field2, 24, 12, 0, gathered, hots_ref.at[1])
     local[...] = along_z(field2, slice(96, 480), zst_ref).reshape(24, NY, NZ)
     for p in range(24):
         laplace = stencil_plane(padded, p + 6) + local[p]
@@ -314,11 +314,11 @@
             for tile in range(2):
                 values_ref[n, i, tile] = values[i][tile]
     partial_ref[0:6] = local[0:6]
-    partial_ref[6:23] = local[6:23] + spread_group(1, 0, 17, placed, own_hot) * (1.0 / HALF)
+    partial_ref[6:23] = local[6:23] + spread_group(1, 0, 17, placed, back_ref) * (1.0 / HALF)
     partial_ref[23] = local[23]
 
 
-def second_step(boxes, hots, padded1, field2, gathered, placed, local, nonlocal_, pot_ref, tables, zst_ref, sums):
+def second_step(boxes, hots, backs, padded1, field2, gathered, placed, local, nonlocal_, pot_ref, tables, zst_ref, sums):
     for group, first, planes, skip in ((0, 0, 11, 6), (1, 6, SPAN, 0)):
         gather_columns(group, field2, first, planes, skip, gathered, hots[group])
     for group in range(2):
@@ -329,14 +329,14 @@
         laplace = stencil_plane(padded1, p + 6) + local[p]
         pot = potential_plane(p + 6, None, pot_ref, None)
         local[p] = -0.5 * laplace + (pot - CENTER) * here
-    nonlocal_[0:12] = spread_group(1, 0, 12, placed, hots[1])
-    nonlocal_[0:5] += spread_group(0, 12, 5, placed, hots[0])
+    nonlocal_[0:12] = spread_group(1, 0, 12, placed, backs[1])
+    nonlocal_[0:5] += spread_group(0, 12, 5, placed, backs[0])
     for p in range(12):
         yield p, (local[p] + nonlocal_[p]) * (2.0 / HALF)
 
 
-def tail_kernel(up_ref, low_ref, high_ref, pot_ref, table_ref, zst_ref, sums_ref,
-                half_ref, values_ref, partial_ref, lowsib_ref, highsib_ref,
+def tail_kernel(up_ref, high_ref, low_ref, pot_ref, table_ref, zst_ref, sums_ref, hot_ref, back_ref,
+                half_ref, values_ref, partial_ref, hots_ref, backs_ref, highsib_ref, lowsib_ref,
                 out_ref, kept_ref, tables_ref,
                 low_xy, own_xy, high_xy, padded1, field2, gathered, placed, local, nonlocal_, work, sems):
     core = lax.axis_index("band") % 2
@@ -346,35 +346,36 @@
     for n, source in enumerate((lowsib_ref, highsib_ref)):
         spread_projectors(lambda part, a: source[TILE_P + 16 * part + a], work, tables_ref.at[n, 1 - core])
         tables_ref[n, core] = half_ref[n]
-    hots = [boxes.one_hot(g) for g in range(3)]
+    hots, backs = (hots_ref.at[0], hot_ref), (backs_ref.at[0], back_ref, backs_ref.at[1])
     boxes.wait()
     sums = sums_ref[...]
     for n, group in enumerate((0, 2)):
         values = [[values_ref[n, i, tile] for tile in range(2)] for i in range(BX)]
         contributions(group, values, tables_ref.at[n], placed, boxes, sums)
-    nonlocal_[0:11] = spread_group(0, 6, 11, placed, hots[0])
+    nonlocal_[0:11] = spread_group(0, 6, 11, placed, backs[0])
     nonlocal_[11:18] = jnp.zeros((7, NY, NZ), jnp.float32)
-    nonlocal_[18:24] = spread_group(2, 0, 6, placed, hots[2])
+    nonlocal_[18:24] = spread_group(2, 0, 6, placed, backs[2])
     for p in range(24):
         updated = partial_ref[p] + nonlocal_[p] * (1.0 / HALF)
         kept_ref[p] = updated
         fill(padded1, p, updated[None])
         field2[16 * p : 16 * p + 16, :] = two_terms(updated, 1)
     tables = (tables_ref.at[0], table_ref)
-    for p, value in second_step(boxes, hots, padded1, field2, gathered, placed, local, nonlocal_, pot_ref, tables,
+    for p, value in second_step(boxes, hots, backs, padded1, field2, gathered, placed, local, nonlocal_, pot_ref, tables,
                                 zst_ref, sums):
         out_ref[2 * p : 2 * p + 2] = (value - up_ref[TILE_Y + 2 * p : TILE_Y + 2 * p + 2].reshape(NY, NZ)).reshape(2, 8, 128)
 
 
-def last_kernel(up_ref, low_ref, high_ref, pot_ref, table_ref, zst_ref, sums_ref, kept_ref, tables_ref,
-                mid_ref, lowy_ref, highy_ref,
+def last_kernel(up_ref, high_ref, low_ref, pot_ref, table_ref, zst_ref, sums_ref, hot_ref, back_ref,
+                kept_ref, tables_ref, hots_ref, backs_ref,
+                mid_ref, highy_ref, lowy_ref,
                 out_ref,
                 low_xy, own_xy, high_xy, padded, padded1, field2, gathered, placed, local, nonlocal_, sems):
     boxes = Boxes((low_ref, up_ref, high_ref), (low_xy, own_xy, high_xy), sems)
     load_fields([r[...] for r in (lowy_ref, mid_ref, highy_ref)], padded, field2)
     clear(placed)
     gathered[2][:, 12:SPAN] = jnp.zeros((2, SPAN - 12, 24, 128), jnp.float32)
-    hots = [boxes.one_hot(g) for g in range(3)]
+    hots, backs = (hots_ref.at[0], hot_ref, hots_ref.at[1]), (backs_ref.at[0], back_ref, backs_ref.at[1])
     sums = sums_ref[...]
     tables = (tables_ref.at[0], table_ref, tables_ref.at[1])
     for group, planes in ((0, SPAN), (1, SPAN), (2, 12)):
@@ -389,15 +390,15 @@
     windows = [read_windows(group, gathered, boxes) for group in range(3)]
     for group in range(3):
         contributions(group, windows[group], tables[group], placed, boxes, sums)
-    nonlocal_[0:11] = spread_group(0, 6, 11, placed, hots[0])
+    nonlocal_[0:11] = spread_group(0, 6, 11, placed, backs[0])
     nonlocal_[11:24] = jnp.zeros((13, NY, NZ), jnp.float32)
-    nonlocal_[6:23] += spread_group(1, 0, 17, placed, hots[1])
-    nonlocal_[18:24] += spread_group(2, 0, 6, placed, hots[2])
+    nonlocal_[6:23] += spread_group(1, 0, 17, placed, backs[1])
+    nonlocal_[18:24] += spread_group(2, 0, 6, placed, backs[2])
     for p in range(24):
         updated = local[p] + nonlocal_[p] * (2.0 / HALF)
         fill(padded1, p, updated[None])
         field2[16 * p : 16 * p + 16, :] = two_terms(updated, 1)
-    for p, value in second_step(boxes, hots, padded1, field2, gathered, placed, local, nonlocal_, pot_ref, tables,
+    for p, value in second_step(boxes, hots, backs, padded1, field2, gathered, placed, local, nonlocal_, pot_ref, tables,
                                 zst_ref, sums):
         out_ref[2 * p : 2 * p + 2] = (value - padded[p + 12, 8:24, :]).reshape(2, 8, 128)
 
@@ -454,26 +455,34 @@
     )
     low = lax.ppermute(up, "dom", ring("dom", 1))
     high = lax.ppermute(down, "dom", ring("dom", -1))
-    table, zst, sums, factors = call(
+    table, zst, sums, hot, back, factors = call(
         prepare_kernel,
         [
             shape(2, PAIRS, 8, 128),
             shape(384, NZ, dtype=jnp.bfloat16),
             shape(LANES, LANES, dtype=jnp.bfloat16),
+            shape(2 * NZ, LANES, dtype=jnp.bfloat16),
+            shape(2 * LANES, NZ, dtype=jnp.bfloat16),
             shape(8, 8, 128),
         ],
-        [VMEM] * 2,
-        (proj, ritz),
+        [VMEM] * 3,
+        (proj, down, ritz),
         "prepare",
         [WORK],
     )
+    highsib = lax.ppermute(high, "band", meet("band", 1))
     lowsib = lax.ppermute(low, "band", meet("band", 1))
-    highsib = lax.ppermute(high, "band", meet("band", 1))
-    common = (up, low, high, pot, table, zst, sums)
-    halves, values, partial = call(
+    common = (down, high, low, pot, table, zst, sums, hot, back)
+    halves, values, partial, hots, backs = call(
         head_kernel,
-        [shape(2, PAIRS, 8, 128), shape(2, BX, 2, 8, 128), shape(24, NY, NZ)],
-        [VMEM] * 7,
+        [
+            shape(2, PAIRS, 8, 128),
+            shape(2, BX, 2, 8, 128),
+            shape(24, NY, NZ),
+            shape(2, 2 * NZ, LANES, dtype=jnp.bfloat16),
+            shape(2, 2 * LANES, NZ, dtype=jnp.bfloat16),
+        ],
+        [VMEM] * 9,
         common,
         "head",
         XY + [PADDED, FIELD2, BOXED, BOXED, PLANES, WORK, COPIES],
@@ -482,8 +491,8 @@
     second, first, tables = call(
         tail_kernel,
         [shape(24, 8, 128), shape(24, NY, NZ), shape(2, 2, PAIRS, 8, 128)],
-        [VMEM] * 12,
-        common + (halves, values, partial, lowsib, highsib),
+        [VMEM] * 16,
+        common + (halves, values, partial, hots, backs, highsib, lowsib),
         "tail",
         XY + [PADDED1, FIELD2, BOXED, BOXED, PLANES, PLANES, WORK, COPIES],
     )
@@ -492,8 +501,8 @@
     (fourth,) = call(
         last_kernel,
         [shape(24, 8, 128)],
-        [VMEM] * 12,
-        common + (first, tables, second, low_y, high_y),
+        [VMEM] * 16,
+        common + (first, tables, hots, backs, second, high_y, low_y),
         "last",
         XY + [PADDED, PADDED1, FIELD2, BOXED, BOXED, PLANES, PLANES, COPIES],
     )

time: 52.8 us -> 48.4 us (0.917)
  waiting for transfers between devices: 19.7 us -> 13.9 us
  starting transfers between devices: 19.3 us -> 20.2 us
    ppermute x1, waiting for transfers between devices: 6.01 us -> 0.01 us  [shards(): high = lax.ppermute(down, 'dom', ring('dom', -1))]
    ppermute x1, starting transfers between devices: 0.09 us -> 4.94 us  [shards(): high_y = lax.ppermute(second, 'dom', ring('dom', -1))]
    ppermute x1, waiting for transfers between devices: 3.66 us -> 6.89 us  [shards(): low = lax.ppermute(up, 'dom', ring('dom', 1))]
    ppermute x1, waiting for transfers between devices: 2.96 us -> 0.01 us  [shards(): high_y = lax.ppermute(second, 'dom', ring('dom', -1))]
    ppermute x1, starting transfers between devices: 0.01 us -> 2.12 us  [shards(): low = lax.ppermute(up, 'dom', ring('dom', 1))]
    ppermute x1, starting transfers between devices: 8.68 us -> 6.65 us  [shards(): high = lax.ppermute(down, 'dom', ring('dom', -1))]
    ppermute x1, starting transfers between devices: 1.55 us -> 0.01 us  [shards(): highsib = lax.ppermute(high, 'band', meet('band', 1))]
    ppermute x1, starting transfers between devices: 1.45 us -> 0.08 us  [shards(): low_y = lax.ppermute(second, 'dom', ring('dom', 1))]
  transfers between devices with their start and end apart: 10 -> 10, of which waited for: 7 -> 5; matrix products, arithmetic and copies ran while one was open for 0% -> 0% of each run, Pallas kernels for 8% -> 9%
where the time goes in v4:
time: 48.4 us; the launch traced here: 47.9 us
  starting transfers between devices  20.2 us (42%)
  waiting for transfers between devices  13.9 us (29%)
  Pallas kernels  12.5 us (26%)
  between operations  1.36 us (3%)
    pallas_call x8, Pallas kernels, call(): pl.pallas_call(kernel, out_shape=outs, in_specs=ins, out_specs=out_specs...  12.5 us
    ppermute x1, waiting for transfers between devices, shards(): low = lax.ppermute(up, 'dom', ring('dom', 1))  6.89 us
    ppermute x1, starting transfers between devices, shards(): high = lax.ppermute(down, 'dom', ring('dom', -1))  6.65 us
    ppermute x1, starting transfers between devices, shards(): high_y = lax.ppermute(second, 'dom', ring('dom', -1))  4.94 us
    ppermute x3, starting transfers between devices, shards(): lax.ppermute(v, 'band', meet('band', 2 * hop))  3.78 us
    ppermute x3, waiting for transfers between devices, shards(): lax.ppermute(v, 'band', meet('band', 2 * hop))  3.65 us
    ppermute x1, waiting for transfers between devices, shards(): low_y = lax.ppermute(second, 'dom', ring('dom', 1))  2.39 us
    ppermute x1, starting transfers between devices, shards(): low = lax.ppermute(up, 'dom', ring('dom', 1))  2.12 us
  transfers between devices with their start and end apart: 10, of which 5 were waited for; matrix products, arithmetic and copies ran while one was open for 0% of the time, Pallas kernels for 9%

profile of v4, /device:TPU:1, one launch (start us, length us, event | category | flops | bytes accessed | tf_op | source)
XLA Modules:
  0.0 47.9 jit_solution(16670006132068315165)
XLA Ops:
  1.3 1.5 %pack.1 = (f32[88,8,128]{2,1,0:T(8,128)S(1)}, f32[88,8,128]{2,1,0:T(8,128)S(1)}, f32[24,8,128]{2,1,0:T(8,128)S(1)}, f32[96,8,128]{2,1,0:T(8,128)S(1)}) custom-call(f32[24,8,128]{2,1,0:T(8,128)} %bitcast.7, f32[24,8,128]{2,1,0:T(8,128)} %bitcast.8, f32[32,8,384]{2,1,0:T(8,128)} %proj_hbm.1, f32[8,32]{1,0:T(8,128)} %bitcast.10, s32[3,32]{1,0:T(4,128)} %bitcast.11, ...), custom_call_target="tpu_custom_call" | custom-call | flops 1000000 | bytes 2000000 | tf_op jit(solution)/shard_map/pack/pallas_call | solution.py:41
  2.8 0.0 copy-start
  2.8 2.1 %collective-permute-start.1 = (f32[88,8,128]{2,1,0:T(8,128)S(1)}, f32[88,8,128]{2,1,0:T(8,128)S(1)}, u32[]{:S(2)}, u32[]{:S(2)}) collective-permute-start(f32[88,8,128]{2,1,0:T(8,128)S(1)} %get-tuple-element.25), channel_id=1, source_target_pairs={{0,8},{8,16},{16,24},{24,32},{32,40},{40,48},{48,56},{56,64},{64,7... | collective-permute-start | bytes 1081352 | tf_op jit(solution)/shard_map/ppermute | solution.py:456
  4.9 6.6 %collective-permute-start = (f32[88,8,128]{2,1,0:T(8,128)S(1)}, f32[88,8,128]{2,1,0:T(8,128)S(1)}, u32[]{:S(2)}, u32[]{:S(2)}) collective-permute-start(f32[88,8,128]{2,1,0:T(8,128)S(1)} %get-tuple-element.24.up_ref), channel_id=1, source_target_pairs={{0,248},{8,0},{16,8},{24,16},{32,24},{40,32},{48,40},{56,48},{64,5... | collective-permute-start | bytes 1081352 | tf_op jit(solution)/shard_map/ppermute | solution.py:457
  11.6 1.1 %prepare.1 = (f32[2,48,8,128]{3,2,1,0:T(8,128)S(1)}, bf16[384,128]{1,0:T(8,128)(2,1)S(1)}, bf16[256,256]{1,0:T(8,128)(2,1)S(1)}, bf16[256,256]{1,0:T(8,128)(2,1)...) custom-call(f32[96,8,128]{2,1,0:T(8,128)S(1)} %get-tuple-element.27.proj_ref, ...), custom_call_target="tpu_custom_call" | custom-call | flops 1000000 | bytes 2000000 | tf_op jit(solution)/shard_map/prepare/pallas_call | solution.py:41
  12.7 6.9 %collective-permute-done.1.low_ref = f32[88,8,128]{2,1,0:T(8,128)S(1)} collective-permute-done((f32[88,8,128]{2,1,0:T(8,128)S(1)}, f32[88,8,128]{2,1,0:T(8,128)S(1)}, u32[]{:S(2)}, u32[]{:S(2)}) %collective-permute-start.1) | collective-permute-done | bytes 360480 | tf_op jit(solution)/shard_map/ppermute | solution.py:456
  19.6 1.2 %collective-permute-start.3 = (f32[88,8,128]{2,1,0:T(8,128)S(1)}, f32[88,8,128]{2,1,0:T(8,128)S(1)}, u32[]{:S(2)}, u32[]{:S(2)}) collective-permute-start(f32[88,8,128]{2,1,0:T(8,128)S(1)} %collective-permute-done.1.low_ref), channel_id=1, source_target_pairs={{0,1},{1,0},{2,3},{3,2},{4,5},{5,4},{6,7},{7,6},{8,9},{9,8},{10,11... | collective-permute-start | bytes 1081352 | tf_op jit(solution)/shard_map/ppermute | solution.py:474
  20.9 0.0 collective-permute-start.2
  20.9 2.6 %head.1 = (f32[2,48,8,128]{3,2,1,0:T(8,128)S(1)}, f32[2,6,2,8,128]{4,3,2,1,0:T(8,128)S(1)}, f32[24,16,128]{2,1,0:T(8,128)S(1)}, bf16[2,256,256]{2,1,0:T(8,128)(2,1)S(1)}, bf16[2,512,128]{2,1,0:T(8,128)(2,1)S(1)}) custom-call(f32[88,8,128]{2,1,0:T(8,128)S(1)} %get-tuple-element.24.up_ref, f32[88,8,128]{2,1,0:T(8,128)S(1)} %collective-permute-done.high_ref, ...), custom_call_target="tpu_custom_call" | custom-call | flops 10000000000 | bytes 2000000 | tf_op jit(solution)/shard_map/head/pallas_call | solution.py:41
  23.5 3.1 %tail.1 = (f32[24,8,128]{2,1,0:T(8,128)S(1)}, f32[24,16,128]{2,1,0:T(8,128)S(1)}, f32[2,2,48,8,128]{4,3,2,1,0:T(8,128)S(1)}) custom-call(f32[88,8,128]{2,1,0:T(8,128)S(1)} %get-tuple-element.24.up_ref, f32[88,8,128]{2,1,0:T(8,128)S(1)} %collective-permute-done.high_ref, f32[88,8,128]{2,1,0:T(8,128)S(1)} %collective-permute-done.1.low_ref, ...), custom_call_target="tpu_custom_call" | custom-call | flops 1000000 | bytes 2000000 | tf_op jit(solution)/shard_map/tail/pallas_call | solution.py:41
  26.5 0.1 collective-permute-start.5
  26.6 4.9 %collective-permute-start.4 = (f32[24,8,128]{2,1,0:T(8,128)S(1)}, f32[24,8,128]{2,1,0:T(8,128)S(1)}, u32[]{:S(2)}, u32[]{:S(2)}) collective-permute-start(f32[24,8,128]{2,1,0:T(8,128)S(1)} %get-tuple-element.40.mid_ref), channel_id=1, source_target_pairs={{0,248},{8,0},{16,8},{24,16},{32,24},{40,32},{48,40},{56,48},{64,5... | collective-permute-start | bytes 294920 | tf_op jit(solution)/shard_map/ppermute | solution.py:500
  31.6 2.4 %collective-permute-done.5.lowy_ref = f32[24,8,128]{2,1,0:T(8,128)S(1)} collective-permute-done((f32[24,8,128]{2,1,0:T(8,128)S(1)}, f32[24,8,128]{2,1,0:T(8,128)S(1)}, u32[]{:S(2)}, u32[]{:S(2)}) %collective-permute-start.5) | collective-permute-done | bytes 98336 | tf_op jit(solution)/shard_map/ppermute | solution.py:499
  34.0 2.8 %last.1.own_ref = f32[24,8,128]{2,1,0:T(8,128)S(1)} custom-call(f32[88,8,128]{2,1,0:T(8,128)S(1)} %get-tuple-element.24.up_ref, f32[88,8,128]{2,1,0:T(8,128)S(1)} %collective-permute-done.high_ref, f32[88,8,128]{2,1,0:T(8,128)S(1)} %collective-permute-done.1.low_ref, f32[24,8,128]{2,1,0:T(8,128)S(1)} %get-tuple-element.26.pot_ref, ...), custom_call_target="tpu_custom_call" | custom-call | flops 1000000 | bytes 2000000 | tf_op jit(solution)/shard_map/last/pallas_call | solution.py:41
  36.8 1.4 %collective-permute-start.6 = (f32[24,8,128]{2,1,0:T(8,128)S(1)}, f32[24,8,128]{2,1,0:T(8,128)S(1)}, u32[]{:S(2)}, u32[]{:S(2)}) collective-permute-start(f32[24,8,128]{2,1,0:T(8,128)S(1)} %last.1.own_ref), channel_id=1, source_target_pairs={{0,1},{1,0},{2,3},{3,2},{4,5},{5,4},{6,7},{7,6},{8,9},{9,8},{10,11... | collective-permute-start | bytes 294920 | tf_op jit(solution)/shard_map/ppermute | solution.py:509
  38.2 0.9 %collective-permute-done.6.other_ref = f32[24,8,128]{2,1,0:T(8,128)S(1)} collective-permute-done((f32[24,8,128]{2,1,0:T(8,128)S(1)}, f32[24,8,128]{2,1,0:T(8,128)S(1)}, u32[]{:S(2)}, u32[]{:S(2)}) %collective-permute-start.6) | collective-permute-done | bytes 98336 | tf_op jit(solution)/shard_map/ppermute | solution.py:509
  39.1 3.0 %collective-permute-start.7 = (f32[24,8,128]{2,1,0:T(8,128)S(1)}, f32[24,8,128]{2,1,0:T(8,128)S(1)}, u32[]{:S(2)}, u32[]{:S(2)}) collective-permute-start(f32[24,8,128]{2,1,0:T(8,128)S(1)} %get-tuple-element.43), channel_id=1, source_target_pairs={{0,4},{1,5},{2,6},{3,7},{4,0},{5,1},{6,2},{7,3},{8,12},{9,13},{10,... | collective-permute-start | bytes 294920 | tf_op jit(solution)/shard_map/ppermute | solution.py:514
  42.1 0.4 collective-permute-start.8
  42.5 0.4 collective-permute-start.9
  42.9 0.6 %store.1 = f32[24,8,128]{2,1,0:T(8,128)} custom-call(f32[24,8,128]{2,1,0:T(8,128)S(1)} %last.1.own_ref), custom_call_target="tpu_custom_call" | custom-call | flops 1000000 | bytes 2000000 | tf_op jit(solution)/shard_map/store/pallas_call | solution.py:41
  43.6 1.2 %collective-permute-done.7.one_ref = f32[24,8,128]{2,1,0:T(8,128)S(1)} collective-permute-done((f32[24,8,128]{2,1,0:T(8,128)S(1)}, f32[24,8,128]{2,1,0:T(8,128)S(1)}, u32[]{:S(2)}, u32[]{:S(2)}) %collective-permute-start.7) | collective-permute-done | bytes 98336 | tf_op jit(solution)/shard_map/ppermute | solution.py:514
  44.8 2.4 %collective-permute-done.8.two_ref = f32[24,8,128]{2,1,0:T(8,128)S(1)} collective-permute-done((f32[24,8,128]{2,1,0:T(8,128)S(1)}, f32[24,8,128]{2,1,0:T(8,128)S(1)}, u32[]{:S(2)}, u32[]{:S(2)}) %collective-permute-start.8) | collective-permute-done | bytes 98336 | tf_op jit(solution)/shard_map/ppermute | solution.py:514
  47.2 0.0 collective-permute-done.9.three_ref
  47.2 0.7 %total.1 = f32[24,8,128]{2,1,0:T(8,128)} custom-call(f32[24,8,128]{2,1,0:T(8,128)S(1)} %get-tuple-element.42.base_ref, f32[24,8,128]{2,1,0:T(8,128)S(1)} %collective-permute-done.7.one_ref, f32[24,8,128]{2,1,0:T(8,128)S(1)} %collective-permute-done.8.two_ref, f32[24,8,128]{2,1,0:T(8,128)S(1)} %collective-permute-done.9.three_ref), custom_call_target="tpu_custom_call" | custom-call | flops 1000000 | bytes 2000000 | tf_op jit(solution)/shard_map/total/pallas_call | solution.py:41
  (6 shorter events, 0.1 us)
Async XLA Ops:
  2.8 8.8 %copy-start = (f32[8,8]{1,0:T(8,128)S(1)}, f32[8,8]{1,0:T(8,128)}, u32[]{:S(2)}) copy-start(f32[8,8]{1,0:T(8,128)} %ritz_ref.1) | copy-start | bytes 772
  2.8 16.8 %collective-permute-start.1 = (f32[88,8,128]{2,1,0:T(8,128)S(1)}, f32[88,8,128]{2,1,0:T(8,128)S(1)}, u32[]{:S(2)}, u32[]{:S(2)}) collective-permute-start(f32[88,8,128]{2,1,0:T(8,128)S(1)} %get-tuple-element.25), channel_id=1, source_target_pairs={{0,8},{8,16},{16,24},{24,32},{32,40},{40,48},{48,56},{56,64},{64,7... | collective-permute-start | bytes 1081352 | tf_op jit(solution)/shard_map/ppermute | solution.py:456
  4.9 15.9 %collective-permute-start = (f32[88,8,128]{2,1,0:T(8,128)S(1)}, f32[88,8,128]{2,1,0:T(8,128)S(1)}, u32[]{:S(2)}, u32[]{:S(2)}) collective-permute-start(f32[88,8,128]{2,1,0:T(8,128)S(1)} %get-tuple-element.24.up_ref), channel_id=1, source_target_pairs={{0,248},{8,0},{16,8},{24,16},{32,24},{40,32},{48,40},{56,48},{64,5... | collective-permute-start | bytes 1081352 | tf_op jit(solution)/shard_map/ppermute | solution.py:457
  19.6 3.8 %collective-permute-start.3 = (f32[88,8,128]{2,1,0:T(8,128)S(1)}, f32[88,8,128]{2,1,0:T(8,128)S(1)}, u32[]{:S(2)}, u32[]{:S(2)}) collective-permute-start(f32[88,8,128]{2,1,0:T(8,128)S(1)} %collective-permute-done.1.low_ref), channel_id=1, source_target_pairs={{0,1},{1,0},{2,3},{3,2},{4,5},{5,4},{6,7},{7,6},{8,9},{9,8},{10,11... | collective-permute-start | bytes 1081352 | tf_op jit(solution)/shard_map/ppermute | solution.py:474
  20.9 2.6 %collective-permute-start.2 = (f32[88,8,128]{2,1,0:T(8,128)S(1)}, f32[88,8,128]{2,1,0:T(8,128)S(1)}, u32[]{:S(2)}, u32[]{:S(2)}) collective-permute-start(f32[88,8,128]{2,1,0:T(8,128)S(1)} %collective-permute-done.high_ref), channel_id=1, source_target_pairs={{0,1},{1,0},{2,3},{3,2},{4,5},{5,4},{6,7},{7,6},{8,9},{9,8},{10,11... | collective-permute-start | bytes 1081352 | tf_op jit(solution)/shard_map/ppermute | solution.py:473
  26.5 7.4 %collective-permute-start.5 = (f32[24,8,128]{2,1,0:T(8,128)S(1)}, f32[24,8,128]{2,1,0:T(8,128)S(1)}, u32[]{:S(2)}, u32[]{:S(2)}) collective-permute-start(f32[24,8,128]{2,1,0:T(8,128)S(1)} %get-tuple-element.40.mid_ref), channel_id=1, source_target_pairs={{0,8},{8,16},{16,24},{24,32},{32,40},{40,48},{48,56},{56,64},{64,7... | collective-permute-start | bytes 294920 | tf_op jit(solution)/shard_map/ppermute | solution.py:499
  26.6 7.3 %collective-permute-start.4 = (f32[24,8,128]{2,1,0:T(8,128)S(1)}, f32[24,8,128]{2,1,0:T(8,128)S(1)}, u32[]{:S(2)}, u32[]{:S(2)}) collective-permute-start(f32[24,8,128]{2,1,0:T(8,128)S(1)} %get-tuple-element.40.mid_ref), channel_id=1, source_target_pairs={{0,248},{8,0},{16,8},{24,16},{32,24},{40,32},{48,40},{56,48},{64,5... | collective-permute-start | bytes 294920 | tf_op jit(solution)/shard_map/ppermute | solution.py:500
  36.8 2.3 %collective-permute-start.6 = (f32[24,8,128]{2,1,0:T(8,128)S(1)}, f32[24,8,128]{2,1,0:T(8,128)S(1)}, u32[]{:S(2)}, u32[]{:S(2)}) collective-permute-start(f32[24,8,128]{2,1,0:T(8,128)S(1)} %last.1.own_ref), channel_id=1, source_target_pairs={{0,1},{1,0},{2,3},{3,2},{4,5},{5,4},{6,7},{7,6},{8,9},{9,8},{10,11... | collective-permute-start | bytes 294920 | tf_op jit(solution)/shard_map/ppermute | solution.py:509
  39.1 5.6 %collective-permute-start.7 = (f32[24,8,128]{2,1,0:T(8,128)S(1)}, f32[24,8,128]{2,1,0:T(8,128)S(1)}, u32[]{:S(2)}, u32[]{:S(2)}) collective-permute-start(f32[24,8,128]{2,1,0:T(8,128)S(1)} %get-tuple-element.43), channel_id=1, source_target_pairs={{0,4},{1,5},{2,6},{3,7},{4,0},{5,1},{6,2},{7,3},{8,12},{9,13},{10,... | collective-permute-start | bytes 294920 | tf_op jit(solution)/shard_map/ppermute | solution.py:514
  42.1 5.1 %collective-permute-start.8 = (f32[24,8,128]{2,1,0:T(8,128)S(1)}, f32[24,8,128]{2,1,0:T(8,128)S(1)}, u32[]{:S(2)}, u32[]{:S(2)}) collective-permute-start(f32[24,8,128]{2,1,0:T(8,128)S(1)} %get-tuple-element.44), channel_id=1, source_target_pairs={{0,2},{1,3},{2,0},{3,1},{4,6},{5,7},{6,4},{7,5},{8,10},{9,11},{10,... | collective-permute-start | bytes 294920 | tf_op jit(solution)/shard_map/ppermute | solution.py:514
  42.5 4.7 %collective-permute-start.9 = (f32[24,8,128]{2,1,0:T(8,128)S(1)}, f32[24,8,128]{2,1,0:T(8,128)S(1)}, u32[]{:S(2)}, u32[]{:S(2)}) collective-permute-start(f32[24,8,128]{2,1,0:T(8,128)S(1)} %get-tuple-element.45), channel_id=1, source_target_pairs={{0,6},{1,7},{2,4},{3,5},{4,2},{5,3},{6,0},{7,1},{8,14},{9,15},{10,... | collective-permute-start | bytes 294920 | tf_op jit(solution)/shard_map/ppermute | solution.py:514

commit v5 on v4

--- a/solution.py
+++ b/solution.py
@@ -37,7 +37,7 @@
     return jax.ShapeDtypeStruct(dims, dtype)
 
 
-def call(kernel, outs, ins, args, name, scratch=(), out_specs=None, flops=1_000_000):
+def call(kernel, outs, ins, args, name, scratch=(), out_specs=None, flops=1_000_000, moved=2_000_000):
     return pl.pallas_call(
         kernel,
         out_shape=outs,
@@ -45,7 +45,7 @@
         out_specs=out_specs or [VMEM] * len(outs),
         scratch_shapes=list(scratch),
         compiler_params=pltpu.CompilerParams(vmem_limit_bytes=32 * 2**20),
-        cost_estimate=pl.CostEstimate(flops=flops, bytes_accessed=2_000_000, transcendentals=0),
+        cost_estimate=pl.CostEstimate(flops=flops, bytes_accessed=moved, transcendentals=0),
         name=name,
     )(*args)
 
@@ -137,8 +137,9 @@
     row = lax.broadcasted_iota(jnp.int32, (8, 8), 0)
     column = lax.broadcasted_iota(jnp.int32, (8, 8), 1)
     for hop in range(4):
-        for n, orbital in enumerate((band, band ^ 1)):
-            picked = jnp.where((row == orbital) & (column == band ^ (2 * hop)), ritz_ref[...], 0.0)
+        for n in range(2):
+            orbital, to = (band ^ (4 + n), band) if hop == 2 else (band ^ n, band ^ (2 * hop))
+            picked = jnp.where((row == orbital) & (column == to), ritz_ref[...], 0.0)
             picked = jnp.sum(jnp.sum(picked, 1, keepdims=True), 0, keepdims=True)
             factors_ref[2 * hop + n] = jnp.broadcast_to(picked, (8, 128))
     for tile in range(2):
@@ -413,9 +414,9 @@
 COPIES = pltpu.SemaphoreType.DMA((3,))
 
 
-def parts_kernel(factors_ref, own_ref, other_ref, base_ref, one_ref, two_ref, three_ref):
+def parts_kernel(factors_ref, own_ref, other_ref, base_ref, one_ref, three_ref):
     own, other = own_ref[...], other_ref[...]
-    for hop, target in enumerate((base_ref, one_ref, two_ref, three_ref)):
+    for hop, target in ((0, base_ref), (1, one_ref), (3, three_ref)):
         target[...] = factors_ref[2 * hop] * own + factors_ref[2 * hop + 1] * other
 
 
@@ -423,8 +424,12 @@
     out_ref[...] = own_ref[...]
 
 
-def total_kernel(base_ref, one_ref, two_ref, three_ref, out_ref):
-    out_ref[...] = (base_ref[...] + one_ref[...]) + (two_ref[...] + three_ref[...])
+def most_kernel(factors_ref, base_ref, one_ref, three_ref, far_ref, out_ref):
+    out_ref[...] = (base_ref[...] + factors_ref[4] * far_ref[...]) + (one_ref[...] + three_ref[...])
+
+
+def total_kernel(factors_ref, most_ref, farsib_ref, out_ref):
+    out_ref[...] = most_ref[...] + factors_ref[5] * farsib_ref[...]
 
 
 def ring(axis, step):
@@ -506,14 +511,16 @@
         "last",
         XY + [PADDED, PADDED1, FIELD2, BOXED, BOXED, PLANES, PLANES, COPIES],
     )
+    far = lax.ppermute(fourth, "band", meet("band", 4))
     other = lax.ppermute(fourth, "band", meet("band", 1))
     field = shape(24, 8, 128)
-    base, one, two, three = call(
-        parts_kernel, [field] * 4, [VMEM] * 3, (factors, fourth, other), "parts"
-    )
-    arrived = [lax.ppermute(v, "band", meet("band", 2 * hop)) for hop, v in ((2, two), (1, one), (3, three))]
-    (filtered,) = call(store_kernel, [field], [VMEM], (fourth,), "store")
-    (rotated,) = call(total_kernel, [field], [VMEM] * 4, (base, *arrived), "total")
+    base, one, three = call(parts_kernel, [field] * 3, [VMEM] * 3, (factors, fourth, other), "parts")
+    one = lax.ppermute(one, "band", meet("band", 2))
+    three = lax.ppermute(three, "band", meet("band", 6))
+    farsib = lax.ppermute(far, "band", meet("band", 1))
+    (filtered,) = call(store_kernel, [field], [VMEM], (fourth,), "store", flops=0, moved=0)
+    (most,) = call(most_kernel, [field], [VMEM] * 5, (factors, base, one, three, far), "most")
+    (rotated,) = call(total_kernel, [field], [VMEM] * 3, (factors, most, farsib), "total")
     return (filtered.reshape(orbitals.shape), rotated.reshape(orbitals.shape))
 
 

time: 48.4 us -> 47.3 us (0.977)
  waiting for transfers between devices: 13.9 us -> 11.8 us
  starting transfers between devices: 20.2 us -> 21.5 us
    ppermute x3 -> x4, starting transfers between devices: 3.78 us -> 5.1 us  [the longest x1 2.93 us: shards(): far = lax.ppermute(fourth, 'band', meet('band', 4))]
    ppermute x3 -> x4, waiting for transfers between devices: 3.65 us -> 2.52 us  [the longest x1 1.59 us: shards(): far = lax.ppermute(fourth, 'band', meet('band', 4))]
    ppermute x1, waiting for transfers between devices: 0.94 us -> 0.01 us  [shards(): other = lax.ppermute(fourth, 'band', meet('band', 1))]
    pallas_call x8 -> x9, Pallas kernels: 12.5 us -> 12.5 us  [call(): pl.pallas_call(kernel, out_shape=outs, in_specs=ins, out_specs=out_specs...]
  transfers between devices with their start and end apart: 10 -> 11, of which waited for: 5 -> 4; matrix products, arithmetic and copies ran while one was open for 0% -> 0% of each run, Pallas kernels for 9% -> 9%
where the time goes in v5:
time: 47.3 us; the launch traced here: 47.2 us
  starting transfers between devices  21.5 us (45%)
  Pallas kernels  12.5 us (26%)
  waiting for transfers between devices  11.8 us (25%)
  between operations  1.37 us (3%)
    pallas_call x9, Pallas kernels, call(): pl.pallas_call(kernel, out_shape=outs, in_specs=ins, out_specs=out_specs...  12.5 us
    ppermute x1, waiting for transfers between devices, shards(): low = lax.ppermute(up, 'dom', ring('dom', 1))  6.89 us
    ppermute x1, starting transfers between devices, shards(): high = lax.ppermute(down, 'dom', ring('dom', -1))  6.65 us
    ppermute x1, starting transfers between devices, shards(): high_y = lax.ppermute(second, 'dom', ring('dom', -1))  4.94 us
    ppermute x1, starting transfers between devices, shards(): far = lax.ppermute(fourth, 'band', meet('band', 4))  2.93 us
    ppermute x1, waiting for transfers between devices, shards(): low_y = lax.ppermute(second, 'dom', ring('dom', 1))  2.39 us
    ppermute x1, starting transfers between devices, shards(): low = lax.ppermute(up, 'dom', ring('dom', 1))  2.12 us
    ppermute x1, waiting for transfers between devices, shards(): far = lax.ppermute(fourth, 'band', meet('band', 4))  1.59 us
  transfers between devices with their start and end apart: 11, of which 4 were waited for; matrix products, arithmetic and copies ran while one was open for 0% of the time, Pallas kernels for 9%

profile of v5, /device:TPU:1, one launch (start us, length us, event | category | flops | bytes accessed | tf_op | source)
XLA Modules:
  0.0 47.2 jit_solution(10507815008417540445)
XLA Ops:
  1.3 1.5 %pack.1 = (f32[88,8,128]{2,1,0:T(8,128)S(1)}, f32[88,8,128]{2,1,0:T(8,128)S(1)}, f32[24,8,128]{2,1,0:T(8,128)S(1)}, f32[96,8,128]{2,1,0:T(8,128)S(1)}) custom-call(f32[24,8,128]{2,1,0:T(8,128)} %bitcast.8, f32[24,8,128]{2,1,0:T(8,128)} %bitcast.9, f32[32,8,384]{2,1,0:T(8,128)} %proj_hbm.1, f32[8,32]{1,0:T(8,128)} %bitcast.10, s32[3,32]{1,0:T(4,128)} %bitcast.11, ...), custom_call_target="tpu_custom_call" | custom-call | flops 1000000 | bytes 2000000 | tf_op jit(solution)/shard_map/pack/pallas_call | solution.py:41
  2.8 0.0 copy-start
  2.8 2.1 %collective-permute-start.1 = (f32[88,8,128]{2,1,0:T(8,128)S(1)}, f32[88,8,128]{2,1,0:T(8,128)S(1)}, u32[]{:S(2)}, u32[]{:S(2)}) collective-permute-start(f32[88,8,128]{2,1,0:T(8,128)S(1)} %get-tuple-element.24), channel_id=1, source_target_pairs={{0,8},{8,16},{16,24},{24,32},{32,40},{40,48},{48,56},{56,64},{64,7... | collective-permute-start | bytes 1081352 | tf_op jit(solution)/shard_map/ppermute | solution.py:461
  4.9 6.6 %collective-permute-start = (f32[88,8,128]{2,1,0:T(8,128)S(1)}, f32[88,8,128]{2,1,0:T(8,128)S(1)}, u32[]{:S(2)}, u32[]{:S(2)}) collective-permute-start(f32[88,8,128]{2,1,0:T(8,128)S(1)} %get-tuple-element.23.up_ref), channel_id=1, source_target_pairs={{0,248},{8,0},{16,8},{24,16},{32,24},{40,32},{48,40},{56,48},{64,5... | collective-permute-start | bytes 1081352 | tf_op jit(solution)/shard_map/ppermute | solution.py:462
  11.6 1.1 %prepare.1 = (f32[2,48,8,128]{3,2,1,0:T(8,128)S(1)}, bf16[384,128]{1,0:T(8,128)(2,1)S(1)}, bf16[256,256]{1,0:T(8,128)(2,1)S(1)}, bf16[256,256]{1,0:T(8,128)(2,1)...) custom-call(f32[96,8,128]{2,1,0:T(8,128)S(1)} %get-tuple-element.26.proj_ref, ...), custom_call_target="tpu_custom_call" | custom-call | flops 1000000 | bytes 2000000 | tf_op jit(solution)/shard_map/prepare/pallas_call | solution.py:41
  12.7 6.9 %collective-permute-done.1.low_ref = f32[88,8,128]{2,1,0:T(8,128)S(1)} collective-permute-done((f32[88,8,128]{2,1,0:T(8,128)S(1)}, f32[88,8,128]{2,1,0:T(8,128)S(1)}, u32[]{:S(2)}, u32[]{:S(2)}) %collective-permute-start.1) | collective-permute-done | bytes 360480 | tf_op jit(solution)/shard_map/ppermute | solution.py:461
  19.6 1.2 %collective-permute-start.3 = (f32[88,8,128]{2,1,0:T(8,128)S(1)}, f32[88,8,128]{2,1,0:T(8,128)S(1)}, u32[]{:S(2)}, u32[]{:S(2)}) collective-permute-start(f32[88,8,128]{2,1,0:T(8,128)S(1)} %collective-permute-done.1.low_ref), channel_id=1, source_target_pairs={{0,1},{1,0},{2,3},{3,2},{4,5},{5,4},{6,7},{7,6},{8,9},{9,8},{10,11... | collective-permute-start | bytes 1081352 | tf_op jit(solution)/shard_map/ppermute | solution.py:479
  20.9 0.0 collective-permute-done.high_ref
  20.9 0.0 collective-permute-start.2
  20.9 2.6 %head.1 = (f32[2,48,8,128]{3,2,1,0:T(8,128)S(1)}, f32[2,6,2,8,128]{4,3,2,1,0:T(8,128)S(1)}, f32[24,16,128]{2,1,0:T(8,128)S(1)}, bf16[2,256,256]{2,1,0:T(8,128)(2,1)S(1)}, bf16[2,512,128]{2,1,0:T(8,128)(2,1)S(1)}) custom-call(f32[88,8,128]{2,1,0:T(8,128)S(1)} %get-tuple-element.23.up_ref, f32[88,8,128]{2,1,0:T(8,128)S(1)} %collective-permute-done.high_ref, ...), custom_call_target="tpu_custom_call" | custom-call | flops 10000000000 | bytes 2000000 | tf_op jit(solution)/shard_map/head/pallas_call | solution.py:41
  23.5 3.1 %tail.1 = (f32[24,8,128]{2,1,0:T(8,128)S(1)}, f32[24,16,128]{2,1,0:T(8,128)S(1)}, f32[2,2,48,8,128]{4,3,2,1,0:T(8,128)S(1)}) custom-call(f32[88,8,128]{2,1,0:T(8,128)S(1)} %get-tuple-element.23.up_ref, f32[88,8,128]{2,1,0:T(8,128)S(1)} %collective-permute-done.high_ref, f32[88,8,128]{2,1,0:T(8,128)S(1)} %collective-permute-done.1.low_ref, ...), custom_call_target="tpu_custom_call" | custom-call | flops 1000000 | bytes 2000000 | tf_op jit(solution)/shard_map/tail/pallas_call | solution.py:41
  26.5 0.1 collective-permute-start.5
  26.6 4.9 %collective-permute-start.4 = (f32[24,8,128]{2,1,0:T(8,128)S(1)}, f32[24,8,128]{2,1,0:T(8,128)S(1)}, u32[]{:S(2)}, u32[]{:S(2)}) collective-permute-start(f32[24,8,128]{2,1,0:T(8,128)S(1)} %get-tuple-element.39.mid_ref), channel_id=1, source_target_pairs={{0,248},{8,0},{16,8},{24,16},{32,24},{40,32},{48,40},{56,48},{64,5... | collective-permute-start | bytes 294920 | tf_op jit(solution)/shard_map/ppermute | solution.py:505
  31.6 2.4 %collective-permute-done.5.lowy_ref = f32[24,8,128]{2,1,0:T(8,128)S(1)} collective-permute-done((f32[24,8,128]{2,1,0:T(8,128)S(1)}, f32[24,8,128]{2,1,0:T(8,128)S(1)}, u32[]{:S(2)}, u32[]{:S(2)}) %collective-permute-start.5) | collective-permute-done | bytes 98336 | tf_op jit(solution)/shard_map/ppermute | solution.py:504
  34.0 2.8 %last.1.own_ref = f32[24,8,128]{2,1,0:T(8,128)S(1)} custom-call(f32[88,8,128]{2,1,0:T(8,128)S(1)} %get-tuple-element.23.up_ref, f32[88,8,128]{2,1,0:T(8,128)S(1)} %collective-permute-done.high_ref, f32[88,8,128]{2,1,0:T(8,128)S(1)} %collective-permute-done.1.low_ref, f32[24,8,128]{2,1,0:T(8,128)S(1)} %get-tuple-element.25.pot_ref, ...), custom_call_target="tpu_custom_call" | custom-call | flops 1000000 | bytes 2000000 | tf_op jit(solution)/shard_map/last/pallas_call | solution.py:41
  36.8 1.4 %collective-permute-start.6 = (f32[24,8,128]{2,1,0:T(8,128)S(1)}, f32[24,8,128]{2,1,0:T(8,128)S(1)}, u32[]{:S(2)}, u32[]{:S(2)}) collective-permute-start(f32[24,8,128]{2,1,0:T(8,128)S(1)} %last.1.own_ref), channel_id=1, source_target_pairs={{0,1},{1,0},{2,3},{3,2},{4,5},{5,4},{6,7},{7,6},{8,9},{9,8},{10,11... | collective-permute-start | bytes 294920 | tf_op jit(solution)/shard_map/ppermute | solution.py:515
  38.1 2.9 %collective-permute-start.9 = (f32[24,8,128]{2,1,0:T(8,128)S(1)}, f32[24,8,128]{2,1,0:T(8,128)S(1)}, u32[]{:S(2)}, u32[]{:S(2)}) collective-permute-start(f32[24,8,128]{2,1,0:T(8,128)S(1)} %last.1.own_ref), channel_id=1, source_target_pairs={{0,4},{1,5},{2,6},{3,7},{4,0},{5,1},{6,2},{7,3},{8,12},{9,13},{10,... | collective-permute-start | bytes 294920 | tf_op jit(solution)/shard_map/ppermute | solution.py:514
  41.1 0.5 %collective-permute-start.7 = (f32[24,8,128]{2,1,0:T(8,128)S(1)}, f32[24,8,128]{2,1,0:T(8,128)S(1)}, u32[]{:S(2)}, u32[]{:S(2)}) collective-permute-start(f32[24,8,128]{2,1,0:T(8,128)S(1)} %get-tuple-element.42), channel_id=1, source_target_pairs={{0,2},{1,3},{2,0},{3,1},{4,6},{5,7},{6,4},{7,5},{8,10},{9,11},{10,... | collective-permute-start | bytes 294920 | tf_op jit(solution)/shard_map/ppermute | solution.py:518
  41.6 0.8 %collective-permute-start.8 = (f32[24,8,128]{2,1,0:T(8,128)S(1)}, f32[24,8,128]{2,1,0:T(8,128)S(1)}, u32[]{:S(2)}, u32[]{:S(2)}) collective-permute-start(f32[24,8,128]{2,1,0:T(8,128)S(1)} %get-tuple-element.43), channel_id=1, source_target_pairs={{0,6},{1,7},{2,4},{3,5},{4,2},{5,3},{6,0},{7,1},{8,14},{9,15},{10,... | collective-permute-start | bytes 294920 | tf_op jit(solution)/shard_map/ppermute | solution.py:519
  42.4 1.6 %collective-permute-done.9.far_ref = f32[24,8,128]{2,1,0:T(8,128)S(1)} collective-permute-done((f32[24,8,128]{2,1,0:T(8,128)S(1)}, f32[24,8,128]{2,1,0:T(8,128)S(1)}, u32[]{:S(2)}, u32[]{:S(2)}) %collective-permute-start.9) | collective-permute-done | bytes 98336 | tf_op jit(solution)/shard_map/ppermute | solution.py:514
  44.0 0.9 %collective-permute-start.10 = (f32[24,8,128]{2,1,0:T(8,128)S(1)}, f32[24,8,128]{2,1,0:T(8,128)S(1)}, u32[]{:S(2)}, u32[]{:S(2)}) collective-permute-start(f32[24,8,128]{2,1,0:T(8,128)S(1)} %collective-permute-done.9.far_ref), channel_id=1, source_target_pairs={{0,1},{1,0},{2,3},{3,2},{4,5},{5,4},{6,7},{7,6},{8,9},{9,8},{10,11... | collective-permute-start | bytes 294920 | tf_op jit(solution)/shard_map/ppermute | solution.py:520
  44.9 0.6 %store.1 = f32[24,8,128]{2,1,0:T(8,128)} custom-call(f32[24,8,128]{2,1,0:T(8,128)S(1)} %last.1.own_ref), custom_call_target="tpu_custom_call" | custom-call | tf_op jit(solution)/shard_map/store/pallas_call | solution.py:41
  45.5 0.9 %collective-permute-done.7.one_ref = f32[24,8,128]{2,1,0:T(8,128)S(1)} collective-permute-done((f32[24,8,128]{2,1,0:T(8,128)S(1)}, f32[24,8,128]{2,1,0:T(8,128)S(1)}, u32[]{:S(2)}, u32[]{:S(2)}) %collective-permute-start.7) | collective-permute-done | bytes 98336 | tf_op jit(solution)/shard_map/ppermute | solution.py:518
  46.5 0.7 %total.1 = f32[24,8,128]{2,1,0:T(8,128)} custom-call(f32[8,8,128]{2,1,0:T(8,128)S(1)} %get-tuple-element.40.factors_ref, f32[24,8,128]{2,1,0:T(8,128)S(1)} %most.1.most_ref, f32[24,8,128]{2,1,0:T(8,128)S(1)} %collective-permute-done.10.farsib_ref), custom_call_target="tpu_custom_call" | custom-call | flops 1000000 | bytes 2000000 | tf_op jit(solution)/shard_map/total/pallas_call | solution.py:41
  (9 shorter events, 0.1 us)
Async XLA Ops:
  2.8 8.8 %copy-start = (f32[8,8]{1,0:T(8,128)S(1)}, f32[8,8]{1,0:T(8,128)}, u32[]{:S(2)}) copy-start(f32[8,8]{1,0:T(8,128)} %ritz_ref.1) | copy-start | bytes 772
  2.8 16.8 %collective-permute-start.1 = (f32[88,8,128]{2,1,0:T(8,128)S(1)}, f32[88,8,128]{2,1,0:T(8,128)S(1)}, u32[]{:S(2)}, u32[]{:S(2)}) collective-permute-start(f32[88,8,128]{2,1,0:T(8,128)S(1)} %get-tuple-element.24), channel_id=1, source_target_pairs={{0,8},{8,16},{16,24},{24,32},{32,40},{40,48},{48,56},{56,64},{64,7... | collective-permute-start | bytes 1081352 | tf_op jit(solution)/shard_map/ppermute | solution.py:461
  4.9 15.9 %collective-permute-start = (f32[88,8,128]{2,1,0:T(8,128)S(1)}, f32[88,8,128]{2,1,0:T(8,128)S(1)}, u32[]{:S(2)}, u32[]{:S(2)}) collective-permute-start(f32[88,8,128]{2,1,0:T(8,128)S(1)} %get-tuple-element.23.up_ref), channel_id=1, source_target_pairs={{0,248},{8,0},{16,8},{24,16},{32,24},{40,32},{48,40},{56,48},{64,5... | collective-permute-start | bytes 1081352 | tf_op jit(solution)/shard_map/ppermute | solution.py:462
  19.6 3.8 %collective-permute-start.3 = (f32[88,8,128]{2,1,0:T(8,128)S(1)}, f32[88,8,128]{2,1,0:T(8,128)S(1)}, u32[]{:S(2)}, u32[]{:S(2)}) collective-permute-start(f32[88,8,128]{2,1,0:T(8,128)S(1)} %collective-permute-done.1.low_ref), channel_id=1, source_target_pairs={{0,1},{1,0},{2,3},{3,2},{4,5},{5,4},{6,7},{7,6},{8,9},{9,8},{10,11... | collective-permute-start | bytes 1081352 | tf_op jit(solution)/shard_map/ppermute | solution.py:479
  20.9 2.6 %collective-permute-start.2 = (f32[88,8,128]{2,1,0:T(8,128)S(1)}, f32[88,8,128]{2,1,0:T(8,128)S(1)}, u32[]{:S(2)}, u32[]{:S(2)}) collective-permute-start(f32[88,8,128]{2,1,0:T(8,128)S(1)} %collective-permute-done.high_ref), channel_id=1, source_target_pairs={{0,1},{1,0},{2,3},{3,2},{4,5},{5,4},{6,7},{7,6},{8,9},{9,8},{10,11... | collective-permute-start | bytes 1081352 | tf_op jit(solution)/shard_map/ppermute | solution.py:478
  26.5 7.4 %collective-permute-start.5 = (f32[24,8,128]{2,1,0:T(8,128)S(1)}, f32[24,8,128]{2,1,0:T(8,128)S(1)}, u32[]{:S(2)}, u32[]{:S(2)}) collective-permute-start(f32[24,8,128]{2,1,0:T(8,128)S(1)} %get-tuple-element.39.mid_ref), channel_id=1, source_target_pairs={{0,8},{8,16},{16,24},{24,32},{32,40},{40,48},{48,56},{56,64},{64,7... | collective-permute-start | bytes 294920 | tf_op jit(solution)/shard_map/ppermute | solution.py:504
  26.6 7.3 %collective-permute-start.4 = (f32[24,8,128]{2,1,0:T(8,128)S(1)}, f32[24,8,128]{2,1,0:T(8,128)S(1)}, u32[]{:S(2)}, u32[]{:S(2)}) collective-permute-start(f32[24,8,128]{2,1,0:T(8,128)S(1)} %get-tuple-element.39.mid_ref), channel_id=1, source_target_pairs={{0,248},{8,0},{16,8},{24,16},{32,24},{40,32},{48,40},{56,48},{64,5... | collective-permute-start | bytes 294920 | tf_op jit(solution)/shard_map/ppermute | solution.py:505
  36.8 4.3 %collective-permute-start.6 = (f32[24,8,128]{2,1,0:T(8,128)S(1)}, f32[24,8,128]{2,1,0:T(8,128)S(1)}, u32[]{:S(2)}, u32[]{:S(2)}) collective-permute-start(f32[24,8,128]{2,1,0:T(8,128)S(1)} %last.1.own_ref), channel_id=1, source_target_pairs={{0,1},{1,0},{2,3},{3,2},{4,5},{5,4},{6,7},{7,6},{8,9},{9,8},{10,11... | collective-permute-start | bytes 294920 | tf_op jit(solution)/shard_map/ppermute | solution.py:515
  38.1 5.9 %collective-permute-start.9 = (f32[24,8,128]{2,1,0:T(8,128)S(1)}, f32[24,8,128]{2,1,0:T(8,128)S(1)}, u32[]{:S(2)}, u32[]{:S(2)}) collective-permute-start(f32[24,8,128]{2,1,0:T(8,128)S(1)} %last.1.own_ref), channel_id=1, source_target_pairs={{0,4},{1,5},{2,6},{3,7},{4,0},{5,1},{6,2},{7,3},{8,12},{9,13},{10,... | collective-permute-start | bytes 294920 | tf_op jit(solution)/shard_map/ppermute | solution.py:514
  41.1 5.3 %collective-permute-start.7 = (f32[24,8,128]{2,1,0:T(8,128)S(1)}, f32[24,8,128]{2,1,0:T(8,128)S(1)}, u32[]{:S(2)}, u32[]{:S(2)}) collective-permute-start(f32[24,8,128]{2,1,0:T(8,128)S(1)} %get-tuple-element.42), channel_id=1, source_target_pairs={{0,2},{1,3},{2,0},{3,1},{4,6},{5,7},{6,4},{7,5},{8,10},{9,11},{10,... | collective-permute-start | bytes 294920 | tf_op jit(solution)/shard_map/ppermute | solution.py:518
  41.6 4.9 %collective-permute-start.8 = (f32[24,8,128]{2,1,0:T(8,128)S(1)}, f32[24,8,128]{2,1,0:T(8,128)S(1)}, u32[]{:S(2)}, u32[]{:S(2)}) collective-permute-start(f32[24,8,128]{2,1,0:T(8,128)S(1)} %get-tuple-element.43), channel_id=1, source_target_pairs={{0,6},{1,7},{2,4},{3,5},{4,2},{5,3},{6,0},{7,1},{8,14},{9,15},{10,... | collective-permute-start | bytes 294920 | tf_op jit(solution)/shard_map/ppermute | solution.py:519
  44.0 2.5 %collective-permute-start.10 = (f32[24,8,128]{2,1,0:T(8,128)S(1)}, f32[24,8,128]{2,1,0:T(8,128)S(1)}, u32[]{:S(2)}, u32[]{:S(2)}) collective-permute-start(f32[24,8,128]{2,1,0:T(8,128)S(1)} %collective-permute-done.9.far_ref), channel_id=1, source_target_pairs={{0,1},{1,0},{2,3},{3,2},{4,5},{5,4},{6,7},{7,6},{8,9},{9,8},{10,11... | collective-permute-start | bytes 294920 | tf_op jit(solution)/shard_map/ppermute | solution.py:520

commit v6 on v5

--- a/solution.py
+++ b/solution.py
@@ -64,53 +64,7 @@
     return slice(128 * tile, 128 * tile + 128)
 
 
-def pack_kernel(y_hbm, pot_hbm, proj_hbm, gamma_hbm, pos_hbm, count_ref,
-                up_ref, down_ref, pot_ref, proj_ref, gamma_ref, pos_ref, sems):
-    core = lax.axis_index("band") % 2
-    first = 16 * core
-    copies = [
-        pltpu.make_async_copy(gamma_hbm, gamma_ref, sems.at[0]),
-        pltpu.make_async_copy(pos_hbm, pos_ref, sems.at[1]),
-    ]
-    moves = [
-        (pot_hbm, pot_ref),
-        (pot_hbm.at[pl.ds(12, 12)], up_ref.at[pl.ds(TILE_POT, 12)]),
-        (pot_hbm.at[pl.ds(0, 12)], down_ref.at[pl.ds(TILE_POT, 12)]),
-    ]
-    for out in (up_ref, down_ref):
-        moves.append((y_hbm, out.at[pl.ds(TILE_Y, 24)]))
-        for part in range(3):
-            source = proj_hbm.at[pl.ds(first, 16), pl.ds(0, 8), pl.ds(128 * part, 128)]
-            moves.append((source, out.at[pl.ds(TILE_P + 16 * part, 16)]))
-    for part in range(3):
-        source = proj_hbm.at[pl.ds(0, ATOMS), pl.ds(0, 8), pl.ds(128 * part, 128)]
-        moves.append((source, proj_ref.at[pl.ds(ATOMS * part, ATOMS)]))
-    for n, (source, target) in enumerate(moves):
-        copies.append(pltpu.make_async_copy(source, target, sems.at[2 + n]))
-    for copy in copies:
-        copy.start()
-    copies[0].wait()
-    copies[1].wait()
-    live = lax.broadcasted_iota(jnp.int32, (1, ATOMS), 1) < count_ref[0]
-    weight = jnp.where(live, gamma_ref[...], 0.0)
-    repeat = lax.broadcasted_iota(jnp.int32, (ATOMS, LANES), 1) >> 3
-    repeat = jnp.where(repeat == lax.broadcasted_iota(jnp.int32, (ATOMS, LANES), 0), 1.0, 0.0)
-    corner = pos_ref[...].astype(jnp.float32)
-    spread = lambda v: jnp.dot(v, repeat, preferred_element_type=jnp.float32, precision=lax.Precision.HIGHEST)
-    weight = spread(weight)
-    column = spread(corner)[2:3] + (lax.broadcasted_iota(jnp.int32, (1, LANES), 1) & 7).astype(jnp.float32)
-    column = jnp.where(column >= NZ, column - NZ, column)
-    for out in (up_ref, down_ref):
-        for tile in range(2):
-            out[TILE_META + 2 * tile] = weight[:, half(tile)]
-            out[TILE_META + 2 * tile + 1] = jnp.broadcast_to(column[:, half(tile)], (8, 128))
-        out[TILE_META + 1, ROW_X0 : ROW_X0 + 1, 0:ATOMS] = corner[0:1]
-        out[TILE_META + 1, ROW_Y0 : ROW_Y0 + 1, 0:ATOMS] = corner[1:2]
-    for copy in copies[2:]:
-        copy.wait()
-
-
-def spread_projectors(read, work, table):
+def spread_projectors(read, work, *tables):
     lane = lax.broadcasted_iota(jnp.int32, (8, 128), 1)
     for part in range(3):
         items = [read(part, a) for a in range(16)]
@@ -128,10 +82,60 @@
             work[i, 8 * j : 8 * j + 8, :] = items[g]
     for i in range(BX):
         for l in range(NPROJ):
-            table[l * BX + i] = work.at[i][pl.ds(l, 8, stride=8), :]
-
-
-def prepare_kernel(proj_ref, up_ref, ritz_ref, table_ref, zst_ref, sums_ref, hot_ref, back_ref, factors_ref, work):
+            laid = work.at[i][pl.ds(l, 8, stride=8), :]
+            for table in tables:
+                table[l * BX + i] = laid
+
+
+def pack_kernel(y_hbm, pot_hbm, proj_hbm, gamma_hbm, pos_hbm, count_ref,
+                up_ref, down_ref, pot_ref, rest_ref, gamma_ref, pos_ref, half_ref, work, sems):
+    core = lax.axis_index("band") % 2
+    copies = [
+        pltpu.make_async_copy(gamma_hbm, gamma_ref, sems.at[0]),
+        pltpu.make_async_copy(pos_hbm, pos_ref, sems.at[1]),
+    ]
+    moves = []
+    for first, target in ((16 * core, half_ref), (16 - 16 * core, rest_ref)):
+        for part in range(3):
+            source = proj_hbm.at[pl.ds(first, 16), pl.ds(0, 8), pl.ds(128 * part, 128)]
+            moves.append((source, target.at[pl.ds(16 * part, 16)]))
+    moves.append((pot_hbm, pot_ref))
+    for out, first in ((up_ref, 12), (down_ref, 0)):
+        moves.append((y_hbm, out.at[pl.ds(TILE_Y, 24)]))
+        moves.append((pot_hbm.at[pl.ds(first, 12)], out.at[pl.ds(TILE_POT, 12)]))
+    for n, (source, target) in enumerate(moves):
+        copies.append(pltpu.make_async_copy(source, target, sems.at[2 + n]))
+    for copy in copies:
+        copy.start()
+    copies[0].wait()
+    copies[1].wait()
+    live = lax.broadcasted_iota(jnp.int32, (1, ATOMS), 1) < count_ref[0]
+    weight = jnp.where(live, gamma_ref[...], 0.0)
+    spread = lambda v, m: jnp.dot(v, m, preferred_element_type=jnp.float32, precision=lax.Precision.HIGHEST)
+    atom = lax.broadcasted_iota(jnp.int32, (ATOMS, LANES), 0)
+    lane = lax.broadcasted_iota(jnp.int32, (ATOMS, LANES), 1)
+    repeat = jnp.where((lane >> 3) ^ (16 * core) == atom, 1.0, 0.0)
+    order = jnp.where(lane[:, half(0)] ^ (16 * core) == atom[:, half(0)], 1.0, 0.0)
+    corner = pos_ref[...].astype(jnp.float32)
+    weight = spread(weight, repeat)
+    column = spread(corner, repeat)[2:3] + (lax.broadcasted_iota(jnp.int32, (1, LANES), 1) & 7).astype(jnp.float32)
+    column = jnp.where(column >= NZ, column - NZ, column)
+    corner = spread(corner, order)
+    for out in (up_ref, down_ref):
+        for tile in range(2):
+            out[TILE_META + 2 * tile] = weight[:, half(tile)]
+            out[TILE_META + 2 * tile + 1] = jnp.broadcast_to(column[:, half(tile)], (8, 128))
+        out[TILE_META + 1, ROW_X0 : ROW_X0 + 1, :] = corner[0:1]
+        out[TILE_META + 1, ROW_Y0 : ROW_Y0 + 1, :] = corner[1:2]
+    for copy in copies[2:5]:
+        copy.wait()
+    tables = [out.at[pl.ds(TILE_P, PAIRS)] for out in (up_ref, down_ref)]
+    spread_projectors(lambda part, a: half_ref[16 * part + a], work, *tables)
+    for copy in copies[5:]:
+        copy.wait()
+
+
+def prepare_kernel(rest_ref, up_ref, ritz_ref, table_ref, zst_ref, sums_ref, hot_ref, back_ref, factors_ref, work):
     write_one_hot(up_ref, hot_ref, back_ref)
     band = lax.axis_index("band")
     row = lax.broadcasted_iota(jnp.int32, (8, 8), 0)
@@ -142,9 +146,7 @@
             picked = jnp.where((row == orbital) & (column == to), ritz_ref[...], 0.0)
             picked = jnp.sum(jnp.sum(picked, 1, keepdims=True), 0, keepdims=True)
             factors_ref[2 * hop + n] = jnp.broadcast_to(picked, (8, 128))
-    for tile in range(2):
-        read = lambda part, a: proj_ref[ATOMS * part + 16 * tile + a]
-        spread_projectors(read, work, table_ref.at[tile])
+    spread_projectors(lambda part, a: rest_ref[16 * part + a], work, table_ref)
     apart = lax.broadcasted_iota(jnp.int32, (NZ, NZ), 0) - lax.broadcasted_iota(jnp.int32, (NZ, NZ), 1)
     full = jnp.zeros((NZ, NZ), jnp.float32)
     for reach in range(1, 7):
@@ -224,9 +226,9 @@
     for tile in range(2):
         rows = []
         for l in range(NPROJ):
-            total = values[0][tile] * table[tile, l * BX]
+            total = values[0][tile] * table[tile][l * BX]
             for i in range(1, BX):
-                total = total + values[i][tile] * table[tile, l * BX + i]
+                total = total + values[i][tile] * table[tile][l * BX + i]
             rows.append(jnp.sum(total, 0, keepdims=True))
         coeffs.append(jnp.concatenate(rows, 0))
     both = dot(two_terms(jnp.concatenate(coeffs, 1), 0), sums)
@@ -236,9 +238,9 @@
     for tile in range(2):
         rows = [jnp.broadcast_to(coeffs[l : l + 1, half(tile)], (8, 128)) for l in range(NPROJ)]
         for i in range(BX):
-            total = rows[0] * table[tile, i]
+            total = rows[0] * table[tile][i]
             for l in range(1, NPROJ):
-                total = total + rows[l] * table[tile, l * BX + i]
+                total = total + rows[l] * table[tile][l * BX + i]
             contrib[i][tile] = total
     for a in range(16):
         mine = (lane >> 3) == a
@@ -282,6 +284,11 @@
         ref[...] = jnp.zeros_like(ref)
 
 
+def laid(first, second):
+    rows = pl.ds(TILE_P, PAIRS)
+    return first.at[rows], second if second.shape[0] == PAIRS else second.at[rows]
+
+
 def load_fields(fields, padded, field2):
     for n, value in enumerate(fields):
         fill(padded, 12 * n, value.reshape(CX, NY, NZ))
@@ -289,8 +296,8 @@
 
 
 def head_kernel(up_ref, high_ref, low_ref, pot_ref, table_ref, zst_ref, sums_ref, hot_ref, back_ref,
-                half_ref, values_ref, partial_ref, hots_ref, backs_ref,
-                low_xy, own_xy, high_xy, padded, field2, gathered, placed, local, work, sems):
+                values_ref, partial_ref, hots_ref, backs_ref,
+                low_xy, own_xy, high_xy, padded, field2, gathered, placed, local, sems):
     boxes = Boxes((low_ref, up_ref, high_ref), (low_xy, own_xy, high_xy), sems)
     load_fields([r[TILE_Y : TILE_Y + 24] for r in (low_ref, up_ref, high_ref)], padded, field2)
     clear(placed)
@@ -305,10 +312,8 @@
         laplace = stencil_plane(padded, p + 6) + local[p]
         pot = potential_plane(p, low_ref, pot_ref, high_ref)
         local[p] = (-0.5 * laplace + (pot - CENTER) * padded[p + 6, 8:24, :]) * (1.0 / HALF)
-    for n, source in enumerate((low_ref, high_ref)):
-        spread_projectors(lambda part, a: source[TILE_P + 16 * part + a], work, half_ref.at[n])
     boxes.wait()
-    contributions(1, read_windows(1, gathered, boxes), table_ref, placed, boxes, sums_ref[...])
+    contributions(1, read_windows(1, gathered, boxes), laid(up_ref, table_ref), placed, boxes, sums_ref[...])
     for n, group in enumerate((0, 2)):
         values = read_windows(group, gathered, boxes)
         for i in range(BX):
@@ -337,22 +342,19 @@
 
 
 def tail_kernel(up_ref, high_ref, low_ref, pot_ref, table_ref, zst_ref, sums_ref, hot_ref, back_ref,
-                half_ref, values_ref, partial_ref, hots_ref, backs_ref, highsib_ref, lowsib_ref,
-                out_ref, kept_ref, tables_ref,
-                low_xy, own_xy, high_xy, padded1, field2, gathered, placed, local, nonlocal_, work, sems):
-    core = lax.axis_index("band") % 2
+                values_ref, partial_ref, hots_ref, backs_ref, highsib_ref, lowsib_ref,
+                out_ref, kept_ref,
+                low_xy, own_xy, high_xy, padded1, field2, gathered, placed, local, nonlocal_, sems):
     boxes = Boxes((low_ref, up_ref, high_ref), (low_xy, own_xy, high_xy), sems)
     clear(placed)
     gathered[0][:, 0:6] = jnp.zeros((2, 6, 24, 128), jnp.float32)
-    for n, source in enumerate((lowsib_ref, highsib_ref)):
-        spread_projectors(lambda part, a: source[TILE_P + 16 * part + a], work, tables_ref.at[n, 1 - core])
-        tables_ref[n, core] = half_ref[n]
+    tables = (laid(low_ref, lowsib_ref), laid(up_ref, table_ref), laid(high_ref, highsib_ref))
     hots, backs = (hots_ref.at[0], hot_ref), (backs_ref.at[0], back_ref, backs_ref.at[1])
     boxes.wait()
     sums = sums_ref[...]
     for n, group in enumerate((0, 2)):
         values = [[values_ref[n, i, tile] for tile in range(2)] for i in range(BX)]
-        contributions(group, values, tables_ref.at[n], placed, boxes, sums)
+        contributions(group, values, tables[group], placed, boxes, sums)
     nonlocal_[0:11] = spread_group(0, 6, 11, placed, backs[0])
     nonlocal_[11:18] = jnp.zeros((7, NY, NZ), jnp.float32)
     nonlocal_[18:24] = spread_group(2, 0, 6, placed, backs[2])
@@ -361,14 +363,13 @@
         kept_ref[p] = updated
         fill(padded1, p, updated[None])
         field2[16 * p : 16 * p + 16, :] = two_terms(updated, 1)
-    tables = (tables_ref.at[0], table_ref)
     for p, value in second_step(boxes, hots, backs, padded1, field2, gathered, placed, local, nonlocal_, pot_ref, tables,
                                 zst_ref, sums):
         out_ref[2 * p : 2 * p + 2] = (value - up_ref[TILE_Y + 2 * p : TILE_Y + 2 * p + 2].reshape(NY, NZ)).reshape(2, 8, 128)
 
 
 def last_kernel(up_ref, high_ref, low_ref, pot_ref, table_ref, zst_ref, sums_ref, hot_ref, back_ref,
-                kept_ref, tables_ref, hots_ref, backs_ref,
+                kept_ref, hots_ref, backs_ref, highsib_ref, lowsib_ref,
                 mid_ref, highy_ref, lowy_ref,
                 out_ref,
                 low_xy, own_xy, high_xy, padded, padded1, field2, gathered, placed, local, nonlocal_, sems):
@@ -378,7 +379,7 @@
     gathered[2][:, 12:SPAN] = jnp.zeros((2, SPAN - 12, 24, 128), jnp.float32)
     hots, backs = (hots_ref.at[0], hot_ref, hots_ref.at[1]), (backs_ref.at[0], back_ref, backs_ref.at[1])
     sums = sums_ref[...]
-    tables = (tables_ref.at[0], table_ref, tables_ref.at[1])
+    tables = (laid(low_ref, lowsib_ref), laid(up_ref, table_ref), laid(high_ref, highsib_ref))
     for group, planes in ((0, SPAN), (1, SPAN), (2, 12)):
         gather_columns(group, field2, 12 * group, planes, 0, gathered, hots[group])
     local[...] = along_z(field2, slice(96, 480), zst_ref).reshape(24, NY, NZ)
@@ -443,9 +444,9 @@
 
 def shards(orbitals, potential, atom_pos, atom_count, projectors, gammas, ritz):
     stay = lambda v: pltpu.with_memory_space_constraint(v, pltpu.HBM)
-    up, down, pot, proj = call(
+    up, down, pot, rest = call(
         pack_kernel,
-        [shape(TILES, 8, 128), shape(TILES, 8, 128), shape(24, 8, 128), shape(3 * ATOMS, 8, 128)],
+        [shape(TILES, 8, 128), shape(TILES, 8, 128), shape(24, 8, 128), shape(PAIRS, 8, 128)],
         [HBM] * 5 + [SMEM],
         (
             stay(orbitals.reshape(24, 8, 128)),
@@ -456,14 +457,20 @@
             atom_count,
         ),
         "pack",
-        [pltpu.VMEM((NPROJ, ATOMS), jnp.float32), pltpu.VMEM((3, ATOMS), jnp.int32), pltpu.SemaphoreType.DMA((16,))],
+        [
+            pltpu.VMEM((NPROJ, ATOMS), jnp.float32),
+            pltpu.VMEM((3, ATOMS), jnp.int32),
+            pltpu.VMEM((PAIRS, 8, 128), jnp.float32),
+            WORK,
+            pltpu.SemaphoreType.DMA((13,)),
+        ],
     )
     low = lax.ppermute(up, "dom", ring("dom", 1))
     high = lax.ppermute(down, "dom", ring("dom", -1))
     table, zst, sums, hot, back, factors = call(
         prepare_kernel,
         [
-            shape(2, PAIRS, 8, 128),
+            shape(PAIRS, 8, 128),
             shape(384, NZ, dtype=jnp.bfloat16),
             shape(LANES, LANES, dtype=jnp.bfloat16),
             shape(2 * NZ, LANES, dtype=jnp.bfloat16),
@@ -471,17 +478,16 @@
             shape(8, 8, 128),
         ],
         [VMEM] * 3,
-        (proj, down, ritz),
+        (rest, down, ritz),
         "prepare",
         [WORK],
     )
     highsib = lax.ppermute(high, "band", meet("band", 1))
     lowsib = lax.ppermute(low, "band", meet("band", 1))
     common = (down, high, low, pot, table, zst, sums, hot, back)
-    halves, values, partial, hots, backs = call(
+    values, partial, hots, backs = call(
         head_kernel,
         [
-            shape(2, PAIRS, 8, 128),
             shape(2, BX, 2, 8, 128),
             shape(24, NY, NZ),
             shape(2, 2 * NZ, LANES, dtype=jnp.bfloat16),
@@ -490,24 +496,24 @@
         [VMEM] * 9,
         common,
         "head",
-        XY + [PADDED, FIELD2, BOXED, BOXED, PLANES, WORK, COPIES],
+        XY + [PADDED, FIELD2, BOXED, BOXED, PLANES, COPIES],
         flops=10_000_000_000,
     )
-    second, first, tables = call(
+    second, first = call(
         tail_kernel,
-        [shape(24, 8, 128), shape(24, NY, NZ), shape(2, 2, PAIRS, 8, 128)],
-        [VMEM] * 16,
-        common + (halves, values, partial, hots, backs, highsib, lowsib),
+        [shape(24, 8, 128), shape(24, NY, NZ)],
+        [VMEM] * 15,
+        common + (values, partial, hots, backs, highsib, lowsib),
         "tail",
-        XY + [PADDED1, FIELD2, BOXED, BOXED, PLANES, PLANES, WORK, COPIES],
+        XY + [PADDED1, FIELD2, BOXED, BOXED, PLANES, PLANES, COPIES],
     )
     low_y = lax.ppermute(second, "dom", ring("dom", 1))
     high_y = lax.ppermute(second, "dom", ring("dom", -1))
     (fourth,) = call(
         last_kernel,
         [shape(24, 8, 128)],
-        [VMEM] * 16,
-        common + (first, tables, hots, backs, second, high_y, low_y),
+        [VMEM] * 17,
+        common + (first, hots, backs, highsib, lowsib, second, high_y, low_y),
         "last",
         XY + [PADDED, PADDED1, FIELD2, BOXED, BOXED, PLANES, PLANES, COPIES],
     )

time: 47.3 us -> 45.5 us (0.962)
  Pallas kernels: 12.5 us -> 10.1 us
  waiting for transfers between devices: 11.8 us -> 12.4 us
    pallas_call x9, Pallas kernels: 12.5 us -> 10.1 us  [call(): pl.pallas_call(kernel, out_shape=outs, in_specs=ins, out_specs=out_specs...]
    ppermute x1, waiting for transfers between devices: 6.89 us -> 7.49 us  [shards(): low = lax.ppermute(up, 'dom', ring('dom', 1))]
  transfers between devices with their start and end apart: 11 -> 11, of which waited for: 4 -> 4; matrix products, arithmetic and copies ran while one was open for 0% -> 0% of each run, Pallas kernels for 9% -> 7%
where the time goes in v6:
time: 45.5 us; the launch traced here: 45.4 us
  starting transfers between devices  21.5 us (47%)
  waiting for transfers between devices  12.4 us (27%)
  Pallas kernels  10.1 us (22%)
  between operations  1.37 us (3%)
    pallas_call x9, Pallas kernels, call(): pl.pallas_call(kernel, out_shape=outs, in_specs=ins, out_specs=out_specs...  10.1 us
    ppermute x1, waiting for transfers between devices, shards(): low = lax.ppermute(up, 'dom', ring('dom', 1))  7.49 us
    ppermute x1, starting transfers between devices, shards(): high = lax.ppermute(down, 'dom', ring('dom', -1))  6.65 us
    ppermute x1, starting transfers between devices, shards(): high_y = lax.ppermute(second, 'dom', ring('dom', -1))  4.94 us
    ppermute x1, starting transfers between devices, shards(): far = lax.ppermute(fourth, 'band', meet('band', 4))  2.93 us
    ppermute x1, waiting for transfers between devices, shards(): low_y = lax.ppermute(second, 'dom', ring('dom', 1))  2.4 us
    ppermute x1, starting transfers between devices, shards(): low = lax.ppermute(up, 'dom', ring('dom', 1))  2.12 us
    ppermute x1, waiting for transfers between devices, shards(): far = lax.ppermute(fourth, 'band', meet('band', 4))  1.59 us
  transfers between devices with their start and end apart: 11, of which 4 were waited for; matrix products, arithmetic and copies ran while one was open for 0% of the time, Pallas kernels for 7%

profile of v6, /device:TPU:1, one launch (start us, length us, event | category | flops | bytes accessed | tf_op | source)
XLA Modules:
  0.0 45.4 jit_solution(3804503339309576767)
XLA Ops:
  1.3 1.4 %pack.1 = (f32[88,8,128]{2,1,0:T(8,128)S(1)}, f32[88,8,128]{2,1,0:T(8,128)S(1)}, f32[24,8,128]{2,1,0:T(8,128)S(1)}, f32[48,8,128]{2,1,0:T(8,128)S(1)}) custom-call(f32[24,8,128]{2,1,0:T(8,128)} %bitcast.8, f32[24,8,128]{2,1,0:T(8,128)} %bitcast.9, f32[32,8,384]{2,1,0:T(8,128)} %proj_hbm.1, f32[8,32]{1,0:T(8,128)} %bitcast.10, s32[3,32]{1,0:T(4,128)} %bitcast.11, ...), custom_call_target="tpu_custom_call" | custom-call | flops 1000000 | bytes 2000000 | tf_op jit(solution)/shard_map/pack/pallas_call | solution.py:41
  2.7 0.0 copy-start
  2.7 2.1 %collective-permute-start.1 = (f32[88,8,128]{2,1,0:T(8,128)S(1)}, f32[88,8,128]{2,1,0:T(8,128)S(1)}, u32[]{:S(2)}, u32[]{:S(2)}) collective-permute-start(f32[88,8,128]{2,1,0:T(8,128)S(1)} %get-tuple-element.22), channel_id=1, source_target_pairs={{0,8},{8,16},{16,24},{24,32},{32,40},{40,48},{48,56},{56,64},{64,7... | collective-permute-start | bytes 1081352 | tf_op jit(solution)/shard_map/ppermute | solution.py:468
  4.8 6.6 %collective-permute-start = (f32[88,8,128]{2,1,0:T(8,128)S(1)}, f32[88,8,128]{2,1,0:T(8,128)S(1)}, u32[]{:S(2)}, u32[]{:S(2)}) collective-permute-start(f32[88,8,128]{2,1,0:T(8,128)S(1)} %get-tuple-element.21.up_ref), channel_id=1, source_target_pairs={{0,248},{8,0},{16,8},{24,16},{32,24},{40,32},{48,40},{56,48},{64,5... | collective-permute-start | bytes 1081352 | tf_op jit(solution)/shard_map/ppermute | solution.py:469
  11.5 0.5 %prepare.1 = (f32[48,8,128]{2,1,0:T(8,128)S(1)}, bf16[384,128]{1,0:T(8,128)(2,1)S(1)}, bf16[256,256]{1,0:T(8,128)(2,1)S(1)}, bf16[256,256]{1,0:T(8,128)(2,1)S(1)...) custom-call(f32[48,8,128]{2,1,0:T(8,128)S(1)} %get-tuple-element.24.rest_ref, ...), custom_call_target="tpu_custom_call" | custom-call | flops 1000000 | bytes 2000000 | tf_op jit(solution)/shard_map/prepare/pallas_call | solution.py:41
  12.0 7.5 %collective-permute-done.1.low_ref = f32[88,8,128]{2,1,0:T(8,128)S(1)} collective-permute-done((f32[88,8,128]{2,1,0:T(8,128)S(1)}, f32[88,8,128]{2,1,0:T(8,128)S(1)}, u32[]{:S(2)}, u32[]{:S(2)}) %collective-permute-start.1) | collective-permute-done | bytes 360480 | tf_op jit(solution)/shard_map/ppermute | solution.py:468
  19.5 1.2 %collective-permute-start.3 = (f32[88,8,128]{2,1,0:T(8,128)S(1)}, f32[88,8,128]{2,1,0:T(8,128)S(1)}, u32[]{:S(2)}, u32[]{:S(2)}) collective-permute-start(f32[88,8,128]{2,1,0:T(8,128)S(1)} %collective-permute-done.1.low_ref), channel_id=1, source_target_pairs={{0,1},{1,0},{2,3},{3,2},{4,5},{5,4},{6,7},{7,6},{8,9},{9,8},{10,11... | collective-permute-start | bytes 1081352 | tf_op jit(solution)/shard_map/ppermute | solution.py:486
  20.8 0.0 collective-permute-done.high_ref
  20.8 0.0 collective-permute-start.2
  20.8 1.9 %head.1 = (f32[2,6,2,8,128]{4,3,2,1,0:T(8,128)S(1)}, f32[24,16,128]{2,1,0:T(8,128)S(1)}, bf16[2,256,256]{2,1,0:T(8,128)(2,1)S(1)}, bf16[2,512,128]{2,1,0:T(8,128)(2,1)S(1)}) custom-call(f32[88,8,128]{2,1,0:T(8,128)S(1)} %get-tuple-element.21.up_ref, f32[88,8,128]{2,1,0:T(8,128)S(1)} %collective-permute-done.high_ref, ...), custom_call_target="tpu_custom_call" | custom-call | flops 10000000000 | bytes 2000000 | tf_op jit(solution)/shard_map/head/pallas_call | solution.py:41
  22.7 2.2 %tail.1 = (f32[24,8,128]{2,1,0:T(8,128)S(1)}, f32[24,16,128]{2,1,0:T(8,128)S(1)}) custom-call(f32[88,8,128]{2,1,0:T(8,128)S(1)} %get-tuple-element.21.up_ref, f32[88,8,128]{2,1,0:T(8,128)S(1)} %collective-permute-done.high_ref, f32[88,8,128]{2,1,0:T(8,128)S(1)} %collective-permute-done.1.low_ref, f32[24,8,128]{2,1,0:T(8,128)S(1)} %get-tuple-element.23.pot_ref, ...), custom_call_target="tpu_custom_call" | custom-call | flops 1000000 | bytes 2000000 | tf_op jit(solution)/shard_map/tail/pallas_call | solution.py:41
  24.9 0.1 collective-permute-start.5
  25.0 4.9 %collective-permute-start.4 = (f32[24,8,128]{2,1,0:T(8,128)S(1)}, f32[24,8,128]{2,1,0:T(8,128)S(1)}, u32[]{:S(2)}, u32[]{:S(2)}) collective-permute-start(f32[24,8,128]{2,1,0:T(8,128)S(1)} %get-tuple-element.35.mid_ref), channel_id=1, source_target_pairs={{0,248},{8,0},{16,8},{24,16},{32,24},{40,32},{48,40},{56,48},{64,5... | collective-permute-start | bytes 294920 | tf_op jit(solution)/shard_map/ppermute | solution.py:511
  30.0 2.4 %collective-permute-done.5.lowy_ref = f32[24,8,128]{2,1,0:T(8,128)S(1)} collective-permute-done((f32[24,8,128]{2,1,0:T(8,128)S(1)}, f32[24,8,128]{2,1,0:T(8,128)S(1)}, u32[]{:S(2)}, u32[]{:S(2)}) %collective-permute-start.5) | collective-permute-done | bytes 98336 | tf_op jit(solution)/shard_map/ppermute | solution.py:510
  32.4 2.7 %last.1.own_ref = f32[24,8,128]{2,1,0:T(8,128)S(1)} custom-call(f32[88,8,128]{2,1,0:T(8,128)S(1)} %get-tuple-element.21.up_ref, f32[88,8,128]{2,1,0:T(8,128)S(1)} %collective-permute-done.high_ref, f32[88,8,128]{2,1,0:T(8,128)S(1)} %collective-permute-done.1.low_ref, f32[24,8,128]{2,1,0:T(8,128)S(1)} %get-tuple-element.23.pot_ref, ...), custom_call_target="tpu_custom_call" | custom-call | flops 1000000 | bytes 2000000 | tf_op jit(solution)/shard_map/last/pallas_call | solution.py:41
  35.1 1.3 %collective-permute-start.6 = (f32[24,8,128]{2,1,0:T(8,128)S(1)}, f32[24,8,128]{2,1,0:T(8,128)S(1)}, u32[]{:S(2)}, u32[]{:S(2)}) collective-permute-start(f32[24,8,128]{2,1,0:T(8,128)S(1)} %last.1.own_ref), channel_id=1, source_target_pairs={{0,1},{1,0},{2,3},{3,2},{4,5},{5,4},{6,7},{7,6},{8,9},{9,8},{10,11... | collective-permute-start | bytes 294920 | tf_op jit(solution)/shard_map/ppermute | solution.py:521
  36.4 2.9 %collective-permute-start.9 = (f32[24,8,128]{2,1,0:T(8,128)S(1)}, f32[24,8,128]{2,1,0:T(8,128)S(1)}, u32[]{:S(2)}, u32[]{:S(2)}) collective-permute-start(f32[24,8,128]{2,1,0:T(8,128)S(1)} %last.1.own_ref), channel_id=1, source_target_pairs={{0,4},{1,5},{2,6},{3,7},{4,0},{5,1},{6,2},{7,3},{8,12},{9,13},{10,... | collective-permute-start | bytes 294920 | tf_op jit(solution)/shard_map/ppermute | solution.py:520
  39.4 0.5 %collective-permute-start.7 = (f32[24,8,128]{2,1,0:T(8,128)S(1)}, f32[24,8,128]{2,1,0:T(8,128)S(1)}, u32[]{:S(2)}, u32[]{:S(2)}) collective-permute-start(f32[24,8,128]{2,1,0:T(8,128)S(1)} %get-tuple-element.38), channel_id=1, source_target_pairs={{0,2},{1,3},{2,0},{3,1},{4,6},{5,7},{6,4},{7,5},{8,10},{9,11},{10,... | collective-permute-start | bytes 294920 | tf_op jit(solution)/shard_map/ppermute | solution.py:524
  39.9 0.8 %collective-permute-start.8 = (f32[24,8,128]{2,1,0:T(8,128)S(1)}, f32[24,8,128]{2,1,0:T(8,128)S(1)}, u32[]{:S(2)}, u32[]{:S(2)}) collective-permute-start(f32[24,8,128]{2,1,0:T(8,128)S(1)} %get-tuple-element.39), channel_id=1, source_target_pairs={{0,6},{1,7},{2,4},{3,5},{4,2},{5,3},{6,0},{7,1},{8,14},{9,15},{10,... | collective-permute-start | bytes 294920 | tf_op jit(solution)/shard_map/ppermute | solution.py:525
  40.7 1.6 %collective-permute-done.9.far_ref = f32[24,8,128]{2,1,0:T(8,128)S(1)} collective-permute-done((f32[24,8,128]{2,1,0:T(8,128)S(1)}, f32[24,8,128]{2,1,0:T(8,128)S(1)}, u32[]{:S(2)}, u32[]{:S(2)}) %collective-permute-start.9) | collective-permute-done | bytes 98336 | tf_op jit(solution)/shard_map/ppermute | solution.py:520
  42.3 0.9 %collective-permute-start.10 = (f32[24,8,128]{2,1,0:T(8,128)S(1)}, f32[24,8,128]{2,1,0:T(8,128)S(1)}, u32[]{:S(2)}, u32[]{:S(2)}) collective-permute-start(f32[24,8,128]{2,1,0:T(8,128)S(1)} %collective-permute-done.9.far_ref), channel_id=1, source_target_pairs={{0,1},{1,0},{2,3},{3,2},{4,5},{5,4},{6,7},{7,6},{8,9},{9,8},{10,11... | collective-permute-start | bytes 294920 | tf_op jit(solution)/shard_map/ppermute | solution.py:526
  43.2 0.6 %store.1 = f32[24,8,128]{2,1,0:T(8,128)} custom-call(f32[24,8,128]{2,1,0:T(8,128)S(1)} %last.1.own_ref), custom_call_target="tpu_custom_call" | custom-call | tf_op jit(solution)/shard_map/store/pallas_call | solution.py:41
  43.8 0.9 %collective-permute-done.7.one_ref = f32[24,8,128]{2,1,0:T(8,128)S(1)} collective-permute-done((f32[24,8,128]{2,1,0:T(8,128)S(1)}, f32[24,8,128]{2,1,0:T(8,128)S(1)}, u32[]{:S(2)}, u32[]{:S(2)}) %collective-permute-start.7) | collective-permute-done | bytes 98336 | tf_op jit(solution)/shard_map/ppermute | solution.py:524
  44.8 0.7 %total.1 = f32[24,8,128]{2,1,0:T(8,128)} custom-call(f32[8,8,128]{2,1,0:T(8,128)S(1)} %get-tuple-element.36.factors_ref, f32[24,8,128]{2,1,0:T(8,128)S(1)} %most.1.most_ref, f32[24,8,128]{2,1,0:T(8,128)S(1)} %collective-permute-done.10.farsib_ref), custom_call_target="tpu_custom_call" | custom-call | flops 1000000 | bytes 2000000 | tf_op jit(solution)/shard_map/total/pallas_call | solution.py:41
  (9 shorter events, 0.1 us)
Async XLA Ops:
  2.7 8.8 %copy-start = (f32[8,8]{1,0:T(8,128)S(1)}, f32[8,8]{1,0:T(8,128)}, u32[]{:S(2)}) copy-start(f32[8,8]{1,0:T(8,128)} %ritz_ref.1) | copy-start | bytes 772
  2.7 16.8 %collective-permute-start.1 = (f32[88,8,128]{2,1,0:T(8,128)S(1)}, f32[88,8,128]{2,1,0:T(8,128)S(1)}, u32[]{:S(2)}, u32[]{:S(2)}) collective-permute-start(f32[88,8,128]{2,1,0:T(8,128)S(1)} %get-tuple-element.22), channel_id=1, source_target_pairs={{0,8},{8,16},{16,24},{24,32},{32,40},{40,48},{48,56},{56,64},{64,7... | collective-permute-start | bytes 1081352 | tf_op jit(solution)/shard_map/ppermute | solution.py:468
  4.8 15.9 %collective-permute-start = (f32[88,8,128]{2,1,0:T(8,128)S(1)}, f32[88,8,128]{2,1,0:T(8,128)S(1)}, u32[]{:S(2)}, u32[]{:S(2)}) collective-permute-start(f32[88,8,128]{2,1,0:T(8,128)S(1)} %get-tuple-element.21.up_ref), channel_id=1, source_target_pairs={{0,248},{8,0},{16,8},{24,16},{32,24},{40,32},{48,40},{56,48},{64,5... | collective-permute-start | bytes 1081352 | tf_op jit(solution)/shard_map/ppermute | solution.py:469
  19.5 3.1 %collective-permute-start.3 = (f32[88,8,128]{2,1,0:T(8,128)S(1)}, f32[88,8,128]{2,1,0:T(8,128)S(1)}, u32[]{:S(2)}, u32[]{:S(2)}) collective-permute-start(f32[88,8,128]{2,1,0:T(8,128)S(1)} %collective-permute-done.1.low_ref), channel_id=1, source_target_pairs={{0,1},{1,0},{2,3},{3,2},{4,5},{5,4},{6,7},{7,6},{8,9},{9,8},{10,11... | collective-permute-start | bytes 1081352 | tf_op jit(solution)/shard_map/ppermute | solution.py:486
  20.8 1.9 %collective-permute-start.2 = (f32[88,8,128]{2,1,0:T(8,128)S(1)}, f32[88,8,128]{2,1,0:T(8,128)S(1)}, u32[]{:S(2)}, u32[]{:S(2)}) collective-permute-start(f32[88,8,128]{2,1,0:T(8,128)S(1)} %collective-permute-done.high_ref), channel_id=1, source_target_pairs={{0,1},{1,0},{2,3},{3,2},{4,5},{5,4},{6,7},{7,6},{8,9},{9,8},{10,11... | collective-permute-start | bytes 1081352 | tf_op jit(solution)/shard_map/ppermute | solution.py:485
  24.9 7.4 %collective-permute-start.5 = (f32[24,8,128]{2,1,0:T(8,128)S(1)}, f32[24,8,128]{2,1,0:T(8,128)S(1)}, u32[]{:S(2)}, u32[]{:S(2)}) collective-permute-start(f32[24,8,128]{2,1,0:T(8,128)S(1)} %get-tuple-element.35.mid_ref), channel_id=1, source_target_pairs={{0,8},{8,16},{16,24},{24,32},{32,40},{40,48},{48,56},{56,64},{64,7... | collective-permute-start | bytes 294920 | tf_op jit(solution)/shard_map/ppermute | solution.py:510
  25.0 7.3 %collective-permute-start.4 = (f32[24,8,128]{2,1,0:T(8,128)S(1)}, f32[24,8,128]{2,1,0:T(8,128)S(1)}, u32[]{:S(2)}, u32[]{:S(2)}) collective-permute-start(f32[24,8,128]{2,1,0:T(8,128)S(1)} %get-tuple-element.35.mid_ref), channel_id=1, source_target_pairs={{0,248},{8,0},{16,8},{24,16},{32,24},{40,32},{48,40},{56,48},{64,5... | collective-permute-start | bytes 294920 | tf_op jit(solution)/shard_map/ppermute | solution.py:511
  35.1 4.3 %collective-permute-start.6 = (f32[24,8,128]{2,1,0:T(8,128)S(1)}, f32[24,8,128]{2,1,0:T(8,128)S(1)}, u32[]{:S(2)}, u32[]{:S(2)}) collective-permute-start(f32[24,8,128]{2,1,0:T(8,128)S(1)} %last.1.own_ref), channel_id=1, source_target_pairs={{0,1},{1,0},{2,3},{3,2},{4,5},{5,4},{6,7},{7,6},{8,9},{9,8},{10,11... | collective-permute-start | bytes 294920 | tf_op jit(solution)/shard_map/ppermute | solution.py:521
  36.4 5.9 %collective-permute-start.9 = (f32[24,8,128]{2,1,0:T(8,128)S(1)}, f32[24,8,128]{2,1,0:T(8,128)S(1)}, u32[]{:S(2)}, u32[]{:S(2)}) collective-permute-start(f32[24,8,128]{2,1,0:T(8,128)S(1)} %last.1.own_ref), channel_id=1, source_target_pairs={{0,4},{1,5},{2,6},{3,7},{4,0},{5,1},{6,2},{7,3},{8,12},{9,13},{10,... | collective-permute-start | bytes 294920 | tf_op jit(solution)/shard_map/ppermute | solution.py:520
  39.4 5.3 %collective-permute-start.7 = (f32[24,8,128]{2,1,0:T(8,128)S(1)}, f32[24,8,128]{2,1,0:T(8,128)S(1)}, u32[]{:S(2)}, u32[]{:S(2)}) collective-permute-start(f32[24,8,128]{2,1,0:T(8,128)S(1)} %get-tuple-element.38), channel_id=1, source_target_pairs={{0,2},{1,3},{2,0},{3,1},{4,6},{5,7},{6,4},{7,5},{8,10},{9,11},{10,... | collective-permute-start | bytes 294920 | tf_op jit(solution)/shard_map/ppermute | solution.py:524
  39.9 4.9 %collective-permute-start.8 = (f32[24,8,128]{2,1,0:T(8,128)S(1)}, f32[24,8,128]{2,1,0:T(8,128)S(1)}, u32[]{:S(2)}, u32[]{:S(2)}) collective-permute-start(f32[24,8,128]{2,1,0:T(8,128)S(1)} %get-tuple-element.39), channel_id=1, source_target_pairs={{0,6},{1,7},{2,4},{3,5},{4,2},{5,3},{6,0},{7,1},{8,14},{9,15},{10,... | collective-permute-start | bytes 294920 | tf_op jit(solution)/shard_map/ppermute | solution.py:525
  42.3 2.5 %collective-permute-start.10 = (f32[24,8,128]{2,1,0:T(8,128)S(1)}, f32[24,8,128]{2,1,0:T(8,128)S(1)}, u32[]{:S(2)}, u32[]{:S(2)}) collective-permute-start(f32[24,8,128]{2,1,0:T(8,128)S(1)} %collective-permute-done.9.far_ref), channel_id=1, source_target_pairs={{0,1},{1,0},{2,3},{3,2},{4,5},{5,4},{6,7},{7,6},{8,9},{9,8},{10,11... | collective-permute-start | bytes 294920 | tf_op jit(solution)/shard_map/ppermute | solution.py:526

commit v7 on v6

--- a/solution.py
+++ b/solution.py
@@ -88,8 +88,9 @@
 
 
 def pack_kernel(y_hbm, pot_hbm, proj_hbm, gamma_hbm, pos_hbm, count_ref,
-                up_ref, down_ref, pot_ref, rest_ref, gamma_ref, pos_ref, half_ref, work, sems):
+                far_ref, near_ref, pot_ref, rest_ref, gamma_ref, pos_ref, half_ref, work, sems):
     core = lax.axis_index("band") % 2
+    odd = lax.axis_index("dom") % 2
     copies = [
         pltpu.make_async_copy(gamma_hbm, gamma_ref, sems.at[0]),
         pltpu.make_async_copy(pos_hbm, pos_ref, sems.at[1]),
@@ -100,7 +101,7 @@
             source = proj_hbm.at[pl.ds(first, 16), pl.ds(0, 8), pl.ds(128 * part, 128)]
             moves.append((source, target.at[pl.ds(16 * part, 16)]))
     moves.append((pot_hbm, pot_ref))
-    for out, first in ((up_ref, 12), (down_ref, 0)):
+    for out, first in ((far_ref, 12 * odd), (near_ref, 12 - 12 * odd)):
         moves.append((y_hbm, out.at[pl.ds(TILE_Y, 24)]))
         moves.append((pot_hbm.at[pl.ds(first, 12)], out.at[pl.ds(TILE_POT, 12)]))
     for n, (source, target) in enumerate(moves):
@@ -121,7 +122,7 @@
     column = spread(corner, repeat)[2:3] + (lax.broadcasted_iota(jnp.int32, (1, LANES), 1) & 7).astype(jnp.float32)
     column = jnp.where(column >= NZ, column - NZ, column)
     corner = spread(corner, order)
-    for out in (up_ref, down_ref):
+    for out in (far_ref, near_ref):
         for tile in range(2):
             out[TILE_META + 2 * tile] = weight[:, half(tile)]
             out[TILE_META + 2 * tile + 1] = jnp.broadcast_to(column[:, half(tile)], (8, 128))
@@ -129,7 +130,7 @@
         out[TILE_META + 1, ROW_Y0 : ROW_Y0 + 1, :] = corner[1:2]
     for copy in copies[2:5]:
         copy.wait()
-    tables = [out.at[pl.ds(TILE_P, PAIRS)] for out in (up_ref, down_ref)]
+    tables = [out.at[pl.ds(TILE_P, PAIRS)] for out in (far_ref, near_ref)]
     spread_projectors(lambda part, a: half_ref[16 * part + a], work, *tables)
     for copy in copies[5:]:
         copy.wait()
@@ -167,11 +168,31 @@
     padded[plane : plane + count, 24:32, :] = value[:, 0:8]
 
 
+class Side:
+    def __init__(self, far, near, share):
+        self.far, self.near, self.share = far, near, share
+        self.shape = far.shape
+
+    def __getitem__(self, index):
+        return self.far[index] * self.share + self.near[index] * (1.0 - self.share)
+
+    def rows(self, rows):
+        return Side(self.far.at[rows], self.near.at[rows], self.share)
+
+
+def sides(far, near):
+    odd = (lax.axis_index("dom") % 2).astype(jnp.float32)
+    return Side(far, near, 1.0 - odd), Side(far, near, odd)
+
+
 class Boxes:
-    def __init__(self, sources, held, sems):
-        self.sources, self.held = sources, held
+    def __init__(self, far, own, near, held, sems):
+        low, high = sides(far, near)
+        self.sources, self.held = (low, own, high), held
+        odd = lax.axis_index("dom") % 2
         self.copies = [
-            pltpu.make_async_copy(s.at[TILE_META + 1], h, sems.at[n]) for n, (s, h) in enumerate(zip(sources, held))
+            pltpu.make_async_copy(source.at[TILE_META + 1], held.at[slot], sems.at[n])
+            for n, (source, slot) in enumerate(((far, 2 * odd), (own, 1), (near, 2 - 2 * odd)))
         ]
         for copy in self.copies:
             copy.start()
@@ -181,8 +202,7 @@
             copy.wait()
 
     def place(self, group, atom):
-        held = self.held[group]
-        return held[ROW_X0, atom].astype(jnp.int32), held[ROW_Y0, atom].astype(jnp.int32)
+        return self.held[group, ROW_X0, atom].astype(jnp.int32), self.held[group, ROW_Y0, atom].astype(jnp.int32)
 
     def weight(self, group):
         source = self.sources[group]
@@ -286,7 +306,7 @@
 
 def laid(first, second):
     rows = pl.ds(TILE_P, PAIRS)
-    return first.at[rows], second if second.shape[0] == PAIRS else second.at[rows]
+    return tuple(v.rows(rows) if isinstance(v, Side) else v if v.shape[0] == PAIRS else v.at[rows] for v in (first, second))
 
 
 def load_fields(fields, padded, field2):
@@ -295,10 +315,11 @@
         field2[192 * n : 192 * n + 192, :] = two_terms(value.reshape(192, NZ), 1)
 
 
-def head_kernel(up_ref, high_ref, low_ref, pot_ref, table_ref, zst_ref, sums_ref, hot_ref, back_ref,
+def head_kernel(up_ref, near_ref, far_ref, pot_ref, table_ref, zst_ref, sums_ref, hot_ref, back_ref,
                 values_ref, partial_ref, hots_ref, backs_ref,
-                low_xy, own_xy, high_xy, padded, field2, gathered, placed, local, sems):
-    boxes = Boxes((low_ref, up_ref, high_ref), (low_xy, own_xy, high_xy), sems)
+                xy, padded, field2, gathered, placed, local, sems):
+    boxes = Boxes(far_ref, up_ref, near_ref, xy, sems)
+    low_ref, high_ref = sides(far_ref, near_ref)
     load_fields([r[TILE_Y : TILE_Y + 24] for r in (low_ref, up_ref, high_ref)], padded, field2)
     clear(placed)
     gathered[2][:, 12:SPAN] = jnp.zeros((2, SPAN - 12, 24, 128), jnp.float32)
@@ -341,11 +362,13 @@
         yield p, (local[p] + nonlocal_[p]) * (2.0 / HALF)
 
 
-def tail_kernel(up_ref, high_ref, low_ref, pot_ref, table_ref, zst_ref, sums_ref, hot_ref, back_ref,
-                values_ref, partial_ref, hots_ref, backs_ref, highsib_ref, lowsib_ref,
+def tail_kernel(up_ref, near_ref, far_ref, pot_ref, table_ref, zst_ref, sums_ref, hot_ref, back_ref,
+                values_ref, partial_ref, hots_ref, backs_ref, nearsib_ref, farsib_ref,
                 out_ref, kept_ref,
-                low_xy, own_xy, high_xy, padded1, field2, gathered, placed, local, nonlocal_, sems):
-    boxes = Boxes((low_ref, up_ref, high_ref), (low_xy, own_xy, high_xy), sems)
+                xy, padded1, field2, gathered, placed, local, nonlocal_, sems):
+    boxes = Boxes(far_ref, up_ref, near_ref, xy, sems)
+    low_ref, high_ref = sides(far_ref, near_ref)
+    lowsib_ref, highsib_ref = sides(farsib_ref, nearsib_ref)
     clear(placed)
     gathered[0][:, 0:6] = jnp.zeros((2, 6, 24, 128), jnp.float32)
     tables = (laid(low_ref, lowsib_ref), laid(up_ref, table_ref), laid(high_ref, highsib_ref))
@@ -368,12 +391,15 @@
         out_ref[2 * p : 2 * p + 2] = (value - up_ref[TILE_Y + 2 * p : TILE_Y + 2 * p + 2].reshape(NY, NZ)).reshape(2, 8, 128)
 
 
-def last_kernel(up_ref, high_ref, low_ref, pot_ref, table_ref, zst_ref, sums_ref, hot_ref, back_ref,
-                kept_ref, hots_ref, backs_ref, highsib_ref, lowsib_ref,
-                mid_ref, highy_ref, lowy_ref,
+def last_kernel(up_ref, near_ref, far_ref, pot_ref, table_ref, zst_ref, sums_ref, hot_ref, back_ref,
+                kept_ref, hots_ref, backs_ref, nearsib_ref, farsib_ref,
+                mid_ref, neary_ref, fary_ref,
                 out_ref,
-                low_xy, own_xy, high_xy, padded, padded1, field2, gathered, placed, local, nonlocal_, sems):
-    boxes = Boxes((low_ref, up_ref, high_ref), (low_xy, own_xy, high_xy), sems)
+                xy, padded, padded1, field2, gathered, placed, local, nonlocal_, sems):
+    boxes = Boxes(far_ref, up_ref, near_ref, xy, sems)
+    low_ref, high_ref = sides(far_ref, near_ref)
+    lowy_ref, highy_ref = sides(fary_ref, neary_ref)
+    lowsib_ref, highsib_ref = sides(farsib_ref, nearsib_ref)
     load_fields([r[...] for r in (lowy_ref, mid_ref, highy_ref)], padded, field2)
     clear(placed)
     gathered[2][:, 12:SPAN] = jnp.zeros((2, SPAN - 12, 24, 128), jnp.float32)
@@ -405,7 +431,7 @@
         out_ref[2 * p : 2 * p + 2] = (value - padded[p + 12, 8:24, :]).reshape(2, 8, 128)
 
 
-XY = [pltpu.SMEM((8, 128), jnp.float32)] * 3
+XY = [pltpu.SMEM((3, 8, 128), jnp.float32)]
 PADDED = pltpu.VMEM((36, 32, NZ), jnp.float32)
 PADDED1 = pltpu.VMEM((24, 32, NZ), jnp.float32)
 FIELD2 = pltpu.VMEM((576, 2 * NZ), jnp.bfloat16)
@@ -433,9 +459,10 @@
     out_ref[...] = most_ref[...] + factors_ref[5] * farsib_ref[...]
 
 
-def ring(axis, step):
-    count = lax.axis_size(axis)
-    return [(i, (i + step) % count) for i in range(count)]
+def couples(first):
+    count = lax.axis_size("dom")
+    pairs = [(i % count, (i + 1) % count) for i in range(first, first + count, 2)]
+    return pairs + [(target, source) for source, target in pairs]
 
 
 def meet(axis, bits):
@@ -444,7 +471,7 @@
 
 def shards(orbitals, potential, atom_pos, atom_count, projectors, gammas, ritz):
     stay = lambda v: pltpu.with_memory_space_constraint(v, pltpu.HBM)
-    up, down, pot, rest = call(
+    far, near, pot, rest = call(
         pack_kernel,
         [shape(TILES, 8, 128), shape(TILES, 8, 128), shape(24, 8, 128), shape(PAIRS, 8, 128)],
         [HBM] * 5 + [SMEM],
@@ -465,8 +492,8 @@
             pltpu.SemaphoreType.DMA((13,)),
         ],
     )
-    low = lax.ppermute(up, "dom", ring("dom", 1))
-    high = lax.ppermute(down, "dom", ring("dom", -1))
+    from_far = lax.ppermute(far, "dom", couples(1))
+    from_near = lax.ppermute(near, "dom", couples(0))
     table, zst, sums, hot, back, factors = call(
         prepare_kernel,
         [
@@ -478,13 +505,13 @@
             shape(8, 8, 128),
         ],
         [VMEM] * 3,
-        (rest, down, ritz),
+        (rest, near, ritz),
         "prepare",
         [WORK],
     )
-    highsib = lax.ppermute(high, "band", meet("band", 1))
-    lowsib = lax.ppermute(low, "band", meet("band", 1))
-    common = (down, high, low, pot, table, zst, sums, hot, back)
+    nearsib = lax.ppermute(from_near, "band", meet("band", 1))
+    farsib = lax.ppermute(from_far, "band", meet("band", 1))
+    common = (near, from_near, from_far, pot, table, zst, sums, hot, back)
     values, partial, hots, backs = call(
         head_kernel,
         [
@@ -503,17 +530,17 @@
         tail_kernel,
         [shape(24, 8, 128), shape(24, NY, NZ)],
         [VMEM] * 15,
-        common + (values, partial, hots, backs, highsib, lowsib),
+        common + (values, partial, hots, backs, nearsib, farsib),
         "tail",
         XY + [PADDED1, FIELD2, BOXED, BOXED, PLANES, PLANES, COPIES],
     )
-    low_y = lax.ppermute(second, "dom", ring("dom", 1))
-    high_y = lax.ppermute(second, "dom", ring("dom", -1))
+    far_y = lax.ppermute(second, "dom", couples(1))
+    near_y = lax.ppermute(second, "dom", couples(0))
     (fourth,) = call(
         last_kernel,
         [shape(24, 8, 128)],
         [VMEM] * 17,
-        common + (first, hots, backs, highsib, lowsib, second, high_y, low_y),
+        common + (first, hots, backs, nearsib, farsib, second, near_y, far_y),
         "last",
         XY + [PADDED, PADDED1, FIELD2, BOXED, BOXED, PLANES, PLANES, COPIES],
     )

time: 45.5 us -> 47.5 us (1.044)
  waiting for transfers between devices: 12.4 us -> 14.5 us
  Pallas kernels: 10.1 us -> 10.6 us
  starting transfers between devices: 21.5 us -> 21 us
    ppermute x6, waiting for transfers between devices: 9.9 us -> 12 us  [the longest x1 7.58 us: shards(): from_far = lax.ppermute(far, 'dom', couples(1))]
where the time goes in v7:
time: 47.5 us; the launch traced here: 47.4 us
  starting transfers between devices  21 us (44%)
  waiting for transfers between devices  14.5 us (31%)
  Pallas kernels  10.6 us (22%)
  between operations  1.37 us (3%)
    pallas_call x9, Pallas kernels, call(): pl.pallas_call(kernel, out_shape=outs, in_specs=ins, out_specs=out_specs...  10.6 us
    ppermute x1, starting transfers between devices, shards(): from_far = lax.ppermute(far, 'dom', couples(1))  8.69 us
    ppermute x1, waiting for transfers between devices, shards(): from_far = lax.ppermute(far, 'dom', couples(1))  7.58 us
    ppermute x1, waiting for transfers between devices, shards(): far_y = lax.ppermute(second, 'dom', couples(1))  4.41 us
    ppermute x1, starting transfers between devices, shards(): far_y = lax.ppermute(second, 'dom', couples(1))  3.42 us
    ppermute x1, starting transfers between devices, shards(): far = lax.ppermute(fourth, 'band', meet('band', 4))  2.93 us
    ppermute x1, waiting for transfers between devices, shards(): far = lax.ppermute(fourth, 'band', meet('band', 4))  1.6 us
    ppermute x1, starting transfers between devices, shards(): nearsib = lax.ppermute(from_near, 'band', meet('band', 1))  1.46 us
  transfers between devices with their start and end apart: 11, of which 4 were waited for; matrix products, arithmetic and copies ran while one was open for 0% of the time, Pallas kernels for 7%

profile of v7, /device:TPU:1, one launch (start us, length us, event | category | flops | bytes accessed | tf_op | source)
XLA Modules:
  0.0 47.4 jit_solution(9048225014343327586)
XLA Ops:
  1.3 1.4 %pack.1 = (f32[88,8,128]{2,1,0:T(8,128)S(1)}, f32[88,8,128]{2,1,0:T(8,128)S(1)}, f32[24,8,128]{2,1,0:T(8,128)S(1)}, f32[48,8,128]{2,1,0:T(8,128)S(1)}) custom-call(f32[24,8,128]{2,1,0:T(8,128)} %bitcast.8, f32[24,8,128]{2,1,0:T(8,128)} %bitcast.9, f32[32,8,384]{2,1,0:T(8,128)} %proj_hbm.1, f32[8,32]{1,0:T(8,128)} %bitcast.10, s32[3,32]{1,0:T(4,128)} %bitcast.11, ...), custom_call_target="tpu_custom_call" | custom-call | flops 1000000 | bytes 2000000 | tf_op jit(solution)/shard_map/pack/pallas_call | solution.py:41
  2.7 0.0 copy-start
  2.7 8.7 %collective-permute-start.1 = (f32[88,8,128]{2,1,0:T(8,128)S(1)}, f32[88,8,128]{2,1,0:T(8,128)S(1)}, u32[]{:S(2)}, u32[]{:S(2)}) collective-permute-start(f32[88,8,128]{2,1,0:T(8,128)S(1)} %get-tuple-element.22), channel_id=1, source_target_pairs={{8,16},{24,32},{40,48},{56,64},{72,80},{88,96},{104,112},{120,128}... | collective-permute-start | bytes 1081352 | tf_op jit(solution)/shard_map/ppermute | solution.py:495
  11.4 0.0 collective-permute-start
  11.4 0.5 %prepare.1 = (f32[48,8,128]{2,1,0:T(8,128)S(1)}, bf16[384,128]{1,0:T(8,128)(2,1)S(1)}, bf16[256,256]{1,0:T(8,128)(2,1)S(1)}, bf16[256,256]{1,0:T(8,128)(2,1)S(1)...) custom-call(f32[48,8,128]{2,1,0:T(8,128)S(1)} %get-tuple-element.24.rest_ref, ...), custom_call_target="tpu_custom_call" | custom-call | flops 1000000 | bytes 2000000 | tf_op jit(solution)/shard_map/prepare/pallas_call | solution.py:41
  12.0 7.6 %collective-permute-done.1.far_ref = f32[88,8,128]{2,1,0:T(8,128)S(1)} collective-permute-done((f32[88,8,128]{2,1,0:T(8,128)S(1)}, f32[88,8,128]{2,1,0:T(8,128)S(1)}, u32[]{:S(2)}, u32[]{:S(2)}) %collective-permute-start.1) | collective-permute-done | bytes 360480 | tf_op jit(solution)/shard_map/ppermute | solution.py:495
  19.5 1.2 %collective-permute-start.3 = (f32[88,8,128]{2,1,0:T(8,128)S(1)}, f32[88,8,128]{2,1,0:T(8,128)S(1)}, u32[]{:S(2)}, u32[]{:S(2)}) collective-permute-start(f32[88,8,128]{2,1,0:T(8,128)S(1)} %collective-permute-done.1.far_ref), channel_id=1, source_target_pairs={{0,1},{1,0},{2,3},{3,2},{4,5},{5,4},{6,7},{7,6},{8,9},{9,8},{10,11... | collective-permute-start | bytes 1081352 | tf_op jit(solution)/shard_map/ppermute | solution.py:513
  20.8 0.0 collective-permute-done.near_ref
  20.8 1.5 %collective-permute-start.2 = (f32[88,8,128]{2,1,0:T(8,128)S(1)}, f32[88,8,128]{2,1,0:T(8,128)S(1)}, u32[]{:S(2)}, u32[]{:S(2)}) collective-permute-start(f32[88,8,128]{2,1,0:T(8,128)S(1)} %collective-permute-done.near_ref), channel_id=1, source_target_pairs={{0,1},{1,0},{2,3},{3,2},{4,5},{5,4},{6,7},{7,6},{8,9},{9,8},{10,11... | collective-permute-start | bytes 1081352 | tf_op jit(solution)/shard_map/ppermute | solution.py:512
  22.2 2.0 %head.1 = (f32[2,6,2,8,128]{4,3,2,1,0:T(8,128)S(1)}, f32[24,16,128]{2,1,0:T(8,128)S(1)}, bf16[2,256,256]{2,1,0:T(8,128)(2,1)S(1)}, bf16[2,512,128]{2,1,0:T(8,128)(2,1)S(1)}) custom-call(f32[88,8,128]{2,1,0:T(8,128)S(1)} %get-tuple-element.21.up_ref, f32[88,8,128]{2,1,0:T(8,128)S(1)} %collective-permute-done.near_ref, ...), custom_call_target="tpu_custom_call" | custom-call | flops 10000000000 | bytes 2000000 | tf_op jit(solution)/shard_map/head/pallas_call | solution.py:41
  24.3 2.3 %tail.1 = (f32[24,8,128]{2,1,0:T(8,128)S(1)}, f32[24,16,128]{2,1,0:T(8,128)S(1)}) custom-call(f32[88,8,128]{2,1,0:T(8,128)S(1)} %get-tuple-element.21.up_ref, f32[88,8,128]{2,1,0:T(8,128)S(1)} %collective-permute-done.near_ref, f32[88,8,128]{2,1,0:T(8,128)S(1)} %collective-permute-done.1.far_ref, f32[24,8,128]{2,1,0:T(8,128)S(1)} %get-tuple-element.23.pot_ref, ...), custom_call_target="tpu_custom_call" | custom-call | flops 1000000 | bytes 2000000 | tf_op jit(solution)/shard_map/tail/pallas_call | solution.py:41
  26.6 3.4 %collective-permute-start.5 = (f32[24,8,128]{2,1,0:T(8,128)S(1)}, f32[24,8,128]{2,1,0:T(8,128)S(1)}, u32[]{:S(2)}, u32[]{:S(2)}) collective-permute-start(f32[24,8,128]{2,1,0:T(8,128)S(1)} %get-tuple-element.35.mid_ref), channel_id=1, source_target_pairs={{8,16},{24,32},{40,48},{56,64},{72,80},{88,96},{104,112},{120,128}... | collective-permute-start | bytes 294920 | tf_op jit(solution)/shard_map/ppermute | solution.py:537
  30.0 0.0 collective-permute-start.4
  30.0 4.4 %collective-permute-done.5.fary_ref = f32[24,8,128]{2,1,0:T(8,128)S(1)} collective-permute-done((f32[24,8,128]{2,1,0:T(8,128)S(1)}, f32[24,8,128]{2,1,0:T(8,128)S(1)}, u32[]{:S(2)}, u32[]{:S(2)}) %collective-permute-start.5) | collective-permute-done | bytes 98336 | tf_op jit(solution)/shard_map/ppermute | solution.py:537
  34.4 2.9 %last.1.own_ref = f32[24,8,128]{2,1,0:T(8,128)S(1)} custom-call(f32[88,8,128]{2,1,0:T(8,128)S(1)} %get-tuple-element.21.up_ref, f32[88,8,128]{2,1,0:T(8,128)S(1)} %collective-permute-done.near_ref, f32[88,8,128]{2,1,0:T(8,128)S(1)} %collective-permute-done.1.far_ref, f32[24,8,128]{2,1,0:T(8,128)S(1)} %get-tuple-element.23.pot_ref, ...), custom_call_target="tpu_custom_call" | custom-call | flops 1000000 | bytes 2000000 | tf_op jit(solution)/shard_map/last/pallas_call | solution.py:41
  37.3 1.1 %collective-permute-start.6 = (f32[24,8,128]{2,1,0:T(8,128)S(1)}, f32[24,8,128]{2,1,0:T(8,128)S(1)}, u32[]{:S(2)}, u32[]{:S(2)}) collective-permute-start(f32[24,8,128]{2,1,0:T(8,128)S(1)} %last.1.own_ref), channel_id=1, source_target_pairs={{0,1},{1,0},{2,3},{3,2},{4,5},{5,4},{6,7},{7,6},{8,9},{9,8},{10,11... | collective-permute-start | bytes 294920 | tf_op jit(solution)/shard_map/ppermute | solution.py:548
  38.4 2.9 %collective-permute-start.9 = (f32[24,8,128]{2,1,0:T(8,128)S(1)}, f32[24,8,128]{2,1,0:T(8,128)S(1)}, u32[]{:S(2)}, u32[]{:S(2)}) collective-permute-start(f32[24,8,128]{2,1,0:T(8,128)S(1)} %last.1.own_ref), channel_id=1, source_target_pairs={{0,4},{1,5},{2,6},{3,7},{4,0},{5,1},{6,2},{7,3},{8,12},{9,13},{10,... | collective-permute-start | bytes 294920 | tf_op jit(solution)/shard_map/ppermute | solution.py:547
  41.4 0.5 %collective-permute-start.7 = (f32[24,8,128]{2,1,0:T(8,128)S(1)}, f32[24,8,128]{2,1,0:T(8,128)S(1)}, u32[]{:S(2)}, u32[]{:S(2)}) collective-permute-start(f32[24,8,128]{2,1,0:T(8,128)S(1)} %get-tuple-element.38), channel_id=1, source_target_pairs={{0,2},{1,3},{2,0},{3,1},{4,6},{5,7},{6,4},{7,5},{8,10},{9,11},{10,... | collective-permute-start | bytes 294920 | tf_op jit(solution)/shard_map/ppermute | solution.py:551
  41.9 0.8 %collective-permute-start.8 = (f32[24,8,128]{2,1,0:T(8,128)S(1)}, f32[24,8,128]{2,1,0:T(8,128)S(1)}, u32[]{:S(2)}, u32[]{:S(2)}) collective-permute-start(f32[24,8,128]{2,1,0:T(8,128)S(1)} %get-tuple-element.39), channel_id=1, source_target_pairs={{0,6},{1,7},{2,4},{3,5},{4,2},{5,3},{6,0},{7,1},{8,14},{9,15},{10,... | collective-permute-start | bytes 294920 | tf_op jit(solution)/shard_map/ppermute | solution.py:552
  42.7 1.6 %collective-permute-done.9.far_ref = f32[24,8,128]{2,1,0:T(8,128)S(1)} collective-permute-done((f32[24,8,128]{2,1,0:T(8,128)S(1)}, f32[24,8,128]{2,1,0:T(8,128)S(1)}, u32[]{:S(2)}, u32[]{:S(2)}) %collective-permute-start.9) | collective-permute-done | bytes 98336 | tf_op jit(solution)/shard_map/ppermute | solution.py:547
  44.3 0.9 %collective-permute-start.10 = (f32[24,8,128]{2,1,0:T(8,128)S(1)}, f32[24,8,128]{2,1,0:T(8,128)S(1)}, u32[]{:S(2)}, u32[]{:S(2)}) collective-permute-start(f32[24,8,128]{2,1,0:T(8,128)S(1)} %collective-permute-done.9.far_ref), channel_id=1, source_target_pairs={{0,1},{1,0},{2,3},{3,2},{4,5},{5,4},{6,7},{7,6},{8,9},{9,8},{10,11... | collective-permute-start | bytes 294920 | tf_op jit(solution)/shard_map/ppermute | solution.py:553
  45.2 0.6 %store.1 = f32[24,8,128]{2,1,0:T(8,128)} custom-call(f32[24,8,128]{2,1,0:T(8,128)S(1)} %last.1.own_ref), custom_call_target="tpu_custom_call" | custom-call | tf_op jit(solution)/shard_map/store/pallas_call | solution.py:41
  45.8 0.9 %collective-permute-done.7.one_ref = f32[24,8,128]{2,1,0:T(8,128)S(1)} collective-permute-done((f32[24,8,128]{2,1,0:T(8,128)S(1)}, f32[24,8,128]{2,1,0:T(8,128)S(1)}, u32[]{:S(2)}, u32[]{:S(2)}) %collective-permute-start.7) | collective-permute-done | bytes 98336 | tf_op jit(solution)/shard_map/ppermute | solution.py:551
  46.8 0.7 %total.1 = f32[24,8,128]{2,1,0:T(8,128)} custom-call(f32[8,8,128]{2,1,0:T(8,128)S(1)} %get-tuple-element.36.factors_ref, f32[24,8,128]{2,1,0:T(8,128)S(1)} %most.1.most_ref, f32[24,8,128]{2,1,0:T(8,128)S(1)} %collective-permute-done.10.farsib_ref), custom_call_target="tpu_custom_call" | custom-call | flops 1000000 | bytes 2000000 | tf_op jit(solution)/shard_map/total/pallas_call | solution.py:41
  (9 shorter events, 0.1 us)
Async XLA Ops:
  2.7 8.7 %copy-start = (f32[8,8]{1,0:T(8,128)S(1)}, f32[8,8]{1,0:T(8,128)}, u32[]{:S(2)}) copy-start(f32[8,8]{1,0:T(8,128)} %ritz_ref.1) | copy-start | bytes 772
  2.7 16.8 %collective-permute-start.1 = (f32[88,8,128]{2,1,0:T(8,128)S(1)}, f32[88,8,128]{2,1,0:T(8,128)S(1)}, u32[]{:S(2)}, u32[]{:S(2)}) collective-permute-start(f32[88,8,128]{2,1,0:T(8,128)S(1)} %get-tuple-element.22), channel_id=1, source_target_pairs={{8,16},{24,32},{40,48},{56,64},{72,80},{88,96},{104,112},{120,128}... | collective-permute-start | bytes 1081352 | tf_op jit(solution)/shard_map/ppermute | solution.py:495
  11.4 9.4 %collective-permute-start = (f32[88,8,128]{2,1,0:T(8,128)S(1)}, f32[88,8,128]{2,1,0:T(8,128)S(1)}, u32[]{:S(2)}, u32[]{:S(2)}) collective-permute-start(f32[88,8,128]{2,1,0:T(8,128)S(1)} %get-tuple-element.21.up_ref), channel_id=1, source_target_pairs={{0,8},{16,24},{32,40},{48,56},{64,72},{80,88},{96,104},{112,120},{... | collective-permute-start | bytes 1081352 | tf_op jit(solution)/shard_map/ppermute | solution.py:496
  19.5 4.7 %collective-permute-start.3 = (f32[88,8,128]{2,1,0:T(8,128)S(1)}, f32[88,8,128]{2,1,0:T(8,128)S(1)}, u32[]{:S(2)}, u32[]{:S(2)}) collective-permute-start(f32[88,8,128]{2,1,0:T(8,128)S(1)} %collective-permute-done.1.far_ref), channel_id=1, source_target_pairs={{0,1},{1,0},{2,3},{3,2},{4,5},{5,4},{6,7},{7,6},{8,9},{9,8},{10,11... | collective-permute-start | bytes 1081352 | tf_op jit(solution)/shard_map/ppermute | solution.py:513
  20.8 3.5 %collective-permute-start.2 = (f32[88,8,128]{2,1,0:T(8,128)S(1)}, f32[88,8,128]{2,1,0:T(8,128)S(1)}, u32[]{:S(2)}, u32[]{:S(2)}) collective-permute-start(f32[88,8,128]{2,1,0:T(8,128)S(1)} %collective-permute-done.near_ref), channel_id=1, source_target_pairs={{0,1},{1,0},{2,3},{3,2},{4,5},{5,4},{6,7},{7,6},{8,9},{9,8},{10,11... | collective-permute-start | bytes 1081352 | tf_op jit(solution)/shard_map/ppermute | solution.py:512
  26.6 7.8 %collective-permute-start.5 = (f32[24,8,128]{2,1,0:T(8,128)S(1)}, f32[24,8,128]{2,1,0:T(8,128)S(1)}, u32[]{:S(2)}, u32[]{:S(2)}) collective-permute-start(f32[24,8,128]{2,1,0:T(8,128)S(1)} %get-tuple-element.35.mid_ref), channel_id=1, source_target_pairs={{8,16},{24,32},{40,48},{56,64},{72,80},{88,96},{104,112},{120,128}... | collective-permute-start | bytes 294920 | tf_op jit(solution)/shard_map/ppermute | solution.py:537
  30.0 4.4 %collective-permute-start.4 = (f32[24,8,128]{2,1,0:T(8,128)S(1)}, f32[24,8,128]{2,1,0:T(8,128)S(1)}, u32[]{:S(2)}, u32[]{:S(2)}) collective-permute-start(f32[24,8,128]{2,1,0:T(8,128)S(1)} %get-tuple-element.35.mid_ref), channel_id=1, source_target_pairs={{0,8},{16,24},{32,40},{48,56},{64,72},{80,88},{96,104},{112,120},{... | collective-permute-start | bytes 294920 | tf_op jit(solution)/shard_map/ppermute | solution.py:538
  37.3 4.0 %collective-permute-start.6 = (f32[24,8,128]{2,1,0:T(8,128)S(1)}, f32[24,8,128]{2,1,0:T(8,128)S(1)}, u32[]{:S(2)}, u32[]{:S(2)}) collective-permute-start(f32[24,8,128]{2,1,0:T(8,128)S(1)} %last.1.own_ref), channel_id=1, source_target_pairs={{0,1},{1,0},{2,3},{3,2},{4,5},{5,4},{6,7},{7,6},{8,9},{9,8},{10,11... | collective-permute-start | bytes 294920 | tf_op jit(solution)/shard_map/ppermute | solution.py:548
  38.4 5.9 %collective-permute-start.9 = (f32[24,8,128]{2,1,0:T(8,128)S(1)}, f32[24,8,128]{2,1,0:T(8,128)S(1)}, u32[]{:S(2)}, u32[]{:S(2)}) collective-permute-start(f32[24,8,128]{2,1,0:T(8,128)S(1)} %last.1.own_ref), channel_id=1, source_target_pairs={{0,4},{1,5},{2,6},{3,7},{4,0},{5,1},{6,2},{7,3},{8,12},{9,13},{10,... | collective-permute-start | bytes 294920 | tf_op jit(solution)/shard_map/ppermute | solution.py:547
  41.4 5.3 %collective-permute-start.7 = (f32[24,8,128]{2,1,0:T(8,128)S(1)}, f32[24,8,128]{2,1,0:T(8,128)S(1)}, u32[]{:S(2)}, u32[]{:S(2)}) collective-permute-start(f32[24,8,128]{2,1,0:T(8,128)S(1)} %get-tuple-element.38), channel_id=1, source_target_pairs={{0,2},{1,3},{2,0},{3,1},{4,6},{5,7},{6,4},{7,5},{8,10},{9,11},{10,... | collective-permute-start | bytes 294920 | tf_op jit(solution)/shard_map/ppermute | solution.py:551
  41.9 4.9 %collective-permute-start.8 = (f32[24,8,128]{2,1,0:T(8,128)S(1)}, f32[24,8,128]{2,1,0:T(8,128)S(1)}, u32[]{:S(2)}, u32[]{:S(2)}) collective-permute-start(f32[24,8,128]{2,1,0:T(8,128)S(1)} %get-tuple-element.39), channel_id=1, source_target_pairs={{0,6},{1,7},{2,4},{3,5},{4,2},{5,3},{6,0},{7,1},{8,14},{9,15},{10,... | collective-permute-start | bytes 294920 | tf_op jit(solution)/shard_map/ppermute | solution.py:552
  44.3 2.5 %collective-permute-start.10 = (f32[24,8,128]{2,1,0:T(8,128)S(1)}, f32[24,8,128]{2,1,0:T(8,128)S(1)}, u32[]{:S(2)}, u32[]{:S(2)}) collective-permute-start(f32[24,8,128]{2,1,0:T(8,128)S(1)} %collective-permute-done.9.far_ref), channel_id=1, source_target_pairs={{0,1},{1,0},{2,3},{3,2},{4,5},{5,4},{6,7},{7,6},{8,9},{9,8},{10,11... | collective-permute-start | bytes 294920 | tf_op jit(solution)/shard_map/ppermute | solution.py:553

commit v8 on v6

--- a/solution.py
+++ b/solution.py
@@ -25,7 +25,7 @@
 LANES = ATOMS * BZ
 SPAN = CX + BX - 1
 PAIRS = NPROJ * BX
-TILE_Y, TILE_POT, TILE_P, TILE_META, TILES = 0, 24, 36, 84, 88
+TILE_Y, TILE_POT, TILE_P, TILE_META, TILES = 0, 24, 30, 78, 82
 ROW_Z, ROW_X0, ROW_Y0 = 0, 1, 2
 
 VMEM = pl.BlockSpec(memory_space=pltpu.VMEM)
@@ -102,7 +102,7 @@
     moves.append((pot_hbm, pot_ref))
     for out, first in ((up_ref, 12), (down_ref, 0)):
         moves.append((y_hbm, out.at[pl.ds(TILE_Y, 24)]))
-        moves.append((pot_hbm.at[pl.ds(first, 12)], out.at[pl.ds(TILE_POT, 12)]))
+        moves.append((pot_hbm.at[pl.ds(first + 6 * core, 6)], out.at[pl.ds(TILE_POT, 6)]))
     for n, (source, target) in enumerate(moves):
         copies.append(pltpu.make_async_copy(source, target, sems.at[2 + n]))
     for copy in copies:
@@ -272,11 +272,17 @@
     return total
 
 
-def potential_plane(p, low_ref, pot_ref, high_ref):
-    source, tile = (
-        (low_ref, TILE_POT + 2 * p) if p < 6 else (pot_ref, 2 * (p - 6)) if p < 18 else (high_ref, TILE_POT + 2 * (p - 18))
-    )
-    return source[tile : tile + 2].reshape(NY, NZ)
+def own_potential(p, pot_ref):
+    return pot_ref[2 * (p - 6) : 2 * (p - 6) + 2].reshape(NY, NZ)
+
+
+def edge_potential(p, low_refs, high_refs):
+    mine, other = low_refs if p < 6 else high_refs
+    plane = p if p < 6 else p - 18
+    tile = TILE_POT + 2 * (plane % 3)
+    upper = (lax.axis_index("band") % 2).astype(jnp.float32)
+    share = upper if plane >= 3 else 1.0 - upper
+    return (mine[tile : tile + 2] * share + other[tile : tile + 2] * (1.0 - share)).reshape(NY, NZ)
 
 
 def clear(boxed):
@@ -310,7 +316,7 @@
     local[...] = along_z(field2, slice(96, 480), zst_ref).reshape(24, NY, NZ)
     for p in range(24):
         laplace = stencil_plane(padded, p + 6) + local[p]
-        pot = potential_plane(p, low_ref, pot_ref, high_ref)
+        pot = own_potential(p, pot_ref) if 6 <= p < 18 else 0.0
         local[p] = (-0.5 * laplace + (pot - CENTER) * padded[p + 6, 8:24, :]) * (1.0 / HALF)
     boxes.wait()
     contributions(1, read_windows(1, gathered, boxes), laid(up_ref, table_ref), placed, boxes, sums_ref[...])
@@ -333,7 +339,7 @@
     for p in range(12):
         here = padded1[p + 6, 8:24, :]
         laplace = stencil_plane(padded1, p + 6) + local[p]
-        pot = potential_plane(p + 6, None, pot_ref, None)
+        pot = own_potential(p + 6, pot_ref)
         local[p] = -0.5 * laplace + (pot - CENTER) * here
     nonlocal_[0:12] = spread_group(1, 0, 12, placed, backs[1])
     nonlocal_[0:5] += spread_group(0, 12, 5, placed, backs[0])
@@ -359,7 +365,12 @@
     nonlocal_[11:18] = jnp.zeros((7, NY, NZ), jnp.float32)
     nonlocal_[18:24] = spread_group(2, 0, 6, placed, backs[2])
     for p in range(24):
-        updated = partial_ref[p] + nonlocal_[p] * (1.0 / HALF)
+        rest = nonlocal_[p]
+        if not 6 <= p < 18:
+            pot = edge_potential(p, (low_ref, lowsib_ref), (high_ref, highsib_ref))
+            field, tile = (low_ref, TILE_Y + 2 * (p + 6)) if p < 6 else (high_ref, TILE_Y + 2 * (p - 18))
+            rest = rest + pot * field[tile : tile + 2].reshape(NY, NZ)
+        updated = partial_ref[p] + rest * (1.0 / HALF)
         kept_ref[p] = updated
         fill(padded1, p, updated[None])
         field2[16 * p : 16 * p + 16, :] = two_terms(updated, 1)
@@ -385,7 +396,10 @@
     local[...] = along_z(field2, slice(96, 480), zst_ref).reshape(24, NY, NZ)
     for p in range(24):
         laplace = stencil_plane(padded, p + 6) + local[p]
-        pot = potential_plane(p, low_ref, pot_ref, high_ref)
+        if 6 <= p < 18:
+            pot = own_potential(p, pot_ref)
+        else:
+            pot = edge_potential(p, (low_ref, lowsib_ref), (high_ref, highsib_ref))
         applied = -0.5 * laplace + (pot - CENTER) * padded[p + 6, 8:24, :]
         local[p] = applied * (2.0 / HALF) - kept_ref[p]
     boxes.wait()

time: 45.5 us -> 45.5 us (level)
  Pallas kernels: 10.1 us -> 10.6 us
  waiting for transfers between devices: 12.4 us -> 11.9 us
    ppermute x1, waiting for transfers between devices: 7.49 us -> 6.97 us  [shards(): low = lax.ppermute(up, 'dom', ring('dom', 1))]
    pallas_call x9, Pallas kernels: 10.1 us -> 10.6 us  [call(): pl.pallas_call(kernel, out_shape=outs, in_specs=ins, out_specs=out_specs...]
where the time goes in v8:
time: 45.5 us; the launch traced here: 45.4 us
  starting transfers between devices  21.5 us (47%)
  waiting for transfers between devices  11.9 us (26%)
  Pallas kernels  10.6 us (23%)
  between operations  1.37 us (3%)
    pallas_call x9, Pallas kernels, call(): pl.pallas_call(kernel, out_shape=outs, in_specs=ins, out_specs=out_specs...  10.6 us
    ppermute x1, waiting for transfers between devices, shards(): low = lax.ppermute(up, 'dom', ring('dom', 1))  6.97 us
    ppermute x1, starting transfers between devices, shards(): high = lax.ppermute(down, 'dom', ring('dom', -1))  6.65 us
    ppermute x1, starting transfers between devices, shards(): high_y = lax.ppermute(second, 'dom', ring('dom', -1))  4.93 us
    ppermute x1, starting transfers between devices, shards(): far = lax.ppermute(fourth, 'band', meet('band', 4))  2.94 us
    ppermute x1, waiting for transfers between devices, shards(): low_y = lax.ppermute(second, 'dom', ring('dom', 1))  2.4 us
    ppermute x1, starting transfers between devices, shards(): low = lax.ppermute(up, 'dom', ring('dom', 1))  2.12 us
    ppermute x1, waiting for transfers between devices, shards(): far = lax.ppermute(fourth, 'band', meet('band', 4))  1.59 us
  transfers between devices with their start and end apart: 11, of which 4 were waited for; matrix products, arithmetic and copies ran while one was open for 0% of the time, Pallas kernels for 7%

profile of v8, /device:TPU:1, one launch (start us, length us, event | category | flops | bytes accessed | tf_op | source)
XLA Modules:
  0.0 45.4 jit_solution(4922938357474365410)
XLA Ops:
  1.3 1.4 %pack.1 = (f32[82,8,128]{2,1,0:T(8,128)S(1)}, f32[82,8,128]{2,1,0:T(8,128)S(1)}, f32[24,8,128]{2,1,0:T(8,128)S(1)}, f32[48,8,128]{2,1,0:T(8,128)S(1)}) custom-call(f32[24,8,128]{2,1,0:T(8,128)} %bitcast.8, f32[24,8,128]{2,1,0:T(8,128)} %bitcast.9, f32[32,8,384]{2,1,0:T(8,128)} %proj_hbm.1, f32[8,32]{1,0:T(8,128)} %bitcast.10, s32[3,32]{1,0:T(4,128)} %bitcast.11, ...), custom_call_target="tpu_custom_call" | custom-call | flops 1000000 | bytes 2000000 | tf_op jit(solution)/shard_map/pack/pallas_call | solution.py:41
  2.7 0.0 copy-start
  2.7 2.1 %collective-permute-start.1 = (f32[82,8,128]{2,1,0:T(8,128)S(1)}, f32[82,8,128]{2,1,0:T(8,128)S(1)}, u32[]{:S(2)}, u32[]{:S(2)}) collective-permute-start(f32[82,8,128]{2,1,0:T(8,128)S(1)} %get-tuple-element.22), channel_id=1, source_target_pairs={{0,8},{8,16},{16,24},{24,32},{32,40},{40,48},{48,56},{56,64},{64,7... | collective-permute-start | bytes 1007624 | tf_op jit(solution)/shard_map/ppermute | solution.py:482
  4.8 6.6 %collective-permute-start = (f32[82,8,128]{2,1,0:T(8,128)S(1)}, f32[82,8,128]{2,1,0:T(8,128)S(1)}, u32[]{:S(2)}, u32[]{:S(2)}) collective-permute-start(f32[82,8,128]{2,1,0:T(8,128)S(1)} %get-tuple-element.21.up_ref), channel_id=1, source_target_pairs={{0,248},{8,0},{16,8},{24,16},{32,24},{40,32},{48,40},{56,48},{64,5... | collective-permute-start | bytes 1007624 | tf_op jit(solution)/shard_map/ppermute | solution.py:483
  11.5 0.5 %prepare.1 = (f32[48,8,128]{2,1,0:T(8,128)S(1)}, bf16[384,128]{1,0:T(8,128)(2,1)S(1)}, bf16[256,256]{1,0:T(8,128)(2,1)S(1)}, bf16[256,256]{1,0:T(8,128)(2,1)S(1)...) custom-call(f32[48,8,128]{2,1,0:T(8,128)S(1)} %get-tuple-element.24.rest_ref, ...), custom_call_target="tpu_custom_call" | custom-call | flops 1000000 | bytes 2000000 | tf_op jit(solution)/shard_map/prepare/pallas_call | solution.py:41
  12.0 7.0 %collective-permute-done.1.low_ref = f32[82,8,128]{2,1,0:T(8,128)S(1)} collective-permute-done((f32[82,8,128]{2,1,0:T(8,128)S(1)}, f32[82,8,128]{2,1,0:T(8,128)S(1)}, u32[]{:S(2)}, u32[]{:S(2)}) %collective-permute-start.1) | collective-permute-done | bytes 335904 | tf_op jit(solution)/shard_map/ppermute | solution.py:482
  19.0 1.2 %collective-permute-start.3 = (f32[82,8,128]{2,1,0:T(8,128)S(1)}, f32[82,8,128]{2,1,0:T(8,128)S(1)}, u32[]{:S(2)}, u32[]{:S(2)}) collective-permute-start(f32[82,8,128]{2,1,0:T(8,128)S(1)} %collective-permute-done.1.low_ref), channel_id=1, source_target_pairs={{0,1},{1,0},{2,3},{3,2},{4,5},{5,4},{6,7},{7,6},{8,9},{9,8},{10,11... | collective-permute-start | bytes 1007624 | tf_op jit(solution)/shard_map/ppermute | solution.py:500
  20.2 0.0 collective-permute-done.high_ref
  20.2 0.0 collective-permute-start.2
  20.3 2.0 %head.1 = (f32[2,6,2,8,128]{4,3,2,1,0:T(8,128)S(1)}, f32[24,16,128]{2,1,0:T(8,128)S(1)}, bf16[2,256,256]{2,1,0:T(8,128)(2,1)S(1)}, bf16[2,512,128]{2,1,0:T(8,128)(2,1)S(1)}) custom-call(f32[82,8,128]{2,1,0:T(8,128)S(1)} %get-tuple-element.21.up_ref, f32[82,8,128]{2,1,0:T(8,128)S(1)} %collective-permute-done.high_ref, ...), custom_call_target="tpu_custom_call" | custom-call | flops 10000000000 | bytes 2000000 | tf_op jit(solution)/shard_map/head/pallas_call | solution.py:41
  22.3 2.3 %tail.1 = (f32[24,8,128]{2,1,0:T(8,128)S(1)}, f32[24,16,128]{2,1,0:T(8,128)S(1)}) custom-call(f32[82,8,128]{2,1,0:T(8,128)S(1)} %get-tuple-element.21.up_ref, f32[82,8,128]{2,1,0:T(8,128)S(1)} %collective-permute-done.high_ref, f32[82,8,128]{2,1,0:T(8,128)S(1)} %collective-permute-done.1.low_ref, f32[24,8,128]{2,1,0:T(8,128)S(1)} %get-tuple-element.23.pot_ref, ...), custom_call_target="tpu_custom_call" | custom-call | flops 1000000 | bytes 2000000 | tf_op jit(solution)/shard_map/tail/pallas_call | solution.py:41
  24.6 0.1 collective-permute-start.5
  24.7 4.9 %collective-permute-start.4 = (f32[24,8,128]{2,1,0:T(8,128)S(1)}, f32[24,8,128]{2,1,0:T(8,128)S(1)}, u32[]{:S(2)}, u32[]{:S(2)}) collective-permute-start(f32[24,8,128]{2,1,0:T(8,128)S(1)} %get-tuple-element.35.mid_ref), channel_id=1, source_target_pairs={{0,248},{8,0},{16,8},{24,16},{32,24},{40,32},{48,40},{56,48},{64,5... | collective-permute-start | bytes 294920 | tf_op jit(solution)/shard_map/ppermute | solution.py:525
  29.6 2.4 %collective-permute-done.5.lowy_ref = f32[24,8,128]{2,1,0:T(8,128)S(1)} collective-permute-done((f32[24,8,128]{2,1,0:T(8,128)S(1)}, f32[24,8,128]{2,1,0:T(8,128)S(1)}, u32[]{:S(2)}, u32[]{:S(2)}) %collective-permute-start.5) | collective-permute-done | bytes 98336 | tf_op jit(solution)/shard_map/ppermute | solution.py:524
  32.0 3.0 %last.1.own_ref = f32[24,8,128]{2,1,0:T(8,128)S(1)} custom-call(f32[82,8,128]{2,1,0:T(8,128)S(1)} %get-tuple-element.21.up_ref, f32[82,8,128]{2,1,0:T(8,128)S(1)} %collective-permute-done.high_ref, f32[82,8,128]{2,1,0:T(8,128)S(1)} %collective-permute-done.1.low_ref, f32[24,8,128]{2,1,0:T(8,128)S(1)} %get-tuple-element.23.pot_ref, ...), custom_call_target="tpu_custom_call" | custom-call | flops 1000000 | bytes 2000000 | tf_op jit(solution)/shard_map/last/pallas_call | solution.py:41
  35.0 1.4 %collective-permute-start.6 = (f32[24,8,128]{2,1,0:T(8,128)S(1)}, f32[24,8,128]{2,1,0:T(8,128)S(1)}, u32[]{:S(2)}, u32[]{:S(2)}) collective-permute-start(f32[24,8,128]{2,1,0:T(8,128)S(1)} %last.1.own_ref), channel_id=1, source_target_pairs={{0,1},{1,0},{2,3},{3,2},{4,5},{5,4},{6,7},{7,6},{8,9},{9,8},{10,11... | collective-permute-start | bytes 294920 | tf_op jit(solution)/shard_map/ppermute | solution.py:535
  36.3 2.9 %collective-permute-start.9 = (f32[24,8,128]{2,1,0:T(8,128)S(1)}, f32[24,8,128]{2,1,0:T(8,128)S(1)}, u32[]{:S(2)}, u32[]{:S(2)}) collective-permute-start(f32[24,8,128]{2,1,0:T(8,128)S(1)} %last.1.own_ref), channel_id=1, source_target_pairs={{0,4},{1,5},{2,6},{3,7},{4,0},{5,1},{6,2},{7,3},{8,12},{9,13},{10,... | collective-permute-start | bytes 294920 | tf_op jit(solution)/shard_map/ppermute | solution.py:534
  39.3 0.5 %collective-permute-start.7 = (f32[24,8,128]{2,1,0:T(8,128)S(1)}, f32[24,8,128]{2,1,0:T(8,128)S(1)}, u32[]{:S(2)}, u32[]{:S(2)}) collective-permute-start(f32[24,8,128]{2,1,0:T(8,128)S(1)} %get-tuple-element.38), channel_id=1, source_target_pairs={{0,2},{1,3},{2,0},{3,1},{4,6},{5,7},{6,4},{7,5},{8,10},{9,11},{10,... | collective-permute-start | bytes 294920 | tf_op jit(solution)/shard_map/ppermute | solution.py:538
  39.8 0.8 %collective-permute-start.8 = (f32[24,8,128]{2,1,0:T(8,128)S(1)}, f32[24,8,128]{2,1,0:T(8,128)S(1)}, u32[]{:S(2)}, u32[]{:S(2)}) collective-permute-start(f32[24,8,128]{2,1,0:T(8,128)S(1)} %get-tuple-element.39), channel_id=1, source_target_pairs={{0,6},{1,7},{2,4},{3,5},{4,2},{5,3},{6,0},{7,1},{8,14},{9,15},{10,... | collective-permute-start | bytes 294920 | tf_op jit(solution)/shard_map/ppermute | solution.py:539
  40.6 1.6 %collective-permute-done.9.far_ref = f32[24,8,128]{2,1,0:T(8,128)S(1)} collective-permute-done((f32[24,8,128]{2,1,0:T(8,128)S(1)}, f32[24,8,128]{2,1,0:T(8,128)S(1)}, u32[]{:S(2)}, u32[]{:S(2)}) %collective-permute-start.9) | collective-permute-done | bytes 98336 | tf_op jit(solution)/shard_map/ppermute | solution.py:534
  42.2 0.9 %collective-permute-start.10 = (f32[24,8,128]{2,1,0:T(8,128)S(1)}, f32[24,8,128]{2,1,0:T(8,128)S(1)}, u32[]{:S(2)}, u32[]{:S(2)}) collective-permute-start(f32[24,8,128]{2,1,0:T(8,128)S(1)} %collective-permute-done.9.far_ref), channel_id=1, source_target_pairs={{0,1},{1,0},{2,3},{3,2},{4,5},{5,4},{6,7},{7,6},{8,9},{9,8},{10,11... | collective-permute-start | bytes 294920 | tf_op jit(solution)/shard_map/ppermute | solution.py:540
  43.1 0.6 %store.1 = f32[24,8,128]{2,1,0:T(8,128)} custom-call(f32[24,8,128]{2,1,0:T(8,128)S(1)} %last.1.own_ref), custom_call_target="tpu_custom_call" | custom-call | tf_op jit(solution)/shard_map/store/pallas_call | solution.py:41
  43.7 0.9 %collective-permute-done.7.one_ref = f32[24,8,128]{2,1,0:T(8,128)S(1)} collective-permute-done((f32[24,8,128]{2,1,0:T(8,128)S(1)}, f32[24,8,128]{2,1,0:T(8,128)S(1)}, u32[]{:S(2)}, u32[]{:S(2)}) %collective-permute-start.7) | collective-permute-done | bytes 98336 | tf_op jit(solution)/shard_map/ppermute | solution.py:538
  44.7 0.7 %total.1 = f32[24,8,128]{2,1,0:T(8,128)} custom-call(f32[8,8,128]{2,1,0:T(8,128)S(1)} %get-tuple-element.36.factors_ref, f32[24,8,128]{2,1,0:T(8,128)S(1)} %most.1.most_ref, f32[24,8,128]{2,1,0:T(8,128)S(1)} %collective-permute-done.10.farsib_ref), custom_call_target="tpu_custom_call" | custom-call | flops 1000000 | bytes 2000000 | tf_op jit(solution)/shard_map/total/pallas_call | solution.py:41
  (9 shorter events, 0.1 us)
Async XLA Ops:
  2.7 8.8 %copy-start = (f32[8,8]{1,0:T(8,128)S(1)}, f32[8,8]{1,0:T(8,128)}, u32[]{:S(2)}) copy-start(f32[8,8]{1,0:T(8,128)} %ritz_ref.1) | copy-start | bytes 772
  2.7 16.3 %collective-permute-start.1 = (f32[82,8,128]{2,1,0:T(8,128)S(1)}, f32[82,8,128]{2,1,0:T(8,128)S(1)}, u32[]{:S(2)}, u32[]{:S(2)}) collective-permute-start(f32[82,8,128]{2,1,0:T(8,128)S(1)} %get-tuple-element.22), channel_id=1, source_target_pairs={{0,8},{8,16},{16,24},{24,32},{32,40},{40,48},{48,56},{56,64},{64,7... | collective-permute-start | bytes 1007624 | tf_op jit(solution)/shard_map/ppermute | solution.py:482
  4.8 15.4 %collective-permute-start = (f32[82,8,128]{2,1,0:T(8,128)S(1)}, f32[82,8,128]{2,1,0:T(8,128)S(1)}, u32[]{:S(2)}, u32[]{:S(2)}) collective-permute-start(f32[82,8,128]{2,1,0:T(8,128)S(1)} %get-tuple-element.21.up_ref), channel_id=1, source_target_pairs={{0,248},{8,0},{16,8},{24,16},{32,24},{40,32},{48,40},{56,48},{64,5... | collective-permute-start | bytes 1007624 | tf_op jit(solution)/shard_map/ppermute | solution.py:483
  19.0 3.3 %collective-permute-start.3 = (f32[82,8,128]{2,1,0:T(8,128)S(1)}, f32[82,8,128]{2,1,0:T(8,128)S(1)}, u32[]{:S(2)}, u32[]{:S(2)}) collective-permute-start(f32[82,8,128]{2,1,0:T(8,128)S(1)} %collective-permute-done.1.low_ref), channel_id=1, source_target_pairs={{0,1},{1,0},{2,3},{3,2},{4,5},{5,4},{6,7},{7,6},{8,9},{9,8},{10,11... | collective-permute-start | bytes 1007624 | tf_op jit(solution)/shard_map/ppermute | solution.py:500
  20.2 2.0 %collective-permute-start.2 = (f32[82,8,128]{2,1,0:T(8,128)S(1)}, f32[82,8,128]{2,1,0:T(8,128)S(1)}, u32[]{:S(2)}, u32[]{:S(2)}) collective-permute-start(f32[82,8,128]{2,1,0:T(8,128)S(1)} %collective-permute-done.high_ref), channel_id=1, source_target_pairs={{0,1},{1,0},{2,3},{3,2},{4,5},{5,4},{6,7},{7,6},{8,9},{9,8},{10,11... | collective-permute-start | bytes 1007624 | tf_op jit(solution)/shard_map/ppermute | solution.py:499
  24.6 7.4 %collective-permute-start.5 = (f32[24,8,128]{2,1,0:T(8,128)S(1)}, f32[24,8,128]{2,1,0:T(8,128)S(1)}, u32[]{:S(2)}, u32[]{:S(2)}) collective-permute-start(f32[24,8,128]{2,1,0:T(8,128)S(1)} %get-tuple-element.35.mid_ref), channel_id=1, source_target_pairs={{0,8},{8,16},{16,24},{24,32},{32,40},{40,48},{48,56},{56,64},{64,7... | collective-permute-start | bytes 294920 | tf_op jit(solution)/shard_map/ppermute | solution.py:524
  24.7 7.3 %collective-permute-start.4 = (f32[24,8,128]{2,1,0:T(8,128)S(1)}, f32[24,8,128]{2,1,0:T(8,128)S(1)}, u32[]{:S(2)}, u32[]{:S(2)}) collective-permute-start(f32[24,8,128]{2,1,0:T(8,128)S(1)} %get-tuple-element.35.mid_ref), channel_id=1, source_target_pairs={{0,248},{8,0},{16,8},{24,16},{32,24},{40,32},{48,40},{56,48},{64,5... | collective-permute-start | bytes 294920 | tf_op jit(solution)/shard_map/ppermute | solution.py:525
  35.0 4.3 %collective-permute-start.6 = (f32[24,8,128]{2,1,0:T(8,128)S(1)}, f32[24,8,128]{2,1,0:T(8,128)S(1)}, u32[]{:S(2)}, u32[]{:S(2)}) collective-permute-start(f32[24,8,128]{2,1,0:T(8,128)S(1)} %last.1.own_ref), channel_id=1, source_target_pairs={{0,1},{1,0},{2,3},{3,2},{4,5},{5,4},{6,7},{7,6},{8,9},{9,8},{10,11... | collective-permute-start | bytes 294920 | tf_op jit(solution)/shard_map/ppermute | solution.py:535
  36.3 5.9 %collective-permute-start.9 = (f32[24,8,128]{2,1,0:T(8,128)S(1)}, f32[24,8,128]{2,1,0:T(8,128)S(1)}, u32[]{:S(2)}, u32[]{:S(2)}) collective-permute-start(f32[24,8,128]{2,1,0:T(8,128)S(1)} %last.1.own_ref), channel_id=1, source_target_pairs={{0,4},{1,5},{2,6},{3,7},{4,0},{5,1},{6,2},{7,3},{8,12},{9,13},{10,... | collective-permute-start | bytes 294920 | tf_op jit(solution)/shard_map/ppermute | solution.py:534
  39.3 5.3 %collective-permute-start.7 = (f32[24,8,128]{2,1,0:T(8,128)S(1)}, f32[24,8,128]{2,1,0:T(8,128)S(1)}, u32[]{:S(2)}, u32[]{:S(2)}) collective-permute-start(f32[24,8,128]{2,1,0:T(8,128)S(1)} %get-tuple-element.38), channel_id=1, source_target_pairs={{0,2},{1,3},{2,0},{3,1},{4,6},{5,7},{6,4},{7,5},{8,10},{9,11},{10,... | collective-permute-start | bytes 294920 | tf_op jit(solution)/shard_map/ppermute | solution.py:538
  39.8 4.8 %collective-permute-start.8 = (f32[24,8,128]{2,1,0:T(8,128)S(1)}, f32[24,8,128]{2,1,0:T(8,128)S(1)}, u32[]{:S(2)}, u32[]{:S(2)}) collective-permute-start(f32[24,8,128]{2,1,0:T(8,128)S(1)} %get-tuple-element.39), channel_id=1, source_target_pairs={{0,6},{1,7},{2,4},{3,5},{4,2},{5,3},{6,0},{7,1},{8,14},{9,15},{10,... | collective-permute-start | bytes 294920 | tf_op jit(solution)/shard_map/ppermute | solution.py:539
  42.2 2.5 %collective-permute-start.10 = (f32[24,8,128]{2,1,0:T(8,128)S(1)}, f32[24,8,128]{2,1,0:T(8,128)S(1)}, u32[]{:S(2)}, u32[]{:S(2)}) collective-permute-start(f32[24,8,128]{2,1,0:T(8,128)S(1)} %collective-permute-done.9.far_ref), channel_id=1, source_target_pairs={{0,1},{1,0},{2,3},{3,2},{4,5},{5,4},{6,7},{7,6},{8,9},{9,8},{10,11... | collective-permute-start | bytes 294920 | tf_op jit(solution)/shard_map/ppermute | solution.py:540

commit v9 on v8

--- a/solution.py
+++ b/solution.py
@@ -276,13 +276,18 @@
     return pot_ref[2 * (p - 6) : 2 * (p - 6) + 2].reshape(NY, NZ)
 
 
-def edge_potential(p, low_refs, high_refs):
-    mine, other = low_refs if p < 6 else high_refs
-    plane = p if p < 6 else p - 18
-    tile = TILE_POT + 2 * (plane % 3)
+def edge_potential(sides, edge_ref):
     upper = (lax.axis_index("band") % 2).astype(jnp.float32)
-    share = upper if plane >= 3 else 1.0 - upper
-    return (mine[tile : tile + 2] * share + other[tile : tile + 2] * (1.0 - share)).reshape(NY, NZ)
+    upper = jnp.full((6, 8, 128), upper, jnp.float32)
+    for n, (mine, other) in enumerate(sides):
+        mine, other = mine[TILE_POT : TILE_POT + 6], other[TILE_POT : TILE_POT + 6]
+        edge_ref[n, 0:6] = mine * (1.0 - upper) + other * upper
+        edge_ref[n, 6:12] = mine * upper + other * (1.0 - upper)
+
+
+def edge_plane(p, edge_ref):
+    n, tile = (0, 2 * p) if p < 6 else (1, 2 * (p - 18))
+    return edge_ref[n, tile : tile + 2].reshape(NY, NZ)
 
 
 def clear(boxed):
@@ -349,12 +354,13 @@
 
 def tail_kernel(up_ref, high_ref, low_ref, pot_ref, table_ref, zst_ref, sums_ref, hot_ref, back_ref,
                 values_ref, partial_ref, hots_ref, backs_ref, highsib_ref, lowsib_ref,
-                out_ref, kept_ref,
+                out_ref, kept_ref, edge_ref,
                 low_xy, own_xy, high_xy, padded1, field2, gathered, placed, local, nonlocal_, sems):
     boxes = Boxes((low_ref, up_ref, high_ref), (low_xy, own_xy, high_xy), sems)
     clear(placed)
     gathered[0][:, 0:6] = jnp.zeros((2, 6, 24, 128), jnp.float32)
     tables = (laid(low_ref, lowsib_ref), laid(up_ref, table_ref), laid(high_ref, highsib_ref))
+    edge_potential(((low_ref, lowsib_ref), (high_ref, highsib_ref)), edge_ref)
     hots, backs = (hots_ref.at[0], hot_ref), (backs_ref.at[0], back_ref, backs_ref.at[1])
     boxes.wait()
     sums = sums_ref[...]
@@ -367,7 +373,7 @@
     for p in range(24):
         rest = nonlocal_[p]
         if not 6 <= p < 18:
-            pot = edge_potential(p, (low_ref, lowsib_ref), (high_ref, highsib_ref))
+            pot = edge_plane(p, edge_ref)
             field, tile = (low_ref, TILE_Y + 2 * (p + 6)) if p < 6 else (high_ref, TILE_Y + 2 * (p - 18))
             rest = rest + pot * field[tile : tile + 2].reshape(NY, NZ)
         updated = partial_ref[p] + rest * (1.0 / HALF)
@@ -380,7 +386,7 @@
 
 
 def last_kernel(up_ref, high_ref, low_ref, pot_ref, table_ref, zst_ref, sums_ref, hot_ref, back_ref,
-                kept_ref, hots_ref, backs_ref, highsib_ref, lowsib_ref,
+                kept_ref, edge_ref, hots_ref, backs_ref, highsib_ref, lowsib_ref,
                 mid_ref, highy_ref, lowy_ref,
                 out_ref,
                 low_xy, own_xy, high_xy, padded, padded1, field2, gathered, placed, local, nonlocal_, sems):
@@ -399,7 +405,7 @@
         if 6 <= p < 18:
             pot = own_potential(p, pot_ref)
         else:
-            pot = edge_potential(p, (low_ref, lowsib_ref), (high_ref, highsib_ref))
+            pot = edge_plane(p, edge_ref)
         applied = -0.5 * laplace + (pot - CENTER) * padded[p + 6, 8:24, :]
         local[p] = applied * (2.0 / HALF) - kept_ref[p]
     boxes.wait()
@@ -513,9 +519,9 @@
         XY + [PADDED, FIELD2, BOXED, BOXED, PLANES, COPIES],
         flops=10_000_000_000,
     )
-    second, first = call(
+    second, first, edge = call(
         tail_kernel,
-        [shape(24, 8, 128), shape(24, NY, NZ)],
+        [shape(24, 8, 128), shape(24, NY, NZ), shape(2, 12, 8, 128)],
         [VMEM] * 15,
         common + (values, partial, hots, backs, highsib, lowsib),
         "tail",
@@ -526,8 +532,8 @@
     (fourth,) = call(
         last_kernel,
         [shape(24, 8, 128)],
-        [VMEM] * 17,
-        common + (first, hots, backs, highsib, lowsib, second, high_y, low_y),
+        [VMEM] * 18,
+        common + (first, edge, hots, backs, highsib, lowsib, second, high_y, low_y),
         "last",
         XY + [PADDED, PADDED1, FIELD2, BOXED, BOXED, PLANES, PLANES, COPIES],
     )

time: 45.5 us -> 45.3 us (level)
  no operation moved by 1% of the time
where the time goes in v9:
time: 45.3 us; the launch traced here: 45.2 us
  starting transfers between devices  21.5 us (47%)
  waiting for transfers between devices  11.9 us (26%)
  Pallas kernels  10.4 us (23%)
  between operations  1.37 us (3%)
    pallas_call x9, Pallas kernels, call(): pl.pallas_call(kernel, out_shape=outs, in_specs=ins, out_specs=out_specs...  10.4 us
    ppermute x1, waiting for transfers between devices, shards(): low = lax.ppermute(up, 'dom', ring('dom', 1))  6.97 us
    ppermute x1, starting transfers between devices, shards(): high = lax.ppermute(down, 'dom', ring('dom', -1))  6.65 us
    ppermute x1, starting transfers between devices, shards(): high_y = lax.ppermute(second, 'dom', ring('dom', -1))  4.94 us
    ppermute x1, starting transfers between devices, shards(): far = lax.ppermute(fourth, 'band', meet('band', 4))  2.93 us
    ppermute x1, waiting for transfers between devices, shards(): low_y = lax.ppermute(second, 'dom', ring('dom', 1))  2.39 us
    ppermute x1, starting transfers between devices, shards(): low = lax.ppermute(up, 'dom', ring('dom', 1))  2.12 us
    ppermute x1, waiting for transfers between devices, shards(): far = lax.ppermute(fourth, 'band', meet('band', 4))  1.59 us
  transfers between devices with their start and end apart: 11, of which 4 were waited for; matrix products, arithmetic and copies ran while one was open for 0% of the time, Pallas kernels for 7%

profile of v9, /device:TPU:1, one launch (start us, length us, event | category | flops | bytes accessed | tf_op | source)
XLA Modules:
  0.0 45.2 jit_solution(16709071985884997865)
XLA Ops:
  1.3 1.4 %pack.1 = (f32[82,8,128]{2,1,0:T(8,128)S(1)}, f32[82,8,128]{2,1,0:T(8,128)S(1)}, f32[24,8,128]{2,1,0:T(8,128)S(1)}, f32[48,8,128]{2,1,0:T(8,128)S(1)}) custom-call(f32[24,8,128]{2,1,0:T(8,128)} %bitcast.8, f32[24,8,128]{2,1,0:T(8,128)} %bitcast.9, f32[32,8,384]{2,1,0:T(8,128)} %proj_hbm.1, f32[8,32]{1,0:T(8,128)} %bitcast.10, s32[3,32]{1,0:T(4,128)} %bitcast.11, ...), custom_call_target="tpu_custom_call" | custom-call | flops 1000000 | bytes 2000000 | tf_op jit(solution)/shard_map/pack/pallas_call | solution.py:41
  2.7 0.0 copy-start
  2.7 2.1 %collective-permute-start.1 = (f32[82,8,128]{2,1,0:T(8,128)S(1)}, f32[82,8,128]{2,1,0:T(8,128)S(1)}, u32[]{:S(2)}, u32[]{:S(2)}) collective-permute-start(f32[82,8,128]{2,1,0:T(8,128)S(1)} %get-tuple-element.23), channel_id=1, source_target_pairs={{0,8},{8,16},{16,24},{24,32},{32,40},{40,48},{48,56},{56,64},{64,7... | collective-permute-start | bytes 1007624 | tf_op jit(solution)/shard_map/ppermute | solution.py:488
  4.8 6.6 %collective-permute-start = (f32[82,8,128]{2,1,0:T(8,128)S(1)}, f32[82,8,128]{2,1,0:T(8,128)S(1)}, u32[]{:S(2)}, u32[]{:S(2)}) collective-permute-start(f32[82,8,128]{2,1,0:T(8,128)S(1)} %get-tuple-element.22.up_ref), channel_id=1, source_target_pairs={{0,248},{8,0},{16,8},{24,16},{32,24},{40,32},{48,40},{56,48},{64,5... | collective-permute-start | bytes 1007624 | tf_op jit(solution)/shard_map/ppermute | solution.py:489
  11.5 0.5 %prepare.1 = (f32[48,8,128]{2,1,0:T(8,128)S(1)}, bf16[384,128]{1,0:T(8,128)(2,1)S(1)}, bf16[256,256]{1,0:T(8,128)(2,1)S(1)}, bf16[256,256]{1,0:T(8,128)(2,1)S(1)...) custom-call(f32[48,8,128]{2,1,0:T(8,128)S(1)} %get-tuple-element.25.rest_ref, ...), custom_call_target="tpu_custom_call" | custom-call | flops 1000000 | bytes 2000000 | tf_op jit(solution)/shard_map/prepare/pallas_call | solution.py:41
  12.0 7.0 %collective-permute-done.1.low_ref = f32[82,8,128]{2,1,0:T(8,128)S(1)} collective-permute-done((f32[82,8,128]{2,1,0:T(8,128)S(1)}, f32[82,8,128]{2,1,0:T(8,128)S(1)}, u32[]{:S(2)}, u32[]{:S(2)}) %collective-permute-start.1) | collective-permute-done | bytes 335904 | tf_op jit(solution)/shard_map/ppermute | solution.py:488
  19.0 1.2 %collective-permute-start.3 = (f32[82,8,128]{2,1,0:T(8,128)S(1)}, f32[82,8,128]{2,1,0:T(8,128)S(1)}, u32[]{:S(2)}, u32[]{:S(2)}) collective-permute-start(f32[82,8,128]{2,1,0:T(8,128)S(1)} %collective-permute-done.1.low_ref), channel_id=1, source_target_pairs={{0,1},{1,0},{2,3},{3,2},{4,5},{5,4},{6,7},{7,6},{8,9},{9,8},{10,11... | collective-permute-start | bytes 1007624 | tf_op jit(solution)/shard_map/ppermute | solution.py:506
  20.2 0.0 collective-permute-start.2
  20.3 2.0 %head.1 = (f32[2,6,2,8,128]{4,3,2,1,0:T(8,128)S(1)}, f32[24,16,128]{2,1,0:T(8,128)S(1)}, bf16[2,256,256]{2,1,0:T(8,128)(2,1)S(1)}, bf16[2,512,128]{2,1,0:T(8,128)(2,1)S(1)}) custom-call(f32[82,8,128]{2,1,0:T(8,128)S(1)} %get-tuple-element.22.up_ref, f32[82,8,128]{2,1,0:T(8,128)S(1)} %collective-permute-done.high_ref, ...), custom_call_target="tpu_custom_call" | custom-call | flops 10000000000 | bytes 2000000 | tf_op jit(solution)/shard_map/head/pallas_call | solution.py:41
  22.3 0.0 collective-permute-done.2.highsib_ref
  22.3 2.3 %tail.1 = (f32[24,8,128]{2,1,0:T(8,128)S(1)}, f32[24,16,128]{2,1,0:T(8,128)S(1)}, f32[2,12,8,128]{3,2,1,0:T(8,128)S(1)}) custom-call(f32[82,8,128]{2,1,0:T(8,128)S(1)} %get-tuple-element.22.up_ref, f32[82,8,128]{2,1,0:T(8,128)S(1)} %collective-permute-done.high_ref, f32[82,8,128]{2,1,0:T(8,128)S(1)} %collective-permute-done.1.low_ref, ...), custom_call_target="tpu_custom_call" | custom-call | flops 1000000 | bytes 2000000 | tf_op jit(solution)/shard_map/tail/pallas_call | solution.py:41
  24.5 0.1 collective-permute-start.5
  24.6 4.9 %collective-permute-start.4 = (f32[24,8,128]{2,1,0:T(8,128)S(1)}, f32[24,8,128]{2,1,0:T(8,128)S(1)}, u32[]{:S(2)}, u32[]{:S(2)}) collective-permute-start(f32[24,8,128]{2,1,0:T(8,128)S(1)} %get-tuple-element.37.mid_ref), channel_id=1, source_target_pairs={{0,248},{8,0},{16,8},{24,16},{32,24},{40,32},{48,40},{56,48},{64,5... | collective-permute-start | bytes 294920 | tf_op jit(solution)/shard_map/ppermute | solution.py:531
  29.6 2.4 %collective-permute-done.5.lowy_ref = f32[24,8,128]{2,1,0:T(8,128)S(1)} collective-permute-done((f32[24,8,128]{2,1,0:T(8,128)S(1)}, f32[24,8,128]{2,1,0:T(8,128)S(1)}, u32[]{:S(2)}, u32[]{:S(2)}) %collective-permute-start.5) | collective-permute-done | bytes 98336 | tf_op jit(solution)/shard_map/ppermute | solution.py:530
  32.0 2.8 %last.1.own_ref = f32[24,8,128]{2,1,0:T(8,128)S(1)} custom-call(f32[82,8,128]{2,1,0:T(8,128)S(1)} %get-tuple-element.22.up_ref, f32[82,8,128]{2,1,0:T(8,128)S(1)} %collective-permute-done.high_ref, f32[82,8,128]{2,1,0:T(8,128)S(1)} %collective-permute-done.1.low_ref, f32[24,8,128]{2,1,0:T(8,128)S(1)} %get-tuple-element.24.pot_ref, ...), custom_call_target="tpu_custom_call" | custom-call | flops 1000000 | bytes 2000000 | tf_op jit(solution)/shard_map/last/pallas_call | solution.py:41
  34.8 1.4 %collective-permute-start.6 = (f32[24,8,128]{2,1,0:T(8,128)S(1)}, f32[24,8,128]{2,1,0:T(8,128)S(1)}, u32[]{:S(2)}, u32[]{:S(2)}) collective-permute-start(f32[24,8,128]{2,1,0:T(8,128)S(1)} %last.1.own_ref), channel_id=1, source_target_pairs={{0,1},{1,0},{2,3},{3,2},{4,5},{5,4},{6,7},{7,6},{8,9},{9,8},{10,11... | collective-permute-start | bytes 294920 | tf_op jit(solution)/shard_map/ppermute | solution.py:541
  36.2 2.9 %collective-permute-start.9 = (f32[24,8,128]{2,1,0:T(8,128)S(1)}, f32[24,8,128]{2,1,0:T(8,128)S(1)}, u32[]{:S(2)}, u32[]{:S(2)}) collective-permute-start(f32[24,8,128]{2,1,0:T(8,128)S(1)} %last.1.own_ref), channel_id=1, source_target_pairs={{0,4},{1,5},{2,6},{3,7},{4,0},{5,1},{6,2},{7,3},{8,12},{9,13},{10,... | collective-permute-start | bytes 294920 | tf_op jit(solution)/shard_map/ppermute | solution.py:540
  39.1 0.5 %collective-permute-start.7 = (f32[24,8,128]{2,1,0:T(8,128)S(1)}, f32[24,8,128]{2,1,0:T(8,128)S(1)}, u32[]{:S(2)}, u32[]{:S(2)}) collective-permute-start(f32[24,8,128]{2,1,0:T(8,128)S(1)} %get-tuple-element.40), channel_id=1, source_target_pairs={{0,2},{1,3},{2,0},{3,1},{4,6},{5,7},{6,4},{7,5},{8,10},{9,11},{10,... | collective-permute-start | bytes 294920 | tf_op jit(solution)/shard_map/ppermute | solution.py:544
  39.6 0.8 %collective-permute-start.8 = (f32[24,8,128]{2,1,0:T(8,128)S(1)}, f32[24,8,128]{2,1,0:T(8,128)S(1)}, u32[]{:S(2)}, u32[]{:S(2)}) collective-permute-start(f32[24,8,128]{2,1,0:T(8,128)S(1)} %get-tuple-element.41), channel_id=1, source_target_pairs={{0,6},{1,7},{2,4},{3,5},{4,2},{5,3},{6,0},{7,1},{8,14},{9,15},{10,... | collective-permute-start | bytes 294920 | tf_op jit(solution)/shard_map/ppermute | solution.py:545
  40.4 1.6 %collective-permute-done.9.far_ref = f32[24,8,128]{2,1,0:T(8,128)S(1)} collective-permute-done((f32[24,8,128]{2,1,0:T(8,128)S(1)}, f32[24,8,128]{2,1,0:T(8,128)S(1)}, u32[]{:S(2)}, u32[]{:S(2)}) %collective-permute-start.9) | collective-permute-done | bytes 98336 | tf_op jit(solution)/shard_map/ppermute | solution.py:540
  42.0 0.9 %collective-permute-start.10 = (f32[24,8,128]{2,1,0:T(8,128)S(1)}, f32[24,8,128]{2,1,0:T(8,128)S(1)}, u32[]{:S(2)}, u32[]{:S(2)}) collective-permute-start(f32[24,8,128]{2,1,0:T(8,128)S(1)} %collective-permute-done.9.far_ref), channel_id=1, source_target_pairs={{0,1},{1,0},{2,3},{3,2},{4,5},{5,4},{6,7},{7,6},{8,9},{9,8},{10,11... | collective-permute-start | bytes 294920 | tf_op jit(solution)/shard_map/ppermute | solution.py:546
  42.9 0.6 %store.1 = f32[24,8,128]{2,1,0:T(8,128)} custom-call(f32[24,8,128]{2,1,0:T(8,128)S(1)} %last.1.own_ref), custom_call_target="tpu_custom_call" | custom-call | tf_op jit(solution)/shard_map/store/pallas_call | solution.py:41
  43.5 0.9 %collective-permute-done.7.one_ref = f32[24,8,128]{2,1,0:T(8,128)S(1)} collective-permute-done((f32[24,8,128]{2,1,0:T(8,128)S(1)}, f32[24,8,128]{2,1,0:T(8,128)S(1)}, u32[]{:S(2)}, u32[]{:S(2)}) %collective-permute-start.7) | collective-permute-done | bytes 98336 | tf_op jit(solution)/shard_map/ppermute | solution.py:544
  44.5 0.7 %total.1 = f32[24,8,128]{2,1,0:T(8,128)} custom-call(f32[8,8,128]{2,1,0:T(8,128)S(1)} %get-tuple-element.38.factors_ref, f32[24,8,128]{2,1,0:T(8,128)S(1)} %most.1.most_ref, f32[24,8,128]{2,1,0:T(8,128)S(1)} %collective-permute-done.10.farsib_ref), custom_call_target="tpu_custom_call" | custom-call | flops 1000000 | bytes 2000000 | tf_op jit(solution)/shard_map/total/pallas_call | solution.py:41
  (9 shorter events, 0.1 us)
Async XLA Ops:
  2.7 8.8 %copy-start = (f32[8,8]{1,0:T(8,128)S(1)}, f32[8,8]{1,0:T(8,128)}, u32[]{:S(2)}) copy-start(f32[8,8]{1,0:T(8,128)} %ritz_ref.1) | copy-start | bytes 772
  2.7 16.3 %collective-permute-start.1 = (f32[82,8,128]{2,1,0:T(8,128)S(1)}, f32[82,8,128]{2,1,0:T(8,128)S(1)}, u32[]{:S(2)}, u32[]{:S(2)}) collective-permute-start(f32[82,8,128]{2,1,0:T(8,128)S(1)} %get-tuple-element.23), channel_id=1, source_target_pairs={{0,8},{8,16},{16,24},{24,32},{32,40},{40,48},{48,56},{56,64},{64,7... | collective-permute-start | bytes 1007624 | tf_op jit(solution)/shard_map/ppermute | solution.py:488
  4.8 15.4 %collective-permute-start = (f32[82,8,128]{2,1,0:T(8,128)S(1)}, f32[82,8,128]{2,1,0:T(8,128)S(1)}, u32[]{:S(2)}, u32[]{:S(2)}) collective-permute-start(f32[82,8,128]{2,1,0:T(8,128)S(1)} %get-tuple-element.22.up_ref), channel_id=1, source_target_pairs={{0,248},{8,0},{16,8},{24,16},{32,24},{40,32},{48,40},{56,48},{64,5... | collective-permute-start | bytes 1007624 | tf_op jit(solution)/shard_map/ppermute | solution.py:489
  19.0 3.2 %collective-permute-start.3 = (f32[82,8,128]{2,1,0:T(8,128)S(1)}, f32[82,8,128]{2,1,0:T(8,128)S(1)}, u32[]{:S(2)}, u32[]{:S(2)}) collective-permute-start(f32[82,8,128]{2,1,0:T(8,128)S(1)} %collective-permute-done.1.low_ref), channel_id=1, source_target_pairs={{0,1},{1,0},{2,3},{3,2},{4,5},{5,4},{6,7},{7,6},{8,9},{9,8},{10,11... | collective-permute-start | bytes 1007624 | tf_op jit(solution)/shard_map/ppermute | solution.py:506
  20.2 2.0 %collective-permute-start.2 = (f32[82,8,128]{2,1,0:T(8,128)S(1)}, f32[82,8,128]{2,1,0:T(8,128)S(1)}, u32[]{:S(2)}, u32[]{:S(2)}) collective-permute-start(f32[82,8,128]{2,1,0:T(8,128)S(1)} %collective-permute-done.high_ref), channel_id=1, source_target_pairs={{0,1},{1,0},{2,3},{3,2},{4,5},{5,4},{6,7},{7,6},{8,9},{9,8},{10,11... | collective-permute-start | bytes 1007624 | tf_op jit(solution)/shard_map/ppermute | solution.py:505
  24.5 7.4 %collective-permute-start.5 = (f32[24,8,128]{2,1,0:T(8,128)S(1)}, f32[24,8,128]{2,1,0:T(8,128)S(1)}, u32[]{:S(2)}, u32[]{:S(2)}) collective-permute-start(f32[24,8,128]{2,1,0:T(8,128)S(1)} %get-tuple-element.37.mid_ref), channel_id=1, source_target_pairs={{0,8},{8,16},{16,24},{24,32},{32,40},{40,48},{48,56},{56,64},{64,7... | collective-permute-start | bytes 294920 | tf_op jit(solution)/shard_map/ppermute | solution.py:530
  24.6 7.3 %collective-permute-start.4 = (f32[24,8,128]{2,1,0:T(8,128)S(1)}, f32[24,8,128]{2,1,0:T(8,128)S(1)}, u32[]{:S(2)}, u32[]{:S(2)}) collective-permute-start(f32[24,8,128]{2,1,0:T(8,128)S(1)} %get-tuple-element.37.mid_ref), channel_id=1, source_target_pairs={{0,248},{8,0},{16,8},{24,16},{32,24},{40,32},{48,40},{56,48},{64,5... | collective-permute-start | bytes 294920 | tf_op jit(solution)/shard_map/ppermute | solution.py:531
  34.8 4.3 %collective-permute-start.6 = (f32[24,8,128]{2,1,0:T(8,128)S(1)}, f32[24,8,128]{2,1,0:T(8,128)S(1)}, u32[]{:S(2)}, u32[]{:S(2)}) collective-permute-start(f32[24,8,128]{2,1,0:T(8,128)S(1)} %last.1.own_ref), channel_id=1, source_target_pairs={{0,1},{1,0},{2,3},{3,2},{4,5},{5,4},{6,7},{7,6},{8,9},{9,8},{10,11... | collective-permute-start | bytes 294920 | tf_op jit(solution)/shard_map/ppermute | solution.py:541
  36.2 5.9 %collective-permute-start.9 = (f32[24,8,128]{2,1,0:T(8,128)S(1)}, f32[24,8,128]{2,1,0:T(8,128)S(1)}, u32[]{:S(2)}, u32[]{:S(2)}) collective-permute-start(f32[24,8,128]{2,1,0:T(8,128)S(1)} %last.1.own_ref), channel_id=1, source_target_pairs={{0,4},{1,5},{2,6},{3,7},{4,0},{5,1},{6,2},{7,3},{8,12},{9,13},{10,... | collective-permute-start | bytes 294920 | tf_op jit(solution)/shard_map/ppermute | solution.py:540
  39.1 5.3 %collective-permute-start.7 = (f32[24,8,128]{2,1,0:T(8,128)S(1)}, f32[24,8,128]{2,1,0:T(8,128)S(1)}, u32[]{:S(2)}, u32[]{:S(2)}) collective-permute-start(f32[24,8,128]{2,1,0:T(8,128)S(1)} %get-tuple-element.40), channel_id=1, source_target_pairs={{0,2},{1,3},{2,0},{3,1},{4,6},{5,7},{6,4},{7,5},{8,10},{9,11},{10,... | collective-permute-start | bytes 294920 | tf_op jit(solution)/shard_map/ppermute | solution.py:544
  39.6 4.8 %collective-permute-start.8 = (f32[24,8,128]{2,1,0:T(8,128)S(1)}, f32[24,8,128]{2,1,0:T(8,128)S(1)}, u32[]{:S(2)}, u32[]{:S(2)}) collective-permute-start(f32[24,8,128]{2,1,0:T(8,128)S(1)} %get-tuple-element.41), channel_id=1, source_target_pairs={{0,6},{1,7},{2,4},{3,5},{4,2},{5,3},{6,0},{7,1},{8,14},{9,15},{10,... | collective-permute-start | bytes 294920 | tf_op jit(solution)/shard_map/ppermute | solution.py:545
  42.0 2.5 %collective-permute-start.10 = (f32[24,8,128]{2,1,0:T(8,128)S(1)}, f32[24,8,128]{2,1,0:T(8,128)S(1)}, u32[]{:S(2)}, u32[]{:S(2)}) collective-permute-start(f32[24,8,128]{2,1,0:T(8,128)S(1)} %collective-permute-done.9.far_ref), channel_id=1, source_target_pairs={{0,1},{1,0},{2,3},{3,2},{4,5},{5,4},{6,7},{7,6},{8,9},{9,8},{10,11... | collective-permute-start | bytes 294920 | tf_op jit(solution)/shard_map/ppermute | solution.py:546

commit v10 on v9

--- a/solution.py
+++ b/solution.py
@@ -222,6 +222,10 @@
 
 
 def contributions(group, values, table, placed, boxes, sums):
+    scatter(group, on_boxes(group, values, table, boxes, sums), placed, boxes)
+
+
+def on_boxes(group, values, table, boxes, sums):
     coeffs = []
     for tile in range(2):
         rows = []
@@ -233,7 +237,6 @@
         coeffs.append(jnp.concatenate(rows, 0))
     both = dot(two_terms(jnp.concatenate(coeffs, 1), 0), sums)
     coeffs = (both[:8] + both[8:]) * boxes.weight(group)
-    lane = lax.broadcasted_iota(jnp.int32, (8, 128), 1)
     contrib = [[None] * 2 for _ in range(BX)]
     for tile in range(2):
         rows = [jnp.broadcast_to(coeffs[l : l + 1, half(tile)], (8, 128)) for l in range(NPROJ)]
@@ -242,6 +245,11 @@
             for l in range(1, NPROJ):
                 total = total + rows[l] * table[tile][l * BX + i]
             contrib[i][tile] = total
+    return contrib
+
+
+def scatter(group, contrib, placed, boxes):
+    lane = lax.broadcasted_iota(jnp.int32, (8, 128), 1)
     for a in range(16):
         mine = (lane >> 3) == a
         for tile in range(2):
@@ -362,11 +370,14 @@
     tables = (laid(low_ref, lowsib_ref), laid(up_ref, table_ref), laid(high_ref, highsib_ref))
     edge_potential(((low_ref, lowsib_ref), (high_ref, highsib_ref)), edge_ref)
     hots, backs = (hots_ref.at[0], hot_ref), (backs_ref.at[0], back_ref, backs_ref.at[1])
-    boxes.wait()
     sums = sums_ref[...]
+    contribs = []
     for n, group in enumerate((0, 2)):
         values = [[values_ref[n, i, tile] for tile in range(2)] for i in range(BX)]
-        contributions(group, values, tables[group], placed, boxes, sums)
+        contribs.append(on_boxes(group, values, tables[group], boxes, sums))
+    boxes.wait()
+    for group, contrib in zip((0, 2), contribs):
+        scatter(group, contrib, placed, boxes)
     nonlocal_[0:11] = spread_group(0, 6, 11, placed, backs[0])
     nonlocal_[11:18] = jnp.zeros((7, NY, NZ), jnp.float32)
     nonlocal_[18:24] = spread_group(2, 0, 6, placed, backs[2])

time: 45.3 us -> 45.3 us (level)
  no operation moved by 1% of the time
where the time goes in v10:
time: 45.3 us; the launch traced here: 45.1 us
  starting transfers between devices  21.5 us (47%)
  waiting for transfers between devices  11.9 us (26%)
  Pallas kernels  10.4 us (23%)
  between operations  1.37 us (3%)
    pallas_call x9, Pallas kernels, call(): pl.pallas_call(kernel, out_shape=outs, in_specs=ins, out_specs=out_specs...  10.4 us
    ppermute x1, waiting for transfers between devices, shards(): low = lax.ppermute(up, 'dom', ring('dom', 1))  6.97 us
    ppermute x1, starting transfers between devices, shards(): high = lax.ppermute(down, 'dom', ring('dom', -1))  6.65 us
    ppermute x1, starting transfers between devices, shards(): high_y = lax.ppermute(second, 'dom', ring('dom', -1))  4.94 us
    ppermute x1, starting transfers between devices, shards(): far = lax.ppermute(fourth, 'band', meet('band', 4))  2.93 us
    ppermute x1, waiting for transfers between devices, shards(): low_y = lax.ppermute(second, 'dom', ring('dom', 1))  2.4 us
    ppermute x1, starting transfers between devices, shards(): low = lax.ppermute(up, 'dom', ring('dom', 1))  2.12 us
    ppermute x1, waiting for transfers between devices, shards(): far = lax.ppermute(fourth, 'band', meet('band', 4))  1.6 us
  transfers between devices with their start and end apart: 11, of which 4 were waited for; matrix products, arithmetic and copies ran while one was open for 0% of the time, Pallas kernels for 7%

profile of v10, /device:TPU:1, one launch (start us, length us, event | category | flops | bytes accessed | tf_op | source)
XLA Modules:
  0.0 45.1 jit_solution(3242024478535008616)
XLA Ops:
  1.3 1.4 %pack.1 = (f32[82,8,128]{2,1,0:T(8,128)S(1)}, f32[82,8,128]{2,1,0:T(8,128)S(1)}, f32[24,8,128]{2,1,0:T(8,128)S(1)}, f32[48,8,128]{2,1,0:T(8,128)S(1)}) custom-call(f32[24,8,128]{2,1,0:T(8,128)} %bitcast.8, f32[24,8,128]{2,1,0:T(8,128)} %bitcast.9, f32[32,8,384]{2,1,0:T(8,128)} %proj_hbm.1, f32[8,32]{1,0:T(8,128)} %bitcast.10, s32[3,32]{1,0:T(4,128)} %bitcast.11, ...), custom_call_target="tpu_custom_call" | custom-call | flops 1000000 | bytes 2000000 | tf_op jit(solution)/shard_map/pack/pallas_call | solution.py:41
  2.7 0.0 copy-start
  2.7 2.1 %collective-permute-start.1 = (f32[82,8,128]{2,1,0:T(8,128)S(1)}, f32[82,8,128]{2,1,0:T(8,128)S(1)}, u32[]{:S(2)}, u32[]{:S(2)}) collective-permute-start(f32[82,8,128]{2,1,0:T(8,128)S(1)} %get-tuple-element.23), channel_id=1, source_target_pairs={{0,8},{8,16},{16,24},{24,32},{32,40},{40,48},{48,56},{56,64},{64,7... | collective-permute-start | bytes 1007624 | tf_op jit(solution)/shard_map/ppermute | solution.py:499
  4.8 6.6 %collective-permute-start = (f32[82,8,128]{2,1,0:T(8,128)S(1)}, f32[82,8,128]{2,1,0:T(8,128)S(1)}, u32[]{:S(2)}, u32[]{:S(2)}) collective-permute-start(f32[82,8,128]{2,1,0:T(8,128)S(1)} %get-tuple-element.22.up_ref), channel_id=1, source_target_pairs={{0,248},{8,0},{16,8},{24,16},{32,24},{40,32},{48,40},{56,48},{64,5... | collective-permute-start | bytes 1007624 | tf_op jit(solution)/shard_map/ppermute | solution.py:500
  11.5 0.5 %prepare.1 = (f32[48,8,128]{2,1,0:T(8,128)S(1)}, bf16[384,128]{1,0:T(8,128)(2,1)S(1)}, bf16[256,256]{1,0:T(8,128)(2,1)S(1)}, bf16[256,256]{1,0:T(8,128)(2,1)S(1)...) custom-call(f32[48,8,128]{2,1,0:T(8,128)S(1)} %get-tuple-element.25.rest_ref, ...), custom_call_target="tpu_custom_call" | custom-call | flops 1000000 | bytes 2000000 | tf_op jit(solution)/shard_map/prepare/pallas_call | solution.py:41
  12.0 7.0 %collective-permute-done.1.low_ref = f32[82,8,128]{2,1,0:T(8,128)S(1)} collective-permute-done((f32[82,8,128]{2,1,0:T(8,128)S(1)}, f32[82,8,128]{2,1,0:T(8,128)S(1)}, u32[]{:S(2)}, u32[]{:S(2)}) %collective-permute-start.1) | collective-permute-done | bytes 335904 | tf_op jit(solution)/shard_map/ppermute | solution.py:499
  19.0 1.2 %collective-permute-start.3 = (f32[82,8,128]{2,1,0:T(8,128)S(1)}, f32[82,8,128]{2,1,0:T(8,128)S(1)}, u32[]{:S(2)}, u32[]{:S(2)}) collective-permute-start(f32[82,8,128]{2,1,0:T(8,128)S(1)} %collective-permute-done.1.low_ref), channel_id=1, source_target_pairs={{0,1},{1,0},{2,3},{3,2},{4,5},{5,4},{6,7},{7,6},{8,9},{9,8},{10,11... | collective-permute-start | bytes 1007624 | tf_op jit(solution)/shard_map/ppermute | solution.py:517
  20.2 0.0 collective-permute-done.high_ref
  20.2 0.0 collective-permute-start.2
  20.3 2.0 %head.1 = (f32[2,6,2,8,128]{4,3,2,1,0:T(8,128)S(1)}, f32[24,16,128]{2,1,0:T(8,128)S(1)}, bf16[2,256,256]{2,1,0:T(8,128)(2,1)S(1)}, bf16[2,512,128]{2,1,0:T(8,128)(2,1)S(1)}) custom-call(f32[82,8,128]{2,1,0:T(8,128)S(1)} %get-tuple-element.22.up_ref, f32[82,8,128]{2,1,0:T(8,128)S(1)} %collective-permute-done.high_ref, ...), custom_call_target="tpu_custom_call" | custom-call | flops 10000000000 | bytes 2000000 | tf_op jit(solution)/shard_map/head/pallas_call | solution.py:41
  22.3 2.2 %tail.1 = (f32[24,8,128]{2,1,0:T(8,128)S(1)}, f32[24,16,128]{2,1,0:T(8,128)S(1)}, f32[2,12,8,128]{3,2,1,0:T(8,128)S(1)}) custom-call(f32[82,8,128]{2,1,0:T(8,128)S(1)} %get-tuple-element.22.up_ref, f32[82,8,128]{2,1,0:T(8,128)S(1)} %collective-permute-done.high_ref, f32[82,8,128]{2,1,0:T(8,128)S(1)} %collective-permute-done.1.low_ref, ...), custom_call_target="tpu_custom_call" | custom-call | flops 1000000 | bytes 2000000 | tf_op jit(solution)/shard_map/tail/pallas_call | solution.py:41
  24.5 0.1 collective-permute-start.5
  24.6 4.9 %collective-permute-start.4 = (f32[24,8,128]{2,1,0:T(8,128)S(1)}, f32[24,8,128]{2,1,0:T(8,128)S(1)}, u32[]{:S(2)}, u32[]{:S(2)}) collective-permute-start(f32[24,8,128]{2,1,0:T(8,128)S(1)} %get-tuple-element.37.mid_ref), channel_id=1, source_target_pairs={{0,248},{8,0},{16,8},{24,16},{32,24},{40,32},{48,40},{56,48},{64,5... | collective-permute-start | bytes 294920 | tf_op jit(solution)/shard_map/ppermute | solution.py:542
  29.5 2.4 %collective-permute-done.5.lowy_ref = f32[24,8,128]{2,1,0:T(8,128)S(1)} collective-permute-done((f32[24,8,128]{2,1,0:T(8,128)S(1)}, f32[24,8,128]{2,1,0:T(8,128)S(1)}, u32[]{:S(2)}, u32[]{:S(2)}) %collective-permute-start.5) | collective-permute-done | bytes 98336 | tf_op jit(solution)/shard_map/ppermute | solution.py:541
  31.9 2.8 %last.1.own_ref = f32[24,8,128]{2,1,0:T(8,128)S(1)} custom-call(f32[82,8,128]{2,1,0:T(8,128)S(1)} %get-tuple-element.22.up_ref, f32[82,8,128]{2,1,0:T(8,128)S(1)} %collective-permute-done.high_ref, f32[82,8,128]{2,1,0:T(8,128)S(1)} %collective-permute-done.1.low_ref, f32[24,8,128]{2,1,0:T(8,128)S(1)} %get-tuple-element.24.pot_ref, ...), custom_call_target="tpu_custom_call" | custom-call | flops 1000000 | bytes 2000000 | tf_op jit(solution)/shard_map/last/pallas_call | solution.py:41
  34.8 1.4 %collective-permute-start.6 = (f32[24,8,128]{2,1,0:T(8,128)S(1)}, f32[24,8,128]{2,1,0:T(8,128)S(1)}, u32[]{:S(2)}, u32[]{:S(2)}) collective-permute-start(f32[24,8,128]{2,1,0:T(8,128)S(1)} %last.1.own_ref), channel_id=1, source_target_pairs={{0,1},{1,0},{2,3},{3,2},{4,5},{5,4},{6,7},{7,6},{8,9},{9,8},{10,11... | collective-permute-start | bytes 294920 | tf_op jit(solution)/shard_map/ppermute | solution.py:552
  36.1 2.9 %collective-permute-start.9 = (f32[24,8,128]{2,1,0:T(8,128)S(1)}, f32[24,8,128]{2,1,0:T(8,128)S(1)}, u32[]{:S(2)}, u32[]{:S(2)}) collective-permute-start(f32[24,8,128]{2,1,0:T(8,128)S(1)} %last.1.own_ref), channel_id=1, source_target_pairs={{0,4},{1,5},{2,6},{3,7},{4,0},{5,1},{6,2},{7,3},{8,12},{9,13},{10,... | collective-permute-start | bytes 294920 | tf_op jit(solution)/shard_map/ppermute | solution.py:551
  39.1 0.5 %collective-permute-start.7 = (f32[24,8,128]{2,1,0:T(8,128)S(1)}, f32[24,8,128]{2,1,0:T(8,128)S(1)}, u32[]{:S(2)}, u32[]{:S(2)}) collective-permute-start(f32[24,8,128]{2,1,0:T(8,128)S(1)} %get-tuple-element.40), channel_id=1, source_target_pairs={{0,2},{1,3},{2,0},{3,1},{4,6},{5,7},{6,4},{7,5},{8,10},{9,11},{10,... | collective-permute-start | bytes 294920 | tf_op jit(solution)/shard_map/ppermute | solution.py:555
  39.6 0.8 %collective-permute-start.8 = (f32[24,8,128]{2,1,0:T(8,128)S(1)}, f32[24,8,128]{2,1,0:T(8,128)S(1)}, u32[]{:S(2)}, u32[]{:S(2)}) collective-permute-start(f32[24,8,128]{2,1,0:T(8,128)S(1)} %get-tuple-element.41), channel_id=1, source_target_pairs={{0,6},{1,7},{2,4},{3,5},{4,2},{5,3},{6,0},{7,1},{8,14},{9,15},{10,... | collective-permute-start | bytes 294920 | tf_op jit(solution)/shard_map/ppermute | solution.py:556
  40.4 1.6 %collective-permute-done.9.far_ref = f32[24,8,128]{2,1,0:T(8,128)S(1)} collective-permute-done((f32[24,8,128]{2,1,0:T(8,128)S(1)}, f32[24,8,128]{2,1,0:T(8,128)S(1)}, u32[]{:S(2)}, u32[]{:S(2)}) %collective-permute-start.9) | collective-permute-done | bytes 98336 | tf_op jit(solution)/shard_map/ppermute | solution.py:551
  42.0 0.9 %collective-permute-start.10 = (f32[24,8,128]{2,1,0:T(8,128)S(1)}, f32[24,8,128]{2,1,0:T(8,128)S(1)}, u32[]{:S(2)}, u32[]{:S(2)}) collective-permute-start(f32[24,8,128]{2,1,0:T(8,128)S(1)} %collective-permute-done.9.far_ref), channel_id=1, source_target_pairs={{0,1},{1,0},{2,3},{3,2},{4,5},{5,4},{6,7},{7,6},{8,9},{9,8},{10,11... | collective-permute-start | bytes 294920 | tf_op jit(solution)/shard_map/ppermute | solution.py:557
  42.9 0.6 %store.1 = f32[24,8,128]{2,1,0:T(8,128)} custom-call(f32[24,8,128]{2,1,0:T(8,128)S(1)} %last.1.own_ref), custom_call_target="tpu_custom_call" | custom-call | tf_op jit(solution)/shard_map/store/pallas_call | solution.py:41
  43.5 0.9 %collective-permute-done.7.one_ref = f32[24,8,128]{2,1,0:T(8,128)S(1)} collective-permute-done((f32[24,8,128]{2,1,0:T(8,128)S(1)}, f32[24,8,128]{2,1,0:T(8,128)S(1)}, u32[]{:S(2)}, u32[]{:S(2)}) %collective-permute-start.7) | collective-permute-done | bytes 98336 | tf_op jit(solution)/shard_map/ppermute | solution.py:555
  44.5 0.7 %total.1 = f32[24,8,128]{2,1,0:T(8,128)} custom-call(f32[8,8,128]{2,1,0:T(8,128)S(1)} %get-tuple-element.38.factors_ref, f32[24,8,128]{2,1,0:T(8,128)S(1)} %most.1.most_ref, f32[24,8,128]{2,1,0:T(8,128)S(1)} %collective-permute-done.10.farsib_ref), custom_call_target="tpu_custom_call" | custom-call | flops 1000000 | bytes 2000000 | tf_op jit(solution)/shard_map/total/pallas_call | solution.py:41
  (9 shorter events, 0.1 us)
Async XLA Ops:
  2.7 8.8 %copy-start = (f32[8,8]{1,0:T(8,128)S(1)}, f32[8,8]{1,0:T(8,128)}, u32[]{:S(2)}) copy-start(f32[8,8]{1,0:T(8,128)} %ritz_ref.1) | copy-start | bytes 772
  2.7 16.3 %collective-permute-start.1 = (f32[82,8,128]{2,1,0:T(8,128)S(1)}, f32[82,8,128]{2,1,0:T(8,128)S(1)}, u32[]{:S(2)}, u32[]{:S(2)}) collective-permute-start(f32[82,8,128]{2,1,0:T(8,128)S(1)} %get-tuple-element.23), channel_id=1, source_target_pairs={{0,8},{8,16},{16,24},{24,32},{32,40},{40,48},{48,56},{56,64},{64,7... | collective-permute-start | bytes 1007624 | tf_op jit(solution)/shard_map/ppermute | solution.py:499
  4.8 15.4 %collective-permute-start = (f32[82,8,128]{2,1,0:T(8,128)S(1)}, f32[82,8,128]{2,1,0:T(8,128)S(1)}, u32[]{:S(2)}, u32[]{:S(2)}) collective-permute-start(f32[82,8,128]{2,1,0:T(8,128)S(1)} %get-tuple-element.22.up_ref), channel_id=1, source_target_pairs={{0,248},{8,0},{16,8},{24,16},{32,24},{40,32},{48,40},{56,48},{64,5... | collective-permute-start | bytes 1007624 | tf_op jit(solution)/shard_map/ppermute | solution.py:500
  19.0 3.2 %collective-permute-start.3 = (f32[82,8,128]{2,1,0:T(8,128)S(1)}, f32[82,8,128]{2,1,0:T(8,128)S(1)}, u32[]{:S(2)}, u32[]{:S(2)}) collective-permute-start(f32[82,8,128]{2,1,0:T(8,128)S(1)} %collective-permute-done.1.low_ref), channel_id=1, source_target_pairs={{0,1},{1,0},{2,3},{3,2},{4,5},{5,4},{6,7},{7,6},{8,9},{9,8},{10,11... | collective-permute-start | bytes 1007624 | tf_op jit(solution)/shard_map/ppermute | solution.py:517
  20.2 2.0 %collective-permute-start.2 = (f32[82,8,128]{2,1,0:T(8,128)S(1)}, f32[82,8,128]{2,1,0:T(8,128)S(1)}, u32[]{:S(2)}, u32[]{:S(2)}) collective-permute-start(f32[82,8,128]{2,1,0:T(8,128)S(1)} %collective-permute-done.high_ref), channel_id=1, source_target_pairs={{0,1},{1,0},{2,3},{3,2},{4,5},{5,4},{6,7},{7,6},{8,9},{9,8},{10,11... | collective-permute-start | bytes 1007624 | tf_op jit(solution)/shard_map/ppermute | solution.py:516
  24.5 7.4 %collective-permute-start.5 = (f32[24,8,128]{2,1,0:T(8,128)S(1)}, f32[24,8,128]{2,1,0:T(8,128)S(1)}, u32[]{:S(2)}, u32[]{:S(2)}) collective-permute-start(f32[24,8,128]{2,1,0:T(8,128)S(1)} %get-tuple-element.37.mid_ref), channel_id=1, source_target_pairs={{0,8},{8,16},{16,24},{24,32},{32,40},{40,48},{48,56},{56,64},{64,7... | collective-permute-start | bytes 294920 | tf_op jit(solution)/shard_map/ppermute | solution.py:541
  24.6 7.3 %collective-permute-start.4 = (f32[24,8,128]{2,1,0:T(8,128)S(1)}, f32[24,8,128]{2,1,0:T(8,128)S(1)}, u32[]{:S(2)}, u32[]{:S(2)}) collective-permute-start(f32[24,8,128]{2,1,0:T(8,128)S(1)} %get-tuple-element.37.mid_ref), channel_id=1, source_target_pairs={{0,248},{8,0},{16,8},{24,16},{32,24},{40,32},{48,40},{56,48},{64,5... | collective-permute-start | bytes 294920 | tf_op jit(solution)/shard_map/ppermute | solution.py:542
  34.8 4.3 %collective-permute-start.6 = (f32[24,8,128]{2,1,0:T(8,128)S(1)}, f32[24,8,128]{2,1,0:T(8,128)S(1)}, u32[]{:S(2)}, u32[]{:S(2)}) collective-permute-start(f32[24,8,128]{2,1,0:T(8,128)S(1)} %last.1.own_ref), channel_id=1, source_target_pairs={{0,1},{1,0},{2,3},{3,2},{4,5},{5,4},{6,7},{7,6},{8,9},{9,8},{10,11... | collective-permute-start | bytes 294920 | tf_op jit(solution)/shard_map/ppermute | solution.py:552
  36.1 5.9 %collective-permute-start.9 = (f32[24,8,128]{2,1,0:T(8,128)S(1)}, f32[24,8,128]{2,1,0:T(8,128)S(1)}, u32[]{:S(2)}, u32[]{:S(2)}) collective-permute-start(f32[24,8,128]{2,1,0:T(8,128)S(1)} %last.1.own_ref), channel_id=1, source_target_pairs={{0,4},{1,5},{2,6},{3,7},{4,0},{5,1},{6,2},{7,3},{8,12},{9,13},{10,... | collective-permute-start | bytes 294920 | tf_op jit(solution)/shard_map/ppermute | solution.py:551
  39.1 5.3 %collective-permute-start.7 = (f32[24,8,128]{2,1,0:T(8,128)S(1)}, f32[24,8,128]{2,1,0:T(8,128)S(1)}, u32[]{:S(2)}, u32[]{:S(2)}) collective-permute-start(f32[24,8,128]{2,1,0:T(8,128)S(1)} %get-tuple-element.40), channel_id=1, source_target_pairs={{0,2},{1,3},{2,0},{3,1},{4,6},{5,7},{6,4},{7,5},{8,10},{9,11},{10,... | collective-permute-start | bytes 294920 | tf_op jit(solution)/shard_map/ppermute | solution.py:555
  39.6 4.8 %collective-permute-start.8 = (f32[24,8,128]{2,1,0:T(8,128)S(1)}, f32[24,8,128]{2,1,0:T(8,128)S(1)}, u32[]{:S(2)}, u32[]{:S(2)}) collective-permute-start(f32[24,8,128]{2,1,0:T(8,128)S(1)} %get-tuple-element.41), channel_id=1, source_target_pairs={{0,6},{1,7},{2,4},{3,5},{4,2},{5,3},{6,0},{7,1},{8,14},{9,15},{10,... | collective-permute-start | bytes 294920 | tf_op jit(solution)/shard_map/ppermute | solution.py:556
  42.0 2.5 %collective-permute-start.10 = (f32[24,8,128]{2,1,0:T(8,128)S(1)}, f32[24,8,128]{2,1,0:T(8,128)S(1)}, u32[]{:S(2)}, u32[]{:S(2)}) collective-permute-start(f32[24,8,128]{2,1,0:T(8,128)S(1)} %collective-permute-done.9.far_ref), channel_id=1, source_target_pairs={{0,1},{1,0},{2,3},{3,2},{4,5},{5,4},{6,7},{7,6},{8,9},{9,8},{10,11... | collective-permute-start | bytes 294920 | tf_op jit(solution)/shard_map/ppermute | solution.py:557

commit v11 on v10

--- a/solution.py
+++ b/solution.py
@@ -346,8 +346,10 @@
 def second_step(boxes, hots, backs, padded1, field2, gathered, placed, local, nonlocal_, pot_ref, tables, zst_ref, sums):
     for group, first, planes, skip in ((0, 0, 11, 6), (1, 6, SPAN, 0)):
         gather_columns(group, field2, first, planes, skip, gathered, hots[group])
+    windows = [read_windows(group, gathered, boxes) for group in range(2)]
+    contribs = [on_boxes(group, windows[group], tables[group], boxes, sums) for group in range(2)]
     for group in range(2):
-        contributions(group, read_windows(group, gathered, boxes), tables[group], placed, boxes, sums)
+        scatter(group, contribs[group], placed, boxes)
     local[0:12] = along_z(field2, slice(96, 288), zst_ref).reshape(12, NY, NZ)
     for p in range(12):
         here = padded1[p + 6, 8:24, :]
@@ -421,8 +423,9 @@
         local[p] = applied * (2.0 / HALF) - kept_ref[p]
     boxes.wait()
     windows = [read_windows(group, gathered, boxes) for group in range(3)]
+    contribs = [on_boxes(group, windows[group], tables[group], boxes, sums) for group in range(3)]
     for group in range(3):
-        contributions(group, windows[group], tables[group], placed, boxes, sums)
+        scatter(group, contribs[group], placed, boxes)
     nonlocal_[0:11] = spread_group(0, 6, 11, placed, backs[0])
     nonlocal_[11:24] = jnp.zeros((13, NY, NZ), jnp.float32)
     nonlocal_[6:23] += spread_group(1, 0, 17, placed, backs[1])

time: 45.3 us -> 45.3 us (level)
  no operation moved by 1% of the time
where the time goes in v11:
time: 45.3 us; the launch traced here: 45.1 us
  starting transfers between devices  21.5 us (47%)
  waiting for transfers between devices  11.9 us (26%)
  Pallas kernels  10.4 us (23%)
  between operations  1.37 us (3%)
    pallas_call x9, Pallas kernels, call(): pl.pallas_call(kernel, out_shape=outs, in_specs=ins, out_specs=out_specs...  10.4 us
    ppermute x1, waiting for transfers between devices, shards(): low = lax.ppermute(up, 'dom', ring('dom', 1))  6.97 us
    ppermute x1, starting transfers between devices, shards(): high = lax.ppermute(down, 'dom', ring('dom', -1))  6.65 us
    ppermute x1, starting transfers between devices, shards(): high_y = lax.ppermute(second, 'dom', ring('dom', -1))  4.95 us
    ppermute x1, starting transfers between devices, shards(): far = lax.ppermute(fourth, 'band', meet('band', 4))  2.93 us
    ppermute x1, waiting for transfers between devices, shards(): low_y = lax.ppermute(second, 'dom', ring('dom', 1))  2.4 us
    ppermute x1, starting transfers between devices, shards(): low = lax.ppermute(up, 'dom', ring('dom', 1))  2.12 us
    ppermute x1, waiting for transfers between devices, shards(): far = lax.ppermute(fourth, 'band', meet('band', 4))  1.59 us
  transfers between devices with their start and end apart: 11, of which 4 were waited for; matrix products, arithmetic and copies ran while one was open for 0% of the time, Pallas kernels for 7%

profile of v11, /device:TPU:1, one launch (start us, length us, event | category | flops | bytes accessed | tf_op | source)
XLA Modules:
  0.0 45.1 jit_solution(3369464861681251465)
XLA Ops:
  1.3 1.4 %pack.1 = (f32[82,8,128]{2,1,0:T(8,128)S(1)}, f32[82,8,128]{2,1,0:T(8,128)S(1)}, f32[24,8,128]{2,1,0:T(8,128)S(1)}, f32[48,8,128]{2,1,0:T(8,128)S(1)}) custom-call(f32[24,8,128]{2,1,0:T(8,128)} %bitcast.8, f32[24,8,128]{2,1,0:T(8,128)} %bitcast.9, f32[32,8,384]{2,1,0:T(8,128)} %proj_hbm.1, f32[8,32]{1,0:T(8,128)} %bitcast.10, s32[3,32]{1,0:T(4,128)} %bitcast.11, ...), custom_call_target="tpu_custom_call" | custom-call | flops 1000000 | bytes 2000000 | tf_op jit(solution)/shard_map/pack/pallas_call | solution.py:41
  2.7 0.0 copy-start
  2.7 2.1 %collective-permute-start.1 = (f32[82,8,128]{2,1,0:T(8,128)S(1)}, f32[82,8,128]{2,1,0:T(8,128)S(1)}, u32[]{:S(2)}, u32[]{:S(2)}) collective-permute-start(f32[82,8,128]{2,1,0:T(8,128)S(1)} %get-tuple-element.23), channel_id=1, source_target_pairs={{0,8},{8,16},{16,24},{24,32},{32,40},{40,48},{48,56},{56,64},{64,7... | collective-permute-start | bytes 1007624 | tf_op jit(solution)/shard_map/ppermute | solution.py:502
  4.8 6.6 %collective-permute-start = (f32[82,8,128]{2,1,0:T(8,128)S(1)}, f32[82,8,128]{2,1,0:T(8,128)S(1)}, u32[]{:S(2)}, u32[]{:S(2)}) collective-permute-start(f32[82,8,128]{2,1,0:T(8,128)S(1)} %get-tuple-element.22.up_ref), channel_id=1, source_target_pairs={{0,248},{8,0},{16,8},{24,16},{32,24},{40,32},{48,40},{56,48},{64,5... | collective-permute-start | bytes 1007624 | tf_op jit(solution)/shard_map/ppermute | solution.py:503
  11.5 0.5 %prepare.1 = (f32[48,8,128]{2,1,0:T(8,128)S(1)}, bf16[384,128]{1,0:T(8,128)(2,1)S(1)}, bf16[256,256]{1,0:T(8,128)(2,1)S(1)}, bf16[256,256]{1,0:T(8,128)(2,1)S(1)...) custom-call(f32[48,8,128]{2,1,0:T(8,128)S(1)} %get-tuple-element.25.rest_ref, ...), custom_call_target="tpu_custom_call" | custom-call | flops 1000000 | bytes 2000000 | tf_op jit(solution)/shard_map/prepare/pallas_call | solution.py:41
  12.0 7.0 %collective-permute-done.1.low_ref = f32[82,8,128]{2,1,0:T(8,128)S(1)} collective-permute-done((f32[82,8,128]{2,1,0:T(8,128)S(1)}, f32[82,8,128]{2,1,0:T(8,128)S(1)}, u32[]{:S(2)}, u32[]{:S(2)}) %collective-permute-start.1) | collective-permute-done | bytes 335904 | tf_op jit(solution)/shard_map/ppermute | solution.py:502
  19.0 1.2 %collective-permute-start.3 = (f32[82,8,128]{2,1,0:T(8,128)S(1)}, f32[82,8,128]{2,1,0:T(8,128)S(1)}, u32[]{:S(2)}, u32[]{:S(2)}) collective-permute-start(f32[82,8,128]{2,1,0:T(8,128)S(1)} %collective-permute-done.1.low_ref), channel_id=1, source_target_pairs={{0,1},{1,0},{2,3},{3,2},{4,5},{5,4},{6,7},{7,6},{8,9},{9,8},{10,11... | collective-permute-start | bytes 1007624 | tf_op jit(solution)/shard_map/ppermute | solution.py:520
  20.2 0.0 collective-permute-done.high_ref
  20.2 0.0 collective-permute-start.2
  20.3 2.0 %head.1 = (f32[2,6,2,8,128]{4,3,2,1,0:T(8,128)S(1)}, f32[24,16,128]{2,1,0:T(8,128)S(1)}, bf16[2,256,256]{2,1,0:T(8,128)(2,1)S(1)}, bf16[2,512,128]{2,1,0:T(8,128)(2,1)S(1)}) custom-call(f32[82,8,128]{2,1,0:T(8,128)S(1)} %get-tuple-element.22.up_ref, f32[82,8,128]{2,1,0:T(8,128)S(1)} %collective-permute-done.high_ref, ...), custom_call_target="tpu_custom_call" | custom-call | flops 10000000000 | bytes 2000000 | tf_op jit(solution)/shard_map/head/pallas_call | solution.py:41
  22.3 2.2 %tail.1 = (f32[24,8,128]{2,1,0:T(8,128)S(1)}, f32[24,16,128]{2,1,0:T(8,128)S(1)}, f32[2,12,8,128]{3,2,1,0:T(8,128)S(1)}) custom-call(f32[82,8,128]{2,1,0:T(8,128)S(1)} %get-tuple-element.22.up_ref, f32[82,8,128]{2,1,0:T(8,128)S(1)} %collective-permute-done.high_ref, f32[82,8,128]{2,1,0:T(8,128)S(1)} %collective-permute-done.1.low_ref, ...), custom_call_target="tpu_custom_call" | custom-call | flops 1000000 | bytes 2000000 | tf_op jit(solution)/shard_map/tail/pallas_call | solution.py:41
  24.5 0.1 collective-permute-start.5
  24.6 5.0 %collective-permute-start.4 = (f32[24,8,128]{2,1,0:T(8,128)S(1)}, f32[24,8,128]{2,1,0:T(8,128)S(1)}, u32[]{:S(2)}, u32[]{:S(2)}) collective-permute-start(f32[24,8,128]{2,1,0:T(8,128)S(1)} %get-tuple-element.37.mid_ref), channel_id=1, source_target_pairs={{0,248},{8,0},{16,8},{24,16},{32,24},{40,32},{48,40},{56,48},{64,5... | collective-permute-start | bytes 294920 | tf_op jit(solution)/shard_map/ppermute | solution.py:545
  29.5 2.4 %collective-permute-done.5.lowy_ref = f32[24,8,128]{2,1,0:T(8,128)S(1)} collective-permute-done((f32[24,8,128]{2,1,0:T(8,128)S(1)}, f32[24,8,128]{2,1,0:T(8,128)S(1)}, u32[]{:S(2)}, u32[]{:S(2)}) %collective-permute-start.5) | collective-permute-done | bytes 98336 | tf_op jit(solution)/shard_map/ppermute | solution.py:544
  31.9 2.8 %last.1.own_ref = f32[24,8,128]{2,1,0:T(8,128)S(1)} custom-call(f32[82,8,128]{2,1,0:T(8,128)S(1)} %get-tuple-element.22.up_ref, f32[82,8,128]{2,1,0:T(8,128)S(1)} %collective-permute-done.high_ref, f32[82,8,128]{2,1,0:T(8,128)S(1)} %collective-permute-done.1.low_ref, f32[24,8,128]{2,1,0:T(8,128)S(1)} %get-tuple-element.24.pot_ref, ...), custom_call_target="tpu_custom_call" | custom-call | flops 1000000 | bytes 2000000 | tf_op jit(solution)/shard_map/last/pallas_call | solution.py:41
  34.8 1.3 %collective-permute-start.6 = (f32[24,8,128]{2,1,0:T(8,128)S(1)}, f32[24,8,128]{2,1,0:T(8,128)S(1)}, u32[]{:S(2)}, u32[]{:S(2)}) collective-permute-start(f32[24,8,128]{2,1,0:T(8,128)S(1)} %last.1.own_ref), channel_id=1, source_target_pairs={{0,1},{1,0},{2,3},{3,2},{4,5},{5,4},{6,7},{7,6},{8,9},{9,8},{10,11... | collective-permute-start | bytes 294920 | tf_op jit(solution)/shard_map/ppermute | solution.py:555
  36.1 2.9 %collective-permute-start.9 = (f32[24,8,128]{2,1,0:T(8,128)S(1)}, f32[24,8,128]{2,1,0:T(8,128)S(1)}, u32[]{:S(2)}, u32[]{:S(2)}) collective-permute-start(f32[24,8,128]{2,1,0:T(8,128)S(1)} %last.1.own_ref), channel_id=1, source_target_pairs={{0,4},{1,5},{2,6},{3,7},{4,0},{5,1},{6,2},{7,3},{8,12},{9,13},{10,... | collective-permute-start | bytes 294920 | tf_op jit(solution)/shard_map/ppermute | solution.py:554
  39.1 0.5 %collective-permute-start.7 = (f32[24,8,128]{2,1,0:T(8,128)S(1)}, f32[24,8,128]{2,1,0:T(8,128)S(1)}, u32[]{:S(2)}, u32[]{:S(2)}) collective-permute-start(f32[24,8,128]{2,1,0:T(8,128)S(1)} %get-tuple-element.40), channel_id=1, source_target_pairs={{0,2},{1,3},{2,0},{3,1},{4,6},{5,7},{6,4},{7,5},{8,10},{9,11},{10,... | collective-permute-start | bytes 294920 | tf_op jit(solution)/shard_map/ppermute | solution.py:558
  39.6 0.8 %collective-permute-start.8 = (f32[24,8,128]{2,1,0:T(8,128)S(1)}, f32[24,8,128]{2,1,0:T(8,128)S(1)}, u32[]{:S(2)}, u32[]{:S(2)}) collective-permute-start(f32[24,8,128]{2,1,0:T(8,128)S(1)} %get-tuple-element.41), channel_id=1, source_target_pairs={{0,6},{1,7},{2,4},{3,5},{4,2},{5,3},{6,0},{7,1},{8,14},{9,15},{10,... | collective-permute-start | bytes 294920 | tf_op jit(solution)/shard_map/ppermute | solution.py:559
  40.4 1.6 %collective-permute-done.9.far_ref = f32[24,8,128]{2,1,0:T(8,128)S(1)} collective-permute-done((f32[24,8,128]{2,1,0:T(8,128)S(1)}, f32[24,8,128]{2,1,0:T(8,128)S(1)}, u32[]{:S(2)}, u32[]{:S(2)}) %collective-permute-start.9) | collective-permute-done | bytes 98336 | tf_op jit(solution)/shard_map/ppermute | solution.py:554
  42.0 0.9 %collective-permute-start.10 = (f32[24,8,128]{2,1,0:T(8,128)S(1)}, f32[24,8,128]{2,1,0:T(8,128)S(1)}, u32[]{:S(2)}, u32[]{:S(2)}) collective-permute-start(f32[24,8,128]{2,1,0:T(8,128)S(1)} %collective-permute-done.9.far_ref), channel_id=1, source_target_pairs={{0,1},{1,0},{2,3},{3,2},{4,5},{5,4},{6,7},{7,6},{8,9},{9,8},{10,11... | collective-permute-start | bytes 294920 | tf_op jit(solution)/shard_map/ppermute | solution.py:560
  42.9 0.6 %store.1 = f32[24,8,128]{2,1,0:T(8,128)} custom-call(f32[24,8,128]{2,1,0:T(8,128)S(1)} %last.1.own_ref), custom_call_target="tpu_custom_call" | custom-call | tf_op jit(solution)/shard_map/store/pallas_call | solution.py:41
  43.5 0.9 %collective-permute-done.7.one_ref = f32[24,8,128]{2,1,0:T(8,128)S(1)} collective-permute-done((f32[24,8,128]{2,1,0:T(8,128)S(1)}, f32[24,8,128]{2,1,0:T(8,128)S(1)}, u32[]{:S(2)}, u32[]{:S(2)}) %collective-permute-start.7) | collective-permute-done | bytes 98336 | tf_op jit(solution)/shard_map/ppermute | solution.py:558
  44.5 0.7 %total.1 = f32[24,8,128]{2,1,0:T(8,128)} custom-call(f32[8,8,128]{2,1,0:T(8,128)S(1)} %get-tuple-element.38.factors_ref, f32[24,8,128]{2,1,0:T(8,128)S(1)} %most.1.most_ref, f32[24,8,128]{2,1,0:T(8,128)S(1)} %collective-permute-done.10.farsib_ref), custom_call_target="tpu_custom_call" | custom-call | flops 1000000 | bytes 2000000 | tf_op jit(solution)/shard_map/total/pallas_call | solution.py:41
  (9 shorter events, 0.1 us)
Async XLA Ops:
  2.7 8.8 %copy-start = (f32[8,8]{1,0:T(8,128)S(1)}, f32[8,8]{1,0:T(8,128)}, u32[]{:S(2)}) copy-start(f32[8,8]{1,0:T(8,128)} %ritz_ref.1) | copy-start | bytes 772
  2.7 16.3 %collective-permute-start.1 = (f32[82,8,128]{2,1,0:T(8,128)S(1)}, f32[82,8,128]{2,1,0:T(8,128)S(1)}, u32[]{:S(2)}, u32[]{:S(2)}) collective-permute-start(f32[82,8,128]{2,1,0:T(8,128)S(1)} %get-tuple-element.23), channel_id=1, source_target_pairs={{0,8},{8,16},{16,24},{24,32},{32,40},{40,48},{48,56},{56,64},{64,7... | collective-permute-start | bytes 1007624 | tf_op jit(solution)/shard_map/ppermute | solution.py:502
  4.8 15.4 %collective-permute-start = (f32[82,8,128]{2,1,0:T(8,128)S(1)}, f32[82,8,128]{2,1,0:T(8,128)S(1)}, u32[]{:S(2)}, u32[]{:S(2)}) collective-permute-start(f32[82,8,128]{2,1,0:T(8,128)S(1)} %get-tuple-element.22.up_ref), channel_id=1, source_target_pairs={{0,248},{8,0},{16,8},{24,16},{32,24},{40,32},{48,40},{56,48},{64,5... | collective-permute-start | bytes 1007624 | tf_op jit(solution)/shard_map/ppermute | solution.py:503
  19.0 3.2 %collective-permute-start.3 = (f32[82,8,128]{2,1,0:T(8,128)S(1)}, f32[82,8,128]{2,1,0:T(8,128)S(1)}, u32[]{:S(2)}, u32[]{:S(2)}) collective-permute-start(f32[82,8,128]{2,1,0:T(8,128)S(1)} %collective-permute-done.1.low_ref), channel_id=1, source_target_pairs={{0,1},{1,0},{2,3},{3,2},{4,5},{5,4},{6,7},{7,6},{8,9},{9,8},{10,11... | collective-permute-start | bytes 1007624 | tf_op jit(solution)/shard_map/ppermute | solution.py:520
  20.2 2.0 %collective-permute-start.2 = (f32[82,8,128]{2,1,0:T(8,128)S(1)}, f32[82,8,128]{2,1,0:T(8,128)S(1)}, u32[]{:S(2)}, u32[]{:S(2)}) collective-permute-start(f32[82,8,128]{2,1,0:T(8,128)S(1)} %collective-permute-done.high_ref), channel_id=1, source_target_pairs={{0,1},{1,0},{2,3},{3,2},{4,5},{5,4},{6,7},{7,6},{8,9},{9,8},{10,11... | collective-permute-start | bytes 1007624 | tf_op jit(solution)/shard_map/ppermute | solution.py:519
  24.5 7.4 %collective-permute-start.5 = (f32[24,8,128]{2,1,0:T(8,128)S(1)}, f32[24,8,128]{2,1,0:T(8,128)S(1)}, u32[]{:S(2)}, u32[]{:S(2)}) collective-permute-start(f32[24,8,128]{2,1,0:T(8,128)S(1)} %get-tuple-element.37.mid_ref), channel_id=1, source_target_pairs={{0,8},{8,16},{16,24},{24,32},{32,40},{40,48},{48,56},{56,64},{64,7... | collective-permute-start | bytes 294920 | tf_op jit(solution)/shard_map/ppermute | solution.py:544
  24.6 7.4 %collective-permute-start.4 = (f32[24,8,128]{2,1,0:T(8,128)S(1)}, f32[24,8,128]{2,1,0:T(8,128)S(1)}, u32[]{:S(2)}, u32[]{:S(2)}) collective-permute-start(f32[24,8,128]{2,1,0:T(8,128)S(1)} %get-tuple-element.37.mid_ref), channel_id=1, source_target_pairs={{0,248},{8,0},{16,8},{24,16},{32,24},{40,32},{48,40},{56,48},{64,5... | collective-permute-start | bytes 294920 | tf_op jit(solution)/shard_map/ppermute | solution.py:545
  34.8 4.3 %collective-permute-start.6 = (f32[24,8,128]{2,1,0:T(8,128)S(1)}, f32[24,8,128]{2,1,0:T(8,128)S(1)}, u32[]{:S(2)}, u32[]{:S(2)}) collective-permute-start(f32[24,8,128]{2,1,0:T(8,128)S(1)} %last.1.own_ref), channel_id=1, source_target_pairs={{0,1},{1,0},{2,3},{3,2},{4,5},{5,4},{6,7},{7,6},{8,9},{9,8},{10,11... | collective-permute-start | bytes 294920 | tf_op jit(solution)/shard_map/ppermute | solution.py:555
  36.1 5.9 %collective-permute-start.9 = (f32[24,8,128]{2,1,0:T(8,128)S(1)}, f32[24,8,128]{2,1,0:T(8,128)S(1)}, u32[]{:S(2)}, u32[]{:S(2)}) collective-permute-start(f32[24,8,128]{2,1,0:T(8,128)S(1)} %last.1.own_ref), channel_id=1, source_target_pairs={{0,4},{1,5},{2,6},{3,7},{4,0},{5,1},{6,2},{7,3},{8,12},{9,13},{10,... | collective-permute-start | bytes 294920 | tf_op jit(solution)/shard_map/ppermute | solution.py:554
  39.1 5.3 %collective-permute-start.7 = (f32[24,8,128]{2,1,0:T(8,128)S(1)}, f32[24,8,128]{2,1,0:T(8,128)S(1)}, u32[]{:S(2)}, u32[]{:S(2)}) collective-permute-start(f32[24,8,128]{2,1,0:T(8,128)S(1)} %get-tuple-element.40), channel_id=1, source_target_pairs={{0,2},{1,3},{2,0},{3,1},{4,6},{5,7},{6,4},{7,5},{8,10},{9,11},{10,... | collective-permute-start | bytes 294920 | tf_op jit(solution)/shard_map/ppermute | solution.py:558
  39.6 4.8 %collective-permute-start.8 = (f32[24,8,128]{2,1,0:T(8,128)S(1)}, f32[24,8,128]{2,1,0:T(8,128)S(1)}, u32[]{:S(2)}, u32[]{:S(2)}) collective-permute-start(f32[24,8,128]{2,1,0:T(8,128)S(1)} %get-tuple-element.41), channel_id=1, source_target_pairs={{0,6},{1,7},{2,4},{3,5},{4,2},{5,3},{6,0},{7,1},{8,14},{9,15},{10,... | collective-permute-start | bytes 294920 | tf_op jit(solution)/shard_map/ppermute | solution.py:559
  42.0 2.5 %collective-permute-start.10 = (f32[24,8,128]{2,1,0:T(8,128)S(1)}, f32[24,8,128]{2,1,0:T(8,128)S(1)}, u32[]{:S(2)}, u32[]{:S(2)}) collective-permute-start(f32[24,8,128]{2,1,0:T(8,128)S(1)} %collective-permute-done.9.far_ref), channel_id=1, source_target_pairs={{0,1},{1,0},{2,3},{3,2},{4,5},{5,4},{6,7},{7,6},{8,9},{9,8},{10,11... | collective-permute-start | bytes 294920 | tf_op jit(solution)/shard_map/ppermute | solution.py:560
